TPU v7x, 32 devices: a whole 2x2x4 slice. The times are simulated.
32 devices in a mesh: az: 16 (over z, x, core), rad: 2 (over y).
Axes of the slice: x: 2, y: 2, z: 4, core: 2. Of those that a mesh axis runs over, the one named last changes fastest.
Arguments:
- pressure: float32 [2, 256, 192, 128], P(None, 'az', 'rad'), may hold values from -6 to 6
- source: float32 [2, 256, 192, 128], P(None, 'az', 'rad'), may hold values from -6 to 6
- diagonal: float32 [2, 256, 192, 128], P(None, 'az', 'rad'), may hold values from 0.5 to 8
- rot_offset: int32 [1], replicated, may hold values from 0 to 255
Outputs:
- corrected: float32 [2, 256, 192, 128], P(None, 'az', 'rad')
All inputs are finite; a program needn't handle non-finite values.
Results may differ from a plain program's by a relative error of at most 0.00002.
Values sent between devices are 32-bit elements; how exact they have to be, the bound alone decides.
No kernel may reach another device: no remote copies, remote signals or barrier semaphores. Data moves between devices by JAX's collectives and lax.ppermute only.
A program may use at most 64 MiB of HBM per device.

v0:
```python
import functools

import jax
import jax.numpy as jnp
from jax import lax
from jax.experimental import pallas as pl
from jax.experimental.pallas import tpu as pltpu
from jax.sharding import PartitionSpec as P

STEPS = 2
SWEEPS = 4
OMEGA = 0.8
TILE = 8
OWN = 2 * TILE
SLOTS = SWEEPS + 2


class Side:
    def __init__(self, low, radial_cells):
        end = OWN + radial_cells
        self.low = low
        self.own = slice(OWN, end)
        self.first = OWN if low else TILE
        self.count = radial_cells + TILE
        self.rows = slice(self.first, self.first + self.count)
        self.cut = slice(end, end + SWEEPS) if low else slice(OWN - SWEEPS, OWN)
        self.tile = slice(end, end + TILE) if low else slice(TILE, OWN)
        self.ghost = OWN - 1 if low else end
        self.edge = OWN if low else end - 1
        self.spare = self.count - TILE + SWEEPS if low else 0
        self.facing = 1 if low else 0
        self.sent = slice(radial_cells - SWEEPS, radial_cells) if low else slice(0, SWEEPS)
        self.sent_tile = radial_cells - TILE if low else 0
        self.edge_tile = 0 if low else radial_cells - TILE


def shifted(s, by):
    return slice(s.start + by, s.stop + by)


def axial_sum(x):
    lane = lax.broadcasted_iota(jnp.int32, x.shape, 1)
    last = x.shape[1] - 1
    return jnp.where(lane == 0, 0.0, pltpu.roll(x, 1, 1)) + jnp.where(
        lane == last, 0.0, pltpu.roll(x, last, 1)
    )


def relaxed(column, side, beside, weight, shift):
    here = column[side.rows]
    radial = column[shifted(side.rows, -1)] + column[shifted(side.rows, 1)]
    nbr = beside + radial + axial_sum(here)
    kept = (1.0 - OMEGA) * here
    if shift is not None:
        kept = kept + shift
    return kept + weight * nbr


def mirror(column, side):
    column[side.ghost : side.ghost + 1] = column[side.edge : side.edge + 1]


def on_each_side(radial_cells, body):
    low = lax.axis_index("rad") == 0

    @pl.when(low)
    def _():
        body(Side(True, radial_cells))

    @pl.when(jnp.logical_not(low))
    def _():
        body(Side(False, radial_cells))


def copy_all(copies):
    for c in copies:
        c.start()
    for c in copies:
        c.wait()


def end_columns(edge, cells, count):
    return slice(0, count) if edge == 0 else slice(cells - count, cells)


def spare_rows(side):
    return [(slot, side.spare + i) for slot in range(SWEEPS) for i in range(TILE - SWEEPS)]


def close(column, side, facing):
    row = slice(side.ghost, side.ghost + 1)
    if facing:
        column[row] = jnp.zeros((1, column.shape[1]), jnp.float32)
    else:
        column[row] = column[side.edge : side.edge + 1]


def trajectories(side, field, other, weight, shift, messages):
    bufs = (field, other)
    for edge, message in enumerate(messages):

        def at(distance, n, edge=edge):
            return distance - 1 if edge == 0 else n - distance

        for k in range(2):
            facing = k == side.facing
            for i in range(SWEEPS):
                close(field.at[edge, k, i], side, facing)
            for sweep in range(SWEEPS):
                src, dst = bufs[sweep % 2], bufs[1 - sweep % 2]
                top = src.at[edge, k, at(1, SWEEPS)]
                message[k, sweep] = top[side.rows]
                for j in range(1, SWEEPS - sweep):
                    here = src.at[edge, k, at(j, SWEEPS)]
                    beside = src[edge, k, at(j + 1, SWEEPS), side.rows]
                    if j > 1:
                        beside = beside + src[edge, k, at(j - 1, SWEEPS), side.rows]
                    i = at(j, SWEEPS - 1)
                    out = dst.at[edge, k, at(j, SWEEPS)]
                    out[side.rows] = relaxed(here, side, beside, weight(edge, k, i), shift(edge, k, i))
                    close(out, side, facing)
            if message.shape[1] == SWEEPS:
                continue
            for i in range(2):
                message[k, SWEEPS + i] = weight(edge, k, at(1 + i, SWEEPS - 1))
            if facing:
                row = side.edge - side.first
                message[k, SWEEPS + 1, side.spare : side.spare + 1] = weight(
                    edge, k, at(3, SWEEPS - 1)
                )[row : row + 1]


def pack(p_ref, s_ref, d_ref, cut_ref, edge_ref, p_ends, s_ends, d_ends, tiles, edge_tiles, sems):
    cells, radial_cells = p_ref.shape[1:3]

    def body(side):
        copies = []

        def fetch(source, target):
            copies.append(pltpu.make_async_copy(source, target, sems.at[len(copies)]))

        rows = pl.ds(side.sent_tile, TILE)
        for i, x in enumerate((p_ref, s_ref, d_ref)):
            fetch(x.at[:, :, rows, :], tiles.at[i])
        fetch(p_ref.at[side.facing, :, pl.ds(side.edge_tile, TILE), :], edge_tiles)
        for source, target in ((p_ref, p_ends), (s_ref, s_ends), (d_ref, d_ends)):
            count = target.shape[2]
            for edge in range(2):
                span = pl.ds(end_columns(edge, cells, count).start, count)
                fetch(source.at[:, span], target.at[edge])
        copy_all(copies)
        cut_ref[...] = tiles[:, :, :, shifted(side.sent, -side.sent_tile), :]
        at = side.edge - OWN - side.edge_tile
        for j in range(cells):
            edge_ref[j : j + 1] = edge_tiles[j, at : at + 1]

    on_each_side(radial_cells, body)


def fill_ends(field, side, p_ends, cut_ref, cells):
    for edge in range(2):
        columns = end_columns(edge, cells, SWEEPS)
        for k in range(2):
            for i in range(SWEEPS):
                field[edge, k, i, side.own] = p_ends[edge, k, i]
                field[edge, k, i, side.cut] = cut_ref[0, k, columns.start + i]


def send_block(side, arriving, block_ref, messages):
    arriving.wait()
    for message in messages:
        for i, (slot, row) in enumerate(spare_rows(side)):
            message[side.facing, slot, row : row + 1] = block_ref[i : i + 1]


def first_edges(
    p_ends, s_ends, d_ends, cut_ref, block_ref, last, first, block, sem, field, other, weight, shift
):
    radial_cells = p_ends.shape[3]
    cells = cut_ref.shape[2]
    n = SWEEPS - 1

    def body(side):
        arriving = pltpu.make_async_copy(block_ref, block, sem)
        arriving.start()
        own = shifted(side.own, -side.first)
        cut = shifted(side.cut, -side.first)
        fill_ends(field, side, p_ends, cut_ref, cells)
        for edge in range(2):
            columns = end_columns(edge, cells, n)
            for k in range(2):
                for i in range(n):
                    for rows, s, d in (
                        (own, s_ends[edge, k, i], d_ends[edge, k, i]),
                        (cut, cut_ref[1, k, columns.start + i], cut_ref[2, k, columns.start + i]),
                    ):
                        w = OMEGA / (6.0 + d)
                        weight[edge, k, i, rows] = w
                        shift[edge, k, i, rows] = w * s
        trajectories(
            side,
            field,
            other,
            lambda e, k, i: weight[e, k, i],
            lambda e, k, i: shift[e, k, i],
            (first, last),
        )
        send_block(side, arriving, block, (first, last))

    on_each_side(radial_cells, body)


def later_edges(p_ends, b_ends, w_ends, cut_ref, block_ref, last, first, block, sem, field, other):
    cells, radial_cells = cut_ref.shape[2], p_ends.shape[3]

    def body(side):
        arriving = pltpu.make_async_copy(block_ref, block, sem)
        arriving.start()
        fill_ends(field, side, p_ends, cut_ref, cells)
        trajectories(
            side,
            field,
            other,
            lambda e, k, i: w_ends[e, k, i + e],
            lambda e, k, i: b_ends[e, k, i + e],
            (first, last),
        )
        send_block(side, arriving, block, (first, last))

    on_each_side(radial_cells, body)


def inner_sweeps(side, levels, weight, shift, last, out_ref, stash, tile_out, w_tile, sems):
    cells = levels.shape[2]
    radial_cells = side.own.stop - side.own.start
    for j in range(cells):
        for k in range(2):
            close(levels.at[0, k, j], side, k == side.facing)
        for n in range(1, SWEEPS):
            close(levels.at[n, side.facing, j], side, True)
    at = side.edge - side.first
    for e, first in enumerate((0, cells - 2)):
        for k in range(2):
            for i in range(2):
                stash[e, 0, k, i] = levels[0, k, first + i]
    for n in range(SWEEPS):
        final = n == SWEEPS - 1

        def step(j, carry, n=n, final=final):
            for k in range(2):
                beside = levels[n, k, j - 1, side.rows] + levels[n, k, j + 1, side.rows]
                new = relaxed(levels.at[n, k, j], side, beside, weight[k, j], shift[k, j])
                if final:
                    last[k, j - SWEEPS] = new[shifted(side.own, -side.first)]
                else:
                    levels[n + 1, k, j, side.rows] = new
                    if k != side.facing:
                        levels[n + 1, k, j, side.ghost : side.ghost + 1] = new[at : at + 1]
            return carry

        lax.fori_loop(n + 1, cells - 1 - n, step, 0, unroll=2)
        if not final:
            for e, first in enumerate((n + 1, cells - 3 - n)):
                for k in range(2):
                    for i in range(2):
                        stash[e, n + 1, k, i] = levels[n + 1, k, first + i]
    inner = pltpu.make_async_copy(
        last, out_ref.at[:, pl.ds(SWEEPS, cells - 2 * SWEEPS)], sems.at[0]
    )
    inner.start()
    tile_out[...] = last[side.facing, :, side.edge_tile : side.edge_tile + TILE, :]
    first = side.edge_tile + OWN - side.first
    w_tile[...] = weight[side.facing, :, first : first + TILE, :]
    return inner


def first_interior(
    p_ref, s_ref, d_ref, cut_ref,
    out_ref, stash, tile_out, w_tile, cut_out, b_ends, w_ends, b_out, w_out,
    levels, last, shift, weight, sems,
):
    cells, radial_cells = p_ref.shape[1:3]

    def body(side):
        own = pl.ds(OWN - side.first, radial_cells)
        copy_all(
            [
                pltpu.make_async_copy(
                    p_ref, levels.at[0, :, :, pl.ds(OWN, radial_cells), :], sems.at[0]
                ),
                pltpu.make_async_copy(s_ref, shift.at[:, :, own, :], sems.at[1]),
                pltpu.make_async_copy(d_ref, weight.at[:, :, own, :], sems.at[2]),
            ]
        )
        cut = shifted(side.cut, -side.first)
        levels[0, :, :, side.cut, :] = cut_ref[0]
        shift[:, :, cut, :] = cut_ref[1]
        weight[:, :, cut, :] = cut_ref[2]

        def invert(j, carry):
            for k in range(2):
                w = OMEGA / (6.0 + weight[k, j])
                weight[k, j] = w
                shift[k, j] = w * shift[k, j]
            return carry

        lax.fori_loop(0, cells, invert, 0)
        pending = [
            pltpu.make_async_copy(shift, b_out, sems.at[1]),
            pltpu.make_async_copy(weight, w_out, sems.at[2]),
        ]
        for c in pending:
            c.start()
        for e in range(2):
            columns = end_columns(e, cells, SWEEPS)
            b_ends[e] = shift[:, columns]
            w_ends[e] = weight[:, columns]
        pending.append(
            inner_sweeps(
                side, levels, weight, shift, last, out_ref, stash, tile_out, w_tile, sems
            )
        )
        cut_out[...] = last[:, :, side.sent, :]
        for c in pending:
            c.wait()

    on_each_side(radial_cells, body)


def later_interior(
    p_ref, b_ref, w_ref, cut_ref, out_ref, stash, tile_out, w_tile, levels, last, shift, weight, sems
):
    cells, radial_cells = p_ref.shape[1:3]

    def body(side):
        copy_all(
            [
                pltpu.make_async_copy(
                    p_ref, levels.at[0, :, :, pl.ds(OWN, radial_cells), :], sems.at[0]
                ),
                pltpu.make_async_copy(b_ref, shift, sems.at[1]),
                pltpu.make_async_copy(w_ref, weight, sems.at[2]),
            ]
        )
        levels[0, :, :, side.cut, :] = cut_ref[0]
        inner_sweeps(
            side, levels, weight, shift, last, out_ref, stash, tile_out, w_tile, sems
        ).wait()

    on_each_side(radial_cells, body)


def ghost_response(side, start_ref, w_tile, block_ref, messages, weights, wide, source):
    facing = side.facing
    cells = w_tile.shape[0]
    reach = SWEEPS - 1
    tile = slice(side.edge_tile + OWN - side.first, side.edge_tile + OWN - side.first + TILE)
    at = side.edge - OWN - side.edge_tile
    rows = spare_rows(side)
    for i, (slot, row) in enumerate(rows):
        wide[i : i + 1] = messages[0][facing, slot, row : row + 1]
        wide[2 * cells + i : 2 * cells + i + 1] = messages[1][facing, slot, row : row + 1]
    wide[cells : 2 * cells] = block_ref[...]
    source[...] = jnp.zeros(source.shape, jnp.float32)
    for c in range(cells + 2 * reach):
        source[c, at : at + 1] = wide[pl.ds(start_ref[0] + c, 1), :]
    row = lax.broadcasted_iota(jnp.int32, source.shape[1:], 0)
    weight = [w_tile[j] for j in range(cells)]
    for e in range(2):
        far = weights[e][facing, SWEEPS + 1, side.spare : side.spare + 1]
        beyond = [
            weights[e][facing, SWEEPS, tile],
            weights[e][facing, SWEEPS + 1, tile],
            jnp.where(row == at, far, 0.0),
        ]
        weight = beyond[::-1] + weight if e == 0 else weight + beyond
    given = [source[c] for c in range(cells + 2 * reach)]
    response = [w * g for w, g in zip(weight, given)]
    for n in range(1, SWEEPS):
        old = response
        response = list(old)
        for c in range(n, len(old) - n):
            x = old[c]
            radial = jnp.where(row == 0, 0.0, pltpu.roll(x, 1, 0)) + jnp.where(
                row == TILE - 1, 0.0, pltpu.roll(x, TILE - 1, 0)
            )
            nbr = (old[c - 1] + old[c + 1]) + (radial + axial_sum(x)) + given[c]
            response[c] = (1.0 - OMEGA) * x + weight[c] * nbr
    return response[reach : reach + cells]


def finish(known, start_ref, b_ends, w_ends, w_tile, stash, block_ref, tile_in, left_ref, right_ref, *rest):
    if known:
        left_w, right_w, _, out_ref, *rest = rest
        weights = (left_w, right_w)
    else:
        cut_in, _, out_ref, cut_out, edge_out, ends_out, *rest = rest
        weights = (left_ref, right_ref)
    levels, last, inner_tiles, near, near2, wide, source, sems = rest
    messages = (left_ref, right_ref)
    cells, radial_cells = out_ref.shape[1:3]

    def column(e, d):
        return d - 1 if e == 0 else cells - d

    def body(side):
        facing = side.facing

        def at(n, e, k, d):
            if d <= n:
                return levels.at[n, e, k, d]
            return stash.at[e, n, k, d - n - 1 if e == 0 else n + 2 - d]

        for e in range(2):
            for k in range(2):
                levels[0, e, k, 0, side.rows] = messages[e][k, 0]
                for buf in (near, near2):
                    buf[e, k] = jnp.zeros(buf.shape[2:], jnp.float32)
        nears = (near, near2)

        def own_column(n, e, k, d):
            i = d - 1 if e == 0 else SWEEPS - d
            beside = at(n, e, k, d - 1)[side.rows] + at(n, e, k, d + 1)[side.rows]
            return relaxed(at(n, e, k, d), side, beside, w_ends[e, k, i], b_ends[e, k, i])

        for n in range(SWEEPS - 1):
            src, dst = nears[n % 2], nears[1 - n % 2]
            for e in range(2):
                for k in range(2):
                    for d in range(1, n + 2):
                        levels[n + 1, e, k, d, side.rows] = own_column(n, e, k, d)
                        close(levels.at[n + 1, e, k, d], side, k == facing)
                    beside = at(n, e, k, 1)[side.rows]
                    if n > 0:
                        beside = beside + src[e, k, 1, side.rows]
                        new = relaxed(src.at[e, k, 0], side, beside, weights[e][k, SWEEPS], None)
                    else:
                        new = weights[e][k, SWEEPS] * beside
                    dst[e, k, 0, side.rows] = new
                    levels[n + 1, e, k, 0, side.rows] = messages[e][k, n + 1] + new
                    close(dst.at[e, k, 0], side, k == facing)
                    if n == 1:
                        dst[e, k, 1, side.rows] = (
                            weights[e][k, SWEEPS + 1] * src[e, k, 0, side.rows]
                        )
        copies = []

        def store(source, target):
            copies.append(pltpu.make_async_copy(source, target, sems.at[len(copies)]))
            copies[-1].start()

        response = None
        tile = slice(side.edge_tile, side.edge_tile + TILE)
        for k in (1 - facing, facing):
            if k == facing:
                response = ghost_response(
                    side, start_ref, w_tile, block_ref, messages, weights, wide, source
                )
                for i in range(cells - 2 * SWEEPS):
                    inner_tiles[i] = tile_in[i] + response[SWEEPS + i]
                store(
                    inner_tiles,
                    out_ref.at[
                        k, pl.ds(SWEEPS, cells - 2 * SWEEPS), pl.ds(side.edge_tile, TILE), :
                    ],
                )
            for e in range(2):
                first = end_columns(e, cells, SWEEPS).start
                for d in range(1, SWEEPS + 1):
                    new = own_column(SWEEPS - 1, e, k, d)[shifted(side.own, -side.first)]
                    i = column(e, d) - first
                    last[e, k, i] = new
                    if k == facing:
                        last[e, k, i, tile] = new[tile] + response[first + i]
                store(last.at[e, k], out_ref.at[k, pl.ds(first, SWEEPS)])
        if not known:
            row = side.edge - OWN
            cut_out[0, :, SWEEPS : cells - SWEEPS] = cut_in[...]
            for i in range(cells - 2 * SWEEPS):
                j = SWEEPS + i
                r = row - side.edge_tile
                edge_out[j : j + 1] = inner_tiles[i, r : r + 1]
            for e in range(2):
                first = end_columns(e, cells, SWEEPS).start
                cut_out[0, :, first : first + SWEEPS] = last[e, :, :, side.sent, :]
                for i in range(SWEEPS):
                    edge_out[first + i : first + i + 1] = last[e, facing, i, row : row + 1]
            ends_out[...] = last[...]
        for c in copies:
            c.wait()

    on_each_side(radial_cells, body)


def ring(size, step):
    return [(i, (i + step) % size) for i in range(size)]


def facing_pairs(size, turn):
    pairs = []
    for i in range(size):
        pairs.append((2 * ((i - turn) % size) + 1, 2 * i))
        pairs.append((2 * ((i + turn) % size), 2 * i + 1))
    return pairs


def far_pairs(size, turn):
    return [(2 * i + r, 2 * ((i + (2 * r - 1) * turn) % size) + r) for i in range(size) for r in range(2)]


def facing_block(edge, offset, radial_index):
    size = lax.axis_size("az")
    cells = edge.shape[0]
    turn = (offset + cells // 2) // cells
    rest = offset - turn * cells
    turn = turn % size
    near = min(size, 16)

    def far(t):
        return lambda e: lax.ppermute(e, ("az", "rad"), far_pairs(size, t * near))

    def branch(t):
        return lambda e: lax.ppermute(e, ("az", "rad"), facing_pairs(size, t))

    if size > near:
        edge = lax.switch(turn // near, [far(t) for t in range(-(-size // near))], edge)
    block = lax.switch(turn % near, [branch(t) for t in range(near)], edge)
    return block, cells - (SWEEPS - 1) + jnp.where(radial_index == 0, -rest, rest)


def per_device(pressure, source, diagonal, rot_offset):
    _, cells, radial_cells, lanes = pressure.shape
    size = lax.axis_size("az")
    radial_index = lax.axis_index("rad")
    rows, span = radial_cells + 4 * TILE, radial_cells + TILE

    def array(*shape):
        return jax.ShapeDtypeStruct(shape, jnp.float32)

    def scratch(*shape):
        return pltpu.VMEM(shape, jnp.float32)

    def pinned(x):
        return pltpu.with_memory_space_constraint(x, pltpu.HBM)

    kept = pltpu.HBM((2, cells, span, lanes), jnp.float32)
    kept_ends = array(2, 2, SWEEPS, span, lanes)
    stash = array(2, SWEEPS, 2, 2, rows, lanes)
    cells_in = cells - 2 * SWEEPS
    tiles = array(cells_in, TILE, lanes)
    vmem = pl.BlockSpec(memory_space=pltpu.VMEM)
    smem = pl.BlockSpec(memory_space=pltpu.SMEM)
    hbm = pl.BlockSpec(memory_space=pltpu.HBM)
    anywhere = pl.BlockSpec(memory_space=pl.ANY)
    columns = scratch(2, 2, SWEEPS, rows, lanes)
    three = scratch(2, 2, SWEEPS - 1, span, lanes)

    def call(kernel, out_shape, in_specs, out_specs, scratch_shapes, operands, work_columns, **more):
        work = 2 * work_columns * span * lanes
        return pl.pallas_call(
            kernel,
            out_shape=out_shape,
            in_specs=in_specs,
            out_specs=out_specs,
            scratch_shapes=scratch_shapes,
            compiler_params=pltpu.CompilerParams(vmem_limit_bytes=28 << 20),
            cost_estimate=pl.CostEstimate(
                flops=12 * work, bytes_accessed=8 * work, transcendentals=0
            ),
            **more,
        )(*operands)

    fields = tuple(pinned(x) for x in (pressure, source, diagonal))
    cut, edge, *ends = call(
        pack,
        (
            array(3, 2, cells, SWEEPS, lanes),
            array(cells, lanes),
            array(2, 2, SWEEPS, radial_cells, lanes),
            array(2, 2, SWEEPS - 1, radial_cells, lanes),
            array(2, 2, SWEEPS - 1, radial_cells, lanes),
        ),
        [hbm] * 3,
        [vmem] * 2 + [anywhere] * 3,
        [
            scratch(3, 2, cells, TILE, lanes),
            scratch(cells, TILE, lanes),
            pltpu.SemaphoreType.DMA((10,)),
        ],
        fields,
        1,
        name="pack",
    )
    for step in range(1, STEPS + 1):
        known = step > 1
        cut = lax.ppermute(cut, "rad", [(0, 1), (1, 0)])
        offset = rot_offset[0] * step % (cells * size)
        block, start = facing_block(edge, offset, radial_index)
        place = start.astype(jnp.int32).reshape(1)
        message = array(2, SWEEPS if known else SLOTS, span, lanes)
        last, first = call(
            later_edges if known else first_edges,
            (message, message),
            [vmem] * 4 + [anywhere],
            [vmem] * 2,
            [scratch(cells, lanes), pltpu.SemaphoreType.DMA, columns, columns]
            + ([] if known else [three] * 2),
            (*ends, cut, block),
            12,
            name="edges",
        )
        left = lax.ppermute(last, "az", ring(size, 1))
        right = lax.ppermute(first, "az", ring(size, -1))
        result = pltpu.HBM(pressure.shape, jnp.float32)
        outs = (result, stash, tiles, array(cells, TILE, lanes))
        out_specs = [hbm] + [vmem] * 3
        if not known:
            outs += (array(2, cells_in, SWEEPS, lanes), kept_ends, kept_ends, kept, kept)
            out_specs += [vmem] * 3 + [hbm] * 2
        inner, saved, inner_tiles, w_tile, *made = call(
            later_interior if known else first_interior,
            outs,
            [hbm] * 3 + [vmem],
            out_specs,
            [
                scratch(SWEEPS, 2, cells, rows, lanes),
                scratch(2, cells_in, radial_cells, lanes),
                scratch(*kept.shape),
                scratch(*kept.shape),
                pltpu.SemaphoreType.DMA((3,)),
            ],
            (*fields, cut),
            44,
            name="interior",
        )
        if not known:
            inner_cut, b_ends, w_ends, shift, weight = made
            beyond = (left, right)
        operands = (
            place,
            b_ends,
            w_ends,
            w_tile,
            saved,
            block,
            inner_tiles,
            left,
            right,
        )
        operands += beyond if known else (inner_cut,)
        outs = result
        if not known:
            outs = (
                result,
                array(1, 2, cells, SWEEPS, lanes),
                array(cells, lanes),
                array(2, 2, SWEEPS, radial_cells, lanes),
            )
        pressure = call(
            functools.partial(finish, known),
            outs,
            [smem] + [vmem] * (len(operands) - 1) + [hbm],
            hbm if known else [hbm] + [vmem] * 3,
            [
                scratch(SWEEPS, 2, 2, SWEEPS, rows, lanes),
                scratch(2, 2, SWEEPS, radial_cells, lanes),
                scratch(*tiles.shape),
                scratch(2, 2, 2, rows, lanes),
                scratch(2, 2, 2, rows, lanes),
                scratch(3 * cells, lanes),
                scratch(cells + 2 * (SWEEPS - 1), TILE, lanes),
                pltpu.SemaphoreType.DMA((5,)),
            ],
            (*operands, inner),
            26,
            input_output_aliases={len(operands): 0},
            name="finish",
        )
        if not known:
            pressure, cut, edge, ends_now = pressure
            fields = tuple(pinned(x) for x in (pressure, shift, weight))
            ends = (ends_now, b_ends, w_ends)
    return pressure


def solution(mesh):
    placed = (
        P(None, "az", "rad", None),
        P(None, "az", "rad", None),
        P(None, "az", "rad", None),
        P(),
    )
    return jax.shard_map(
        per_device,
        mesh=mesh,
        in_specs=placed,
        out_specs=P(None, "az", "rad", None),
        check_vma=False,
    )
```

profile of v0, /device:TPU:1, one launch (start us, length us, event | category | flops | bytes accessed | tf_op | source)
XLA Modules:
  0.0 59.9 jit_solution(3724550275200697586)
XLA Ops:
  0.0 1.8 %pack.1 = (f32[3,2,16,4,128]{4,3,2,1,0:T(4,128)S(1)}, f32[16,128]{1,0:T(8,128)S(1)}, f32[2,2,4,96,128]{4,3,2,1,0:T(8,128)S(1)}, f32[2,2,3,96,128]{4,3,2,1,0:T(8,128)S(1)}, f32[2,2,3,96,128]{4,3,2,1,0:T(8,128)S(1)}) custom-call(f32[2,16,96,128]{3,2,1,0:T(8,128)} %p_ref.3, f32[2,16,96,128]{3,2,1,0:T(8,128)} %s_ref.3, f32[2,16,96,128]{3,2,1,0:T(8,128)} %d_ref.3), custom_call_target="tpu_custom_call" | custom-call | flops 319488 | bytes 212992 | tf_op jit(solution)/shard_map/pack/pallas_call | solution.py:560
  1.8 2.1 %collective-permute-start.32 = (f32[3,2,16,4,128]{4,3,2,1,0:T(4,128)S(1)}, f32[3,2,16,4,128]{4,3,2,1,0:T(4,128)S(1)}, u32[]{:S(2)}, u32[]{:S(2)}) collective-permute-start(f32[3,2,16,4,128]{4,3,2,1,0:T(4,128)S(1)} %get-tuple-element.97), channel_id=1, source_target_pairs={{0,1},{1,0},{2,3},{3,2},{4,5},{5,4},{6,7},{7,6},{8,9},{9,8},{10,11... | collective-permute-start | bytes 589832 | tf_op jit(solution)/shard_map/ppermute | solution.py:596
  4.7 6.9 %conditional.2 = (f32[16,128]{1,0:T(8,128)}) conditional(s32[]{:T(128)} %clamp.6, f32[16,128]{1,0:T(8,128)S(1)} %get-tuple-element.102, f32[16,128]{1,0:T(8,128)S(1)} %get-tuple-element.102, f32[16,128]{1,0:T(8,128)S(1)} %get-tuple-element.102, f32[16,128]{1,0:T(8,128)S(1)} %get-tuple-element.102, ...), branch_computations={%region_0.1_spmd, %region_1.2_spmd, %region_2.3_spmd, %region_3.4_... | conditional | bytes 32816 | solution.py:527
  4.7 5.1 %collective-permute-start.3 = (f32[16,128]{1,0:T(8,128)S(1)}, f32[16,128]{1,0:T(8,128)}, u32[]{:S(2)}, u32[]{:S(2)}) collective-permute-start(f32[16,128]{1,0:T(8,128)S(1)} %param.3), channel_id=1, source_target_pairs={{27,0},{6,1},{29,2},{8,3},{31,4},{10,5},{1,6},{12,7},{3,8},{14,9},... | collective-permute-start | bytes 24584 | tf_op jit(solution)/shard_map/cond/branch_3_fun/ppermute | solution.py:523
  9.8 1.7 %collective-permute-done.3 = f32[16,128]{1,0:T(8,128)} collective-permute-done((f32[16,128]{1,0:T(8,128)S(1)}, f32[16,128]{1,0:T(8,128)}, u32[]{:S(2)}, u32[]{:S(2)}) %collective-permute-start.3) | collective-permute-done | bytes 8224 | tf_op jit(solution)/shard_map/cond/branch_3_fun/ppermute | solution.py:523
  11.6 0.0 collective-permute-done.32.cut_ref
  11.6 2.6 %edges.2 = (f32[2,6,104,128]{3,2,1,0:T(8,128)}, f32[2,6,104,128]{3,2,1,0:T(8,128)}) custom-call(f32[2,2,4,96,128]{4,3,2,1,0:T(8,128)S(1)} %get-tuple-element.104.p_ends, f32[2,2,3,96,128]{4,3,2,1,0:T(8,128)S(1)} %get-tuple-element.105.s_ends, f32[2,2,3,96,128]{4,3,2,1,0:T(8,128)S(1)} %get-tuple-element.106.d_ends, ...), custom_call_target="tpu_custom_call" | custom-call | flops 3833856 | bytes 2555904 | tf_op jit(solution)/shard_map/edges/pallas_call | solution.py:560
  14.2 1.2 %collective-permute-start.33 = (f32[2,6,104,128]{3,2,1,0:T(8,128)}, f32[2,6,104,128]{3,2,1,0:T(8,128)S(1)}, u32[]{:S(2)}, u32[]{:S(2)}) collective-permute-start(f32[2,6,104,128]{3,2,1,0:T(8,128)} %get-tuple-element.107), channel_id=1, source_target_pairs={{0,2},{2,4},{4,6},{6,8},{8,10},{10,12},{12,14},{14,16},{16,18},{18... | collective-permute-start | bytes 1916936 | tf_op jit(solution)/shard_map/ppermute | solution.py:612
  15.4 0.0 collective-permute-start.34
  15.4 8.2 %interior.2 = (f32[2,16,96,128]{3,2,1,0:T(8,128)}, f32[2,4,2,2,128,128]{5,4,3,2,1,0:T(8,128)S(1)}, f32[8,8,128]{2,1,0:T(8,128)S(1)}, f32[16,8,128]{2,1,0:T(8,128...) custom-call(f32[2,16,96,128]{3,2,1,0:T(8,128)} %p_ref.3, ...), custom_call_target="tpu_custom_call" | custom-call | flops 14057472 | bytes 9371648 | tf_op jit(solution)/shard_map/interior/pallas_call | solution.py:560
  23.5 6.4 %collective-permute-done.33.left_ref.rest_0_ = f32[2,6,104,128]{3,2,1,0:T(8,128)S(1)} collective-permute-done((f32[2,6,104,128]{3,2,1,0:T(8,128)}, f32[2,6,104,128]{3,2,1,0:T(8,128)S(1)}, u32[]{:S(2)}, u32[]{:S(2)}) %collective-permute-start.33) | collective-permute-done | bytes 639008 | tf_op jit(solution)/shard_map/ppermute | solution.py:612
  29.9 2.4 %collective-permute-done.34.right_ref.rest_1_ = f32[2,6,104,128]{3,2,1,0:T(8,128)S(1)} collective-permute-done((f32[2,6,104,128]{3,2,1,0:T(8,128)}, f32[2,6,104,128]{3,2,1,0:T(8,128)S(1)}, u32[]{:S(2)}, u32[]{:S(2)}) %collective-permute-start.34) | collective-permute-done | bytes 639008 | tf_op jit(solution)/shard_map/ppermute | solution.py:613
  32.3 3.2 %finish.2 = (f32[2,16,96,128]{3,2,1,0:T(8,128)}, f32[1,2,16,4,128]{4,3,2,1,0:T(4,128)S(1)}, f32[16,128]{1,0:T(8,128)S(1)}, f32[2,2,4,96,128]{4,3,2,1,0:T(8,128)S(1)}) custom-call(s32[1]{0:T(128)} %bitcast.2.start_ref, f32[2,2,4,104,128]{4,3,2,1,0:T(8,128)S(1)} %get-tuple-element.98.b_ends, ...), custom_call_target="tpu_custom_call", output_to_operand_aliasing={{0}: (10, {})} | custom-call | flops 8306688 | bytes 5537792 | tf_op jit(solution)/shard_map/finish/pallas_call | solution.py:560
  35.5 0.0 copy-start
  35.5 0.9 %copy-done = f32[2,2,4,96,128]{4,3,2,1,0:T(8,128)} copy-done((f32[2,2,4,96,128]{4,3,2,1,0:T(8,128)}, f32[2,2,4,96,128]{4,3,2,1,0:T(8,128)S(1)}, u32[]{:S(2)}) %copy-start) | copy-done | bytes 786456
  36.4 0.0 collective-permute-start.35
  36.4 5.9 %conditional.3 = (f32[16,128]{1,0:T(8,128)}) conditional(s32[]{:T(128)} %clamp.7, f32[16,128]{1,0:T(8,128)S(1)} %get-tuple-element.117, f32[16,128]{1,0:T(8,128)S(1)} %get-tuple-element.117, f32[16,128]{1,0:T(8,128)S(1)} %get-tuple-element.117, f32[16,128]{1,0:T(8,128)S(1)} %get-tuple-element.117, ...), branch_computations={%region_16.17_spmd, %region_17.18_spmd, %region_18.19_spmd, %regio... | conditional | bytes 32816 | solution.py:527
  36.4 5.9 %collective-permute-done.21 = f32[16,128]{1,0:T(8,128)} collective-permute-done((f32[16,128]{1,0:T(8,128)S(1)}, f32[16,128]{1,0:T(8,128)}, u32[]{:S(2)}, u32[]{:S(2)}) %collective-permute-start.21) | collective-permute-done | bytes 8224 | tf_op jit(solution)/shard_map/cond/branch_5_fun/ppermute | solution.py:523
  42.2 1.1 %copy-done.1 = f32[2,2,4,96,128]{4,3,2,1,0:T(8,128)S(1)} copy-done((f32[2,2,4,96,128]{4,3,2,1,0:T(8,128)S(1)}, f32[2,2,4,96,128]{4,3,2,1,0:T(8,128)}, u32[]{:S(2)}) %copy-start.1) | copy-done | bytes 786456
  43.4 1.8 %edges.3 = (f32[2,4,104,128]{3,2,1,0:T(8,128)}, f32[2,4,104,128]{3,2,1,0:T(8,128)}) custom-call(f32[2,2,4,96,128]{4,3,2,1,0:T(8,128)S(1)} %copy-done.1, f32[2,2,4,104,128]{4,3,2,1,0:T(8,128)S(1)} %get-tuple-element.98.b_ends, f32[2,2,4,104,128]{4,3,2,1,0:T(8,128)S(1)} %get-tuple-element.99.w_ends, f32[1,2,16,4,128]{4,3,2,1,0:T(4,128)S(1)} %collective-permute-done.35.cut_ref, ...), custom_call_target="tpu_custom_call" | custom-call | flops 3833856 | bytes 2555904 | tf_op jit(solution)/shard_map/edges/pallas_call | solution.py:560
  45.2 1.2 %collective-permute-start.36 = (f32[2,4,104,128]{3,2,1,0:T(8,128)}, f32[2,4,104,128]{3,2,1,0:T(8,128)S(1)}, u32[]{:S(2)}, u32[]{:S(2)}) collective-permute-start(f32[2,4,104,128]{3,2,1,0:T(8,128)} %get-tuple-element.120), channel_id=1, source_target_pairs={{0,2},{2,4},{4,6},{6,8},{8,10},{10,12},{12,14},{14,16},{16,18},{18... | collective-permute-start | bytes 1277960 | tf_op jit(solution)/shard_map/ppermute | solution.py:612
  46.4 7.7 %interior.3 = (f32[2,16,96,128]{3,2,1,0:T(8,128)}, f32[2,4,2,2,128,128]{5,4,3,2,1,0:T(8,128)S(1)}, f32[8,8,128]{2,1,0:T(8,128)S(1)}, f32[16,8,128]{2,1,0:T(8,128)S(1)}) custom-call(f32[2,16,96,128]{3,2,1,0:T(8,128)} %get-tuple-element.111.p_ref, f32[2,16,104,128]{3,2,1,0:T(8,128)} %get-tuple-element.112.b_ref, f32[2,16,104,128]{3,2,1,0:T(8,128)} %get-tuple-element.113.w_ref, ...), custom_call_target="tpu_custom_call" | custom-call | flops 14057472 | bytes 9371648 | tf_op jit(solution)/shard_map/interior/pallas_call | solution.py:560
  54.1 2.3 %collective-permute-done.36.left_ref = f32[2,4,104,128]{3,2,1,0:T(8,128)S(1)} collective-permute-done((f32[2,4,104,128]{3,2,1,0:T(8,128)}, f32[2,4,104,128]{3,2,1,0:T(8,128)S(1)}, u32[]{:S(2)}, u32[]{:S(2)}) %collective-permute-start.36) | collective-permute-done | bytes 426016 | tf_op jit(solution)/shard_map/ppermute | solution.py:612
  56.4 3.3 %finish.3 = f32[2,16,96,128]{3,2,1,0:T(8,128)} custom-call(s32[1]{0:T(128)} %bitcast.1.start_ref, f32[2,2,4,104,128]{4,3,2,1,0:T(8,128)S(1)} %get-tuple-element.98.b_ends, f32[2,2,4,104,128]{4,3,2,1,0:T(8,128)S(1)} %get-tuple-element.99.w_ends, f32[16,8,128]{2,1,0:T(8,128)S(1)} %get-tuple-element.115.w_tile, ...), custom_call_target="tpu_custom_call", output_to_operand_aliasing={{}: (11, {})} | custom-call | flops 8306688 | bytes 5537792 | tf_op jit(solution)/shard_map/finish/pallas_call | solution.py:560
  (5 shorter events, 0.0 us)
Async XLA Ops:
  1.8 9.7 %collective-permute-start.32 = (f32[3,2,16,4,128]{4,3,2,1,0:T(4,128)S(1)}, f32[3,2,16,4,128]{4,3,2,1,0:T(4,128)S(1)}, u32[]{:S(2)}, u32[]{:S(2)}) collective-permute-start(f32[3,2,16,4,128]{4,3,2,1,0:T(4,128)S(1)} %get-tuple-element.97), channel_id=1, source_target_pairs={{0,1},{1,0},{2,3},{3,2},{4,5},{5,4},{6,7},{7,6},{8,9},{9,8},{10,11... | collective-permute-start | bytes 589832 | tf_op jit(solution)/shard_map/ppermute | solution.py:596
  4.7 6.8 %collective-permute-start.3 = (f32[16,128]{1,0:T(8,128)S(1)}, f32[16,128]{1,0:T(8,128)}, u32[]{:S(2)}, u32[]{:S(2)}) collective-permute-start(f32[16,128]{1,0:T(8,128)S(1)} %param.3), channel_id=1, source_target_pairs={{27,0},{6,1},{29,2},{8,3},{31,4},{10,5},{1,6},{12,7},{3,8},{14,9},... | collective-permute-start | bytes 24584 | tf_op jit(solution)/shard_map/cond/branch_3_fun/ppermute | solution.py:523
  14.2 15.7 %collective-permute-start.33 = (f32[2,6,104,128]{3,2,1,0:T(8,128)}, f32[2,6,104,128]{3,2,1,0:T(8,128)S(1)}, u32[]{:S(2)}, u32[]{:S(2)}) collective-permute-start(f32[2,6,104,128]{3,2,1,0:T(8,128)} %get-tuple-element.107), channel_id=1, source_target_pairs={{0,2},{2,4},{4,6},{6,8},{8,10},{10,12},{12,14},{14,16},{16,18},{18... | collective-permute-start | bytes 1916936 | tf_op jit(solution)/shard_map/ppermute | solution.py:612
  15.4 16.9 %collective-permute-start.34 = (f32[2,6,104,128]{3,2,1,0:T(8,128)}, f32[2,6,104,128]{3,2,1,0:T(8,128)S(1)}, u32[]{:S(2)}, u32[]{:S(2)}) collective-permute-start(f32[2,6,104,128]{3,2,1,0:T(8,128)} %get-tuple-element.108), channel_id=1, source_target_pairs={{0,30},{2,0},{4,2},{6,4},{8,6},{10,8},{12,10},{14,12},{16,14},{18,... | collective-permute-start | bytes 1916936 | tf_op jit(solution)/shard_map/ppermute | solution.py:613
  35.5 0.9 %copy-start = (f32[2,2,4,96,128]{4,3,2,1,0:T(8,128)}, f32[2,2,4,96,128]{4,3,2,1,0:T(8,128)S(1)}, u32[]{:S(2)}) copy-start(f32[2,2,4,96,128]{4,3,2,1,0:T(8,128)S(1)} %get-tuple-element.119.p_ends) | copy-start | bytes 2359300
  36.4 5.9 %collective-permute-start.35 = (f32[1,2,16,4,128]{4,3,2,1,0:T(4,128)S(1)}, f32[1,2,16,4,128]{4,3,2,1,0:T(4,128)S(1)}, u32[]{:S(2)}, u32[]{:S(2)}) collective-permute-start(f32[1,2,16,4,128]{4,3,2,1,0:T(4,128)S(1)} %get-tuple-element.114), channel_id=1, source_target_pairs={{0,1},{1,0},{2,3},{3,2},{4,5},{5,4},{6,7},{7,6},{8,9},{9,8},{10,11... | collective-permute-start | bytes 196616 | tf_op jit(solution)/shard_map/ppermute | solution.py:596
  36.4 5.9 %collective-permute-start.21 = (f32[16,128]{1,0:T(8,128)S(1)}, f32[16,128]{1,0:T(8,128)}, u32[]{:S(2)}, u32[]{:S(2)}) collective-permute-start(f32[16,128]{1,0:T(8,128)S(1)} %param.21), channel_id=1, source_target_pairs={{23,0},{10,1},{25,2},{12,3},{27,4},{14,5},{29,6},{16,7},{31,8},{18... | collective-permute-start | bytes 24584 | tf_op jit(solution)/shard_map/cond/branch_5_fun/ppermute | solution.py:523
  42.2 1.1 %copy-start.1 = (f32[2,2,4,96,128]{4,3,2,1,0:T(8,128)S(1)}, f32[2,2,4,96,128]{4,3,2,1,0:T(8,128)}, u32[]{:S(2)}) copy-start(f32[2,2,4,96,128]{4,3,2,1,0:T(8,128)} %copy-done) | copy-start | bytes 2359300
  45.2 11.2 %collective-permute-start.36 = (f32[2,4,104,128]{3,2,1,0:T(8,128)}, f32[2,4,104,128]{3,2,1,0:T(8,128)S(1)}, u32[]{:S(2)}, u32[]{:S(2)}) collective-permute-start(f32[2,4,104,128]{3,2,1,0:T(8,128)} %get-tuple-element.120), channel_id=1, source_target_pairs={{0,2},{2,4},{4,6},{6,8},{8,10},{10,12},{12,14},{14,16},{16,18},{18... | collective-permute-start | bytes 1277960 | tf_op jit(solution)/shard_map/ppermute | solution.py:612
  46.4 10.0 %collective-permute-start.37 = (f32[2,4,104,128]{3,2,1,0:T(8,128)}, f32[2,4,104,128]{3,2,1,0:T(8,128)}, u32[]{:S(2)}, u32[]{:S(2)}) collective-permute-start(f32[2,4,104,128]{3,2,1,0:T(8,128)} %get-tuple-element.121), channel_id=1, source_target_pairs={{0,30},{2,0},{4,2},{6,4},{8,6},{10,8},{12,10},{14,12},{16,14},{18,... | collective-permute-start | bytes 1277960 | tf_op jit(solution)/shard_map/ppermute | solution.py:613
where the time goes:
time: 59.7 us; the launch traced here: 59.9 us
  Pallas kernels  28.6 us (48%)
  waiting for transfers between devices  18.6 us (31%)
  starting transfers between devices  9.67 us (16%)
  local copies, waits for them, and re-layouts  2.01 us (3%)
  between operations  0.95 us (2%)
    pallas_call x7, Pallas kernels, call(): pl.pallas_call(kernel, out_shape=out_shape, in_specs=in_specs, out_specs=...  28.6 us
    ppermute x2, waiting for transfers between devices, per_device(): left = lax.ppermute(last, 'az', ring(size, 1))  8.6 us
    ppermute x2, waiting for transfers between devices, branch(): return lambda e: lax.ppermute(e, ('az', 'rad'), facing_pairs(size, t))  7.62 us
    ppermute x2, starting transfers between devices, branch(): return lambda e: lax.ppermute(e, ('az', 'rad'), facing_pairs(size, t))  5.1 us
    ppermute x2, starting transfers between devices, per_device(): left = lax.ppermute(last, 'az', ring(size, 1))  2.42 us
    ppermute x2, waiting for transfers between devices, per_device(): right = lax.ppermute(first, 'az', ring(size, -1))  2.38 us
    ppermute x2, starting transfers between devices, per_device(): cut = lax.ppermute(cut, 'rad', [(0, 1), (1, 0)])  2.14 us
    unnamed x4, local copies, waits for them, and re-layouts  2.01 us
  transfers between devices with their start and end apart: 8, of which 5 were waited for; matrix products, arithmetic and copies ran while one was open for 0% of the time, Pallas kernels for 26%

commit v1 on v0

--- a/solution.py
+++ b/solution.py
@@ -46,18 +46,36 @@
     )
 
 
-def relaxed(column, side, beside, weight, shift):
-    here = column[side.rows]
-    radial = column[shifted(side.rows, -1)] + column[shifted(side.rows, 1)]
-    nbr = beside + radial + axial_sum(here)
-    kept = (1.0 - OMEGA) * here
-    if shift is not None:
-        kept = kept + shift
-    return kept + weight * nbr
-
-
-def mirror(column, side):
-    column[side.ghost : side.ghost + 1] = column[side.edge : side.edge + 1]
+def neighbour_matrix(lanes):
+    gap = lax.broadcasted_iota(jnp.int32, (lanes, lanes), 0) - lax.broadcasted_iota(
+        jnp.int32, (lanes, lanes), 1
+    )
+    return jnp.where(jnp.abs(gap) == 1, 1.0, 0.0).astype(jnp.bfloat16)
+
+
+def axial_product(x, matrix):
+    high = x.astype(jnp.bfloat16)
+    low = (x - high.astype(jnp.float32)).astype(jnp.bfloat16)
+    return jnp.dot(high, matrix, preferred_element_type=jnp.float32) + jnp.dot(
+        low, matrix, preferred_element_type=jnp.float32
+    )
+
+
+def relax_all(side, matrix, items):
+    by_matrix = len(items) // 4 * 2
+    axial = []
+    if by_matrix:
+        here = jnp.concatenate([item[0][side.rows] for item in items[:by_matrix]], axis=0)
+        product = axial_product(here, matrix)
+        axial = [product[i * side.count : (i + 1) * side.count] for i in range(by_matrix)]
+    for i, (column, beside, weight, shift, take) in enumerate(items):
+        here = column[side.rows]
+        radial = column[shifted(side.rows, -1)] + column[shifted(side.rows, 1)]
+        nbr = beside() + radial + (axial[i] if i < by_matrix else axial_sum(here))
+        kept = (1.0 - OMEGA) * here
+        if shift is not None:
+            kept = kept + shift()
+        take(kept + weight() * nbr)
 
 
 def on_each_side(radial_cells, body):
@@ -97,36 +115,55 @@
 
 def trajectories(side, field, other, weight, shift, messages):
     bufs = (field, other)
+    matrix = neighbour_matrix(field.shape[-1])
+
+    def at(edge, distance, n):
+        return distance - 1 if edge == 0 else n - distance
+
+    for edge in range(2):
+        for k in range(2):
+            for i in range(SWEEPS):
+                close(field.at[edge, k, i], side, k == side.facing)
+    for sweep in range(SWEEPS):
+        src, dst = bufs[sweep % 2], bufs[1 - sweep % 2]
+        items = []
+        for edge, message in enumerate(messages):
+            for k in range(2):
+                message[k, sweep] = src[edge, k, at(edge, 1, SWEEPS), side.rows]
+                for j in range(1, SWEEPS - sweep):
+                    i = at(edge, j, SWEEPS - 1)
+
+                    def beside(edge=edge, k=k, j=j):
+                        total = src[edge, k, at(edge, j + 1, SWEEPS), side.rows]
+                        if j > 1:
+                            total = total + src[edge, k, at(edge, j - 1, SWEEPS), side.rows]
+                        return total
+
+                    def take(new, edge=edge, k=k, j=j):
+                        out = dst.at[edge, k, at(edge, j, SWEEPS)]
+                        out[side.rows] = new
+                        close(out, side, k == side.facing)
+
+                    items.append(
+                        (
+                            src.at[edge, k, at(edge, j, SWEEPS)],
+                            beside,
+                            functools.partial(weight, edge, k, i),
+                            functools.partial(shift, edge, k, i),
+                            take,
+                        )
+                    )
+        relax_all(side, matrix, items)
     for edge, message in enumerate(messages):
-
-        def at(distance, n, edge=edge):
-            return distance - 1 if edge == 0 else n - distance
-
+        if message.shape[1] == SWEEPS:
+            continue
         for k in range(2):
-            facing = k == side.facing
-            for i in range(SWEEPS):
-                close(field.at[edge, k, i], side, facing)
-            for sweep in range(SWEEPS):
-                src, dst = bufs[sweep % 2], bufs[1 - sweep % 2]
-                top = src.at[edge, k, at(1, SWEEPS)]
-                message[k, sweep] = top[side.rows]
-                for j in range(1, SWEEPS - sweep):
-                    here = src.at[edge, k, at(j, SWEEPS)]
-                    beside = src[edge, k, at(j + 1, SWEEPS), side.rows]
-                    if j > 1:
-                        beside = beside + src[edge, k, at(j - 1, SWEEPS), side.rows]
-                    i = at(j, SWEEPS - 1)
-                    out = dst.at[edge, k, at(j, SWEEPS)]
-                    out[side.rows] = relaxed(here, side, beside, weight(edge, k, i), shift(edge, k, i))
-                    close(out, side, facing)
-            if message.shape[1] == SWEEPS:
-                continue
             for i in range(2):
-                message[k, SWEEPS + i] = weight(edge, k, at(1 + i, SWEEPS - 1))
-            if facing:
+                message[k, SWEEPS + i] = weight(edge, k, at(edge, 1 + i, SWEEPS - 1))
+            if k == side.facing:
                 row = side.edge - side.first
                 message[k, SWEEPS + 1, side.spare : side.spare + 1] = weight(
-                    edge, k, at(3, SWEEPS - 1)
+                    edge, k, at(edge, 3, SWEEPS - 1)
                 )[row : row + 1]
 
 
@@ -243,22 +280,39 @@
         for k in range(2):
             for i in range(2):
                 stash[e, 0, k, i] = levels[0, k, first + i]
+    matrix = neighbour_matrix(levels.shape[-1])
     for n in range(SWEEPS):
         final = n == SWEEPS - 1
 
-        def step(j, carry, n=n, final=final):
-            for k in range(2):
-                beside = levels[n, k, j - 1, side.rows] + levels[n, k, j + 1, side.rows]
-                new = relaxed(levels.at[n, k, j], side, beside, weight[k, j], shift[k, j])
-                if final:
-                    last[k, j - SWEEPS] = new[shifted(side.own, -side.first)]
-                else:
-                    levels[n + 1, k, j, side.rows] = new
-                    if k != side.facing:
-                        levels[n + 1, k, j, side.ghost : side.ghost + 1] = new[at : at + 1]
+        def step(i, carry, n=n, final=final):
+            items = []
+            for k in (1, 0):
+                for j in (n + 1 + 2 * i, n + 2 + 2 * i):
+
+                    def beside(k=k, j=j):
+                        return levels[n, k, j - 1, side.rows] + levels[n, k, j + 1, side.rows]
+
+                    def take(new, k=k, j=j):
+                        if final:
+                            last[k, j - SWEEPS] = new[shifted(side.own, -side.first)]
+                            return
+                        levels[n + 1, k, j, side.rows] = new
+                        if k != side.facing:
+                            levels[n + 1, k, j, side.ghost : side.ghost + 1] = new[at : at + 1]
+
+                    items.append(
+                        (
+                            levels.at[n, k, j],
+                            beside,
+                            functools.partial(lambda k, j: weight[k, j], k, j),
+                            functools.partial(lambda k, j: shift[k, j], k, j),
+                            take,
+                        )
+                    )
+            relax_all(side, matrix, items)
             return carry
 
-        lax.fori_loop(n + 1, cells - 1 - n, step, 0, unroll=2)
+        lax.fori_loop(0, cells // 2 - 1 - n, step, 0, unroll=2 if n % 2 else 1)
         if not final:
             for e, first in enumerate((n + 1, cells - 3 - n)):
                 for k in range(2):
@@ -367,10 +421,10 @@
     row = lax.broadcasted_iota(jnp.int32, source.shape[1:], 0)
     weight = [w_tile[j] for j in range(cells)]
     for e in range(2):
-        far = weights[e][facing, SWEEPS + 1, side.spare : side.spare + 1]
+        far = weights[e][facing, 1, side.spare : side.spare + 1]
         beyond = [
-            weights[e][facing, SWEEPS, tile],
-            weights[e][facing, SWEEPS + 1, tile],
+            weights[e][facing, 0, tile],
+            weights[e][facing, 1, tile],
             jnp.where(row == at, far, 0.0),
         ]
         weight = beyond[::-1] + weight if e == 0 else weight + beyond
@@ -391,11 +445,11 @@
 
 def finish(known, start_ref, b_ends, w_ends, w_tile, stash, block_ref, tile_in, left_ref, right_ref, *rest):
     if known:
-        left_w, right_w, _, out_ref, *rest = rest
-        weights = (left_w, right_w)
+        beyond, _, out_ref, *rest = rest
+        weights = (beyond.at[0], beyond.at[1])
     else:
-        cut_in, _, out_ref, cut_out, edge_out, ends_out, *rest = rest
-        weights = (left_ref, right_ref)
+        cut_in, _, out_ref, cut_out, edge_out, ends_out, beyond_out, *rest = rest
+        weights = tuple(x.at[:, pl.ds(SWEEPS, 2)] for x in (left_ref, right_ref))
     levels, last, inner_tiles, near, near2, wide, source, sems = rest
     messages = (left_ref, right_ref)
     cells, radial_cells = out_ref.shape[1:3]
@@ -418,31 +472,51 @@
                     buf[e, k] = jnp.zeros(buf.shape[2:], jnp.float32)
         nears = (near, near2)
 
-        def own_column(n, e, k, d):
+        matrix = neighbour_matrix(levels.shape[-1])
+
+        def own_column(n, e, k, d, take):
             i = d - 1 if e == 0 else SWEEPS - d
-            beside = at(n, e, k, d - 1)[side.rows] + at(n, e, k, d + 1)[side.rows]
-            return relaxed(at(n, e, k, d), side, beside, w_ends[e, k, i], b_ends[e, k, i])
+            return (
+                at(n, e, k, d),
+                lambda: at(n, e, k, d - 1)[side.rows] + at(n, e, k, d + 1)[side.rows],
+                lambda: w_ends[e, k, i],
+                lambda: b_ends[e, k, i],
+                take,
+            )
 
         for n in range(SWEEPS - 1):
             src, dst = nears[n % 2], nears[1 - n % 2]
+            items = []
             for e in range(2):
                 for k in range(2):
                     for d in range(1, n + 2):
-                        levels[n + 1, e, k, d, side.rows] = own_column(n, e, k, d)
-                        close(levels.at[n + 1, e, k, d], side, k == facing)
-                    beside = at(n, e, k, 1)[side.rows]
-                    if n > 0:
-                        beside = beside + src[e, k, 1, side.rows]
-                        new = relaxed(src.at[e, k, 0], side, beside, weights[e][k, SWEEPS], None)
-                    else:
-                        new = weights[e][k, SWEEPS] * beside
-                    dst[e, k, 0, side.rows] = new
-                    levels[n + 1, e, k, 0, side.rows] = messages[e][k, n + 1] + new
-                    close(dst.at[e, k, 0], side, k == facing)
+
+                        def take(new, e=e, k=k, d=d):
+                            levels[n + 1, e, k, d, side.rows] = new
+                            close(levels.at[n + 1, e, k, d], side, k == facing)
+
+                        items.append(own_column(n, e, k, d, take))
+
+                    def take(new, e=e, k=k):
+                        dst[e, k, 0, side.rows] = new
+                        levels[n + 1, e, k, 0, side.rows] = messages[e][k, n + 1] + new
+                        close(dst.at[e, k, 0], side, k == facing)
+
+                    if n == 0:
+                        take(weights[e][k, 0] * at(n, e, k, 1)[side.rows])
+                        continue
+                    items.append(
+                        (
+                            src.at[e, k, 0],
+                            lambda e=e, k=k: at(n, e, k, 1)[side.rows] + src[e, k, 1, side.rows],
+                            lambda e=e, k=k: weights[e][k, 0],
+                            None,
+                            take,
+                        )
+                    )
                     if n == 1:
-                        dst[e, k, 1, side.rows] = (
-                            weights[e][k, SWEEPS + 1] * src[e, k, 0, side.rows]
-                        )
+                        dst[e, k, 1, side.rows] = weights[e][k, 1] * src[e, k, 0, side.rows]
+            relax_all(side, matrix, items)
         copies = []
 
         def store(source, target):
@@ -464,14 +538,21 @@
                         k, pl.ds(SWEEPS, cells - 2 * SWEEPS), pl.ds(side.edge_tile, TILE), :
                     ],
                 )
+            items = []
+            for d in range(1, SWEEPS + 1):
+                for e in range(2):
+                    first = end_columns(e, cells, SWEEPS).start
+
+                    def take(new, e=e, k=k, i=column(e, d) - first, first=first):
+                        new = new[shifted(side.own, -side.first)]
+                        last[e, k, i] = new
+                        if k == facing:
+                            last[e, k, i, tile] = new[tile] + response[first + i]
+
+                    items.append(own_column(SWEEPS - 1, e, k, d, take))
+            relax_all(side, matrix, items)
             for e in range(2):
                 first = end_columns(e, cells, SWEEPS).start
-                for d in range(1, SWEEPS + 1):
-                    new = own_column(SWEEPS - 1, e, k, d)[shifted(side.own, -side.first)]
-                    i = column(e, d) - first
-                    last[e, k, i] = new
-                    if k == facing:
-                        last[e, k, i, tile] = new[tile] + response[first + i]
                 store(last.at[e, k], out_ref.at[k, pl.ds(first, SWEEPS)])
         if not known:
             row = side.edge - OWN
@@ -486,6 +567,8 @@
                 for i in range(SWEEPS):
                     edge_out[first + i : first + i + 1] = last[e, facing, i, row : row + 1]
             ends_out[...] = last[...]
+            for e in range(2):
+                beyond_out[e] = weights[e][...]
         for c in copies:
             c.wait()
 
@@ -635,7 +718,6 @@
         )
         if not known:
             inner_cut, b_ends, w_ends, shift, weight = made
-            beyond = (left, right)
         operands = (
             place,
             b_ends,
@@ -647,7 +729,7 @@
             left,
             right,
         )
-        operands += beyond if known else (inner_cut,)
+        operands += (beyond,) if known else (inner_cut,)
         outs = result
         if not known:
             outs = (
@@ -655,12 +737,13 @@
                 array(1, 2, cells, SWEEPS, lanes),
                 array(cells, lanes),
                 array(2, 2, SWEEPS, radial_cells, lanes),
+                array(2, 2, 2, span, lanes),
             )
         pressure = call(
             functools.partial(finish, known),
             outs,
             [smem] + [vmem] * (len(operands) - 1) + [hbm],
-            hbm if known else [hbm] + [vmem] * 3,
+            hbm if known else [hbm] + [vmem] * 4,
             [
                 scratch(SWEEPS, 2, 2, SWEEPS, rows, lanes),
                 scratch(2, 2, SWEEPS, radial_cells, lanes),
@@ -677,7 +760,7 @@
             name="finish",
         )
         if not known:
-            pressure, cut, edge, ends_now = pressure
+            pressure, cut, edge, ends_now, beyond = pressure
             fields = tuple(pinned(x) for x in (pressure, shift, weight))
             ends = (ends_now, b_ends, w_ends)
     return pressure

time: 59.7 us -> 58.7 us (0.983); the launches traced: 59.9 us -> 58.1 us
  starting transfers between devices: 9.67 us -> 14.6 us
  waiting for transfers between devices: 18.6 us -> 13.8 us
  local copies, waits for them, and re-layouts: 2.01 us -> 0 us
    ppermute x2, waiting for transfers between devices: 7.62 us -> 4.22 us  [branch(): return lambda e: lax.ppermute(e, ('az', 'rad'), facing_pairs(size, t))]
    ppermute x2, starting transfers between devices: 2.42 us -> 5.65 us  [per_device(): left = lax.ppermute(last, 'az', ring(size, 1))]
    ppermute x2, waiting for transfers between devices: 8.6 us -> 6.54 us  [per_device(): left = lax.ppermute(last, 'az', ring(size, 1))]
    unnamed x4 -> x0, local copies, waits for them, and re-layouts: 2.01 us -> none
    ppermute x2, starting transfers between devices: 2.14 us -> 3.06 us  [per_device(): cut = lax.ppermute(cut, 'rad', [(0, 1), (1, 0)])]
    ppermute x2, starting transfers between devices: 5.1 us -> 5.87 us  [branch(): return lambda e: lax.ppermute(e, ('az', 'rad'), facing_pairs(size, t))]
    ppermute x2, waiting for transfers between devices: 2.38 us -> 3.01 us  [per_device(): right = lax.ppermute(first, 'az', ring(size, -1))]
  transfers between devices with their start and end apart: 8 -> 8, of which waited for: 5 -> 5; matrix products, arithmetic and copies ran while one was open for 0% -> 0% of each run, Pallas kernels for 26% -> 27%
where the time goes in v1:
time: 58.7 us; the launch traced here: 58.1 us
  Pallas kernels  28.7 us (49%)
  starting transfers between devices  14.6 us (25%)
  waiting for transfers between devices  13.8 us (24%)
  between operations  0.95 us (2%)
    pallas_call x7, Pallas kernels, call(): pl.pallas_call(kernel, out_shape=out_shape, in_specs=in_specs, out_specs=...  28.7 us
    ppermute x2, waiting for transfers between devices, per_device(): left = lax.ppermute(last, 'az', ring(size, 1))  6.54 us
    ppermute x2, starting transfers between devices, branch(): return lambda e: lax.ppermute(e, ('az', 'rad'), facing_pairs(size, t))  5.87 us
    ppermute x2, starting transfers between devices, per_device(): left = lax.ppermute(last, 'az', ring(size, 1))  5.65 us
    ppermute x2, waiting for transfers between devices, branch(): return lambda e: lax.ppermute(e, ('az', 'rad'), facing_pairs(size, t))  4.22 us
    ppermute x2, starting transfers between devices, per_device(): cut = lax.ppermute(cut, 'rad', [(0, 1), (1, 0)])  3.06 us
    ppermute x2, waiting for transfers between devices, per_device(): right = lax.ppermute(first, 'az', ring(size, -1))  3.01 us
  transfers between devices with their start and end apart: 8, of which 5 were waited for; matrix products, arithmetic and copies ran while one was open for 0% of the time, Pallas kernels for 27%

profile of v1, /device:TPU:1, one launch (start us, length us, event | category | flops | bytes accessed | tf_op | source)
XLA Modules:
  0.0 58.1 jit_solution(3511420473068077451)
XLA Ops:
  0.0 1.8 %pack.1 = (f32[3,2,16,4,128]{4,3,2,1,0:T(4,128)S(1)}, f32[16,128]{1,0:T(8,128)S(1)}, f32[2,2,4,96,128]{4,3,2,1,0:T(8,128)S(1)}, f32[2,2,3,96,128]{4,3,2,1,0:T(8,128)S(1)}, f32[2,2,3,96,128]{4,3,2,1,0:T(8,128)S(1)}) custom-call(f32[2,16,96,128]{3,2,1,0:T(8,128)} %p_ref.3, f32[2,16,96,128]{3,2,1,0:T(8,128)} %s_ref.3, f32[2,16,96,128]{3,2,1,0:T(8,128)} %d_ref.3), custom_call_target="tpu_custom_call" | custom-call | flops 319488 | bytes 212992 | tf_op jit(solution)/shard_map/pack/pallas_call | solution.py:643
  1.8 2.1 %collective-permute-start.32 = (f32[3,2,16,4,128]{4,3,2,1,0:T(4,128)S(1)}, f32[3,2,16,4,128]{4,3,2,1,0:T(4,128)S(1)}, u32[]{:S(2)}, u32[]{:S(2)}) collective-permute-start(f32[3,2,16,4,128]{4,3,2,1,0:T(4,128)S(1)} %get-tuple-element.98), channel_id=1, source_target_pairs={{0,1},{1,0},{2,3},{3,2},{4,5},{5,4},{6,7},{7,6},{8,9},{9,8},{10,11... | collective-permute-start | bytes 589832 | tf_op jit(solution)/shard_map/ppermute | solution.py:679
  4.7 4.6 %conditional.2 = (f32[16,128]{1,0:T(8,128)}) conditional(s32[]{:T(128)} %clamp.6, f32[16,128]{1,0:T(8,128)S(1)} %get-tuple-element.103, f32[16,128]{1,0:T(8,128)S(1)} %get-tuple-element.103, f32[16,128]{1,0:T(8,128)S(1)} %get-tuple-element.103, f32[16,128]{1,0:T(8,128)S(1)} %get-tuple-element.103, ...), branch_computations={%region_0.1_spmd, %region_1.2_spmd, %region_2.3_spmd, %region_3.4_... | conditional | bytes 32816 | solution.py:610
  4.7 2.2 %collective-permute-start.10 = (f32[16,128]{1,0:T(8,128)S(1)}, f32[16,128]{1,0:T(8,128)}, u32[]{:S(2)}, u32[]{:S(2)}) collective-permute-start(f32[16,128]{1,0:T(8,128)S(1)} %param.10), channel_id=1, source_target_pairs={{13,0},{20,1},{15,2},{22,3},{17,4},{24,5},{19,6},{26,7},{21,8},{28... | collective-permute-start | bytes 24584 | tf_op jit(solution)/shard_map/cond/branch_10_fun/ppermute | solution.py:606
  6.9 2.3 %collective-permute-done.10 = f32[16,128]{1,0:T(8,128)} collective-permute-done((f32[16,128]{1,0:T(8,128)S(1)}, f32[16,128]{1,0:T(8,128)}, u32[]{:S(2)}, u32[]{:S(2)}) %collective-permute-start.10) | collective-permute-done | bytes 8224 | tf_op jit(solution)/shard_map/cond/branch_10_fun/ppermute | solution.py:606
  9.3 0.0 collective-permute-done.32.cut_ref
  9.3 2.4 %edges.2 = (f32[2,6,104,128]{3,2,1,0:T(8,128)}, f32[2,6,104,128]{3,2,1,0:T(8,128)}) custom-call(f32[2,2,4,96,128]{4,3,2,1,0:T(8,128)S(1)} %get-tuple-element.105.p_ends, f32[2,2,3,96,128]{4,3,2,1,0:T(8,128)S(1)} %get-tuple-element.106.s_ends, f32[2,2,3,96,128]{4,3,2,1,0:T(8,128)S(1)} %get-tuple-element.107.d_ends, ...), custom_call_target="tpu_custom_call" | custom-call | flops 3833856 | bytes 2555904 | tf_op jit(solution)/shard_map/edges/pallas_call | solution.py:643
  11.7 4.0 %collective-permute-start.33 = (f32[2,6,104,128]{3,2,1,0:T(8,128)}, f32[2,6,104,128]{3,2,1,0:T(8,128)S(1)}, u32[]{:S(2)}, u32[]{:S(2)}) collective-permute-start(f32[2,6,104,128]{3,2,1,0:T(8,128)} %get-tuple-element.108), channel_id=1, source_target_pairs={{0,2},{2,4},{4,6},{6,8},{8,10},{10,12},{12,14},{14,16},{16,18},{18... | collective-permute-start | bytes 1916936 | tf_op jit(solution)/shard_map/ppermute | solution.py:695
  15.7 0.0 collective-permute-start.34
  15.7 8.0 %interior.2 = (f32[2,16,96,128]{3,2,1,0:T(8,128)}, f32[2,4,2,2,128,128]{5,4,3,2,1,0:T(8,128)S(1)}, f32[8,8,128]{2,1,0:T(8,128)S(1)}, f32[16,8,128]{2,1,0:T(8,128...) custom-call(f32[2,16,96,128]{3,2,1,0:T(8,128)} %p_ref.3, ...), custom_call_target="tpu_custom_call" | custom-call | flops 14057472 | bytes 9371648 | tf_op jit(solution)/shard_map/interior/pallas_call | solution.py:643
  23.7 6.5 %collective-permute-done.33.left_ref = f32[2,6,104,128]{3,2,1,0:T(8,128)S(1)} collective-permute-done((f32[2,6,104,128]{3,2,1,0:T(8,128)}, f32[2,6,104,128]{3,2,1,0:T(8,128)S(1)}, u32[]{:S(2)}, u32[]{:S(2)}) %collective-permute-start.33) | collective-permute-done | bytes 639008 | tf_op jit(solution)/shard_map/ppermute | solution.py:695
  30.2 2.5 %collective-permute-done.34.right_ref = f32[2,6,104,128]{3,2,1,0:T(8,128)} collective-permute-done((f32[2,6,104,128]{3,2,1,0:T(8,128)}, f32[2,6,104,128]{3,2,1,0:T(8,128)}, u32[]{:S(2)}, u32[]{:S(2)}) %collective-permute-start.34) | collective-permute-done | bytes 639008 | tf_op jit(solution)/shard_map/ppermute | solution.py:696
  32.7 4.2 %finish.2 = (f32[2,16,96,128]{3,2,1,0:T(8,128)}, f32[1,2,16,4,128]{4,3,2,1,0:T(4,128)}, f32[16,128]{1,0:T(8,128)}, f32[2,2,4,96,128]{4,3,2,1,0:T(8,128)S(1)}, f32[2,2,2,104,128]{4,3,2,1,0:T(8,128)S(1)}) custom-call(s32[1]{0:T(128)} %bitcast.2.start_ref, f32[2,2,4,104,128]{4,3,2,1,0:T(8,128)S(1)} %get-tuple-element.99.b_ends, ...), custom_call_target="tpu_custom_call", output_to_operand_aliasing={{0}: (10, {})} | custom-call | flops 8306688 | bytes 5537792 | tf_op jit(solution)/shard_map/finish/pallas_call | solution.py:643
  37.0 0.9 %collective-permute-start.35 = (f32[1,2,16,4,128]{4,3,2,1,0:T(4,128)}, f32[1,2,16,4,128]{4,3,2,1,0:T(4,128)S(1)}, u32[]{:S(2)}, u32[]{:S(2)}) collective-permute-start(f32[1,2,16,4,128]{4,3,2,1,0:T(4,128)} %get-tuple-element.115), channel_id=1, source_target_pairs={{0,1},{1,0},{2,3},{3,2},{4,5},{5,4},{6,7},{7,6},{8,9},{9,8},{10,11... | collective-permute-start | bytes 196616 | tf_op jit(solution)/shard_map/ppermute | solution.py:679
  37.9 5.5 %conditional.3 = (f32[16,128]{1,0:T(8,128)}) conditional(s32[]{:T(128)} %clamp.7, f32[16,128]{1,0:T(8,128)} %get-tuple-element.118, f32[16,128]{1,0:T(8,128)} %get-tuple-element.118, f32[16,128]{1,0:T(8,128)} %get-tuple-element.118, f32[16,128]{1,0:T(8,128)} %get-tuple-element.118, ...), branch_computations={%region_16.17_spmd, %region_17.18_spmd, %region_18.19_spmd, %regio... | conditional | bytes 32816 | solution.py:610
  37.9 3.6 %collective-permute-start.20 = (f32[16,128]{1,0:T(8,128)}, f32[16,128]{1,0:T(8,128)}, u32[]{:S(2)}, u32[]{:S(2)}) collective-permute-start(f32[16,128]{1,0:T(8,128)} %param.20), channel_id=1, source_target_pairs={{25,0},{8,1},{27,2},{10,3},{29,4},{12,5},{31,6},{14,7},{1,8},{16,9... | collective-permute-start | bytes 24584 | tf_op jit(solution)/shard_map/cond/branch_4_fun/ppermute | solution.py:606
  41.5 1.9 %collective-permute-done.20 = f32[16,128]{1,0:T(8,128)} collective-permute-done((f32[16,128]{1,0:T(8,128)}, f32[16,128]{1,0:T(8,128)}, u32[]{:S(2)}, u32[]{:S(2)}) %collective-permute-start.20) | collective-permute-done | bytes 8224 | tf_op jit(solution)/shard_map/cond/branch_4_fun/ppermute | solution.py:606
  43.4 1.8 %edges.3 = (f32[2,4,104,128]{3,2,1,0:T(8,128)}, f32[2,4,104,128]{3,2,1,0:T(8,128)S(1)}) custom-call(f32[2,2,4,96,128]{4,3,2,1,0:T(8,128)S(1)} %get-tuple-element.120.p_ends, f32[2,2,4,104,128]{4,3,2,1,0:T(8,128)S(1)} %get-tuple-element.99.b_ends, f32[2,2,4,104,128]{4,3,2,1,0:T(8,128)S(1)} %get-tuple-element.100.w_ends, ...), custom_call_target="tpu_custom_call" | custom-call | flops 3833856 | bytes 2555904 | tf_op jit(solution)/shard_map/edges/pallas_call | solution.py:643
  45.2 1.6 %collective-permute-start.36 = (f32[2,4,104,128]{3,2,1,0:T(8,128)}, f32[2,4,104,128]{3,2,1,0:T(8,128)S(1)}, u32[]{:S(2)}, u32[]{:S(2)}) collective-permute-start(f32[2,4,104,128]{3,2,1,0:T(8,128)} %get-tuple-element.121), channel_id=1, source_target_pairs={{0,2},{2,4},{4,6},{6,8},{8,10},{10,12},{12,14},{14,16},{16,18},{18... | collective-permute-start | bytes 1277960 | tf_op jit(solution)/shard_map/ppermute | solution.py:695
  46.8 0.0 collective-permute-start.37
  46.8 7.5 %interior.3 = (f32[2,16,96,128]{3,2,1,0:T(8,128)}, f32[2,4,2,2,128,128]{5,4,3,2,1,0:T(8,128)S(1)}, f32[8,8,128]{2,1,0:T(8,128)S(1)}, f32[16,8,128]{2,1,0:T(8,128)S(1)}) custom-call(f32[2,16,96,128]{3,2,1,0:T(8,128)} %get-tuple-element.112.p_ref, f32[2,16,104,128]{3,2,1,0:T(8,128)} %get-tuple-element.113.b_ref, f32[2,16,104,128]{3,2,1,0:T(8,128)} %get-tuple-element.114.w_ref, ...), custom_call_target="tpu_custom_call" | custom-call | flops 14057472 | bytes 9371648 | tf_op jit(solution)/shard_map/interior/pallas_call | solution.py:643
  54.3 0.0 collective-permute-done.36.left_ref
  54.3 0.5 collective-permute-done.37.right_ref
  54.8 3.1 %finish.3 = f32[2,16,96,128]{3,2,1,0:T(8,128)} custom-call(s32[1]{0:T(128)} %bitcast.1.start_ref, f32[2,2,4,104,128]{4,3,2,1,0:T(8,128)S(1)} %get-tuple-element.99.b_ends, f32[2,2,4,104,128]{4,3,2,1,0:T(8,128)S(1)} %get-tuple-element.100.w_ends, f32[16,8,128]{2,1,0:T(8,128)S(1)} %get-tuple-element.116.w_tile, ...), custom_call_target="tpu_custom_call", output_to_operand_aliasing={{}: (10, {})} | custom-call | flops 8306688 | bytes 5537792 | tf_op jit(solution)/shard_map/finish/pallas_call | solution.py:643
  (1 shorter events, 0.0 us)
Async XLA Ops:
  1.8 7.5 %collective-permute-start.32 = (f32[3,2,16,4,128]{4,3,2,1,0:T(4,128)S(1)}, f32[3,2,16,4,128]{4,3,2,1,0:T(4,128)S(1)}, u32[]{:S(2)}, u32[]{:S(2)}) collective-permute-start(f32[3,2,16,4,128]{4,3,2,1,0:T(4,128)S(1)} %get-tuple-element.98), channel_id=1, source_target_pairs={{0,1},{1,0},{2,3},{3,2},{4,5},{5,4},{6,7},{7,6},{8,9},{9,8},{10,11... | collective-permute-start | bytes 589832 | tf_op jit(solution)/shard_map/ppermute | solution.py:679
  4.7 4.6 %collective-permute-start.10 = (f32[16,128]{1,0:T(8,128)S(1)}, f32[16,128]{1,0:T(8,128)}, u32[]{:S(2)}, u32[]{:S(2)}) collective-permute-start(f32[16,128]{1,0:T(8,128)S(1)} %param.10), channel_id=1, source_target_pairs={{13,0},{20,1},{15,2},{22,3},{17,4},{24,5},{19,6},{26,7},{21,8},{28... | collective-permute-start | bytes 24584 | tf_op jit(solution)/shard_map/cond/branch_10_fun/ppermute | solution.py:606
  11.7 18.6 %collective-permute-start.33 = (f32[2,6,104,128]{3,2,1,0:T(8,128)}, f32[2,6,104,128]{3,2,1,0:T(8,128)S(1)}, u32[]{:S(2)}, u32[]{:S(2)}) collective-permute-start(f32[2,6,104,128]{3,2,1,0:T(8,128)} %get-tuple-element.108), channel_id=1, source_target_pairs={{0,2},{2,4},{4,6},{6,8},{8,10},{10,12},{12,14},{14,16},{16,18},{18... | collective-permute-start | bytes 1916936 | tf_op jit(solution)/shard_map/ppermute | solution.py:695
  15.7 17.0 %collective-permute-start.34 = (f32[2,6,104,128]{3,2,1,0:T(8,128)}, f32[2,6,104,128]{3,2,1,0:T(8,128)}, u32[]{:S(2)}, u32[]{:S(2)}) collective-permute-start(f32[2,6,104,128]{3,2,1,0:T(8,128)} %get-tuple-element.109), channel_id=1, source_target_pairs={{0,30},{2,0},{4,2},{6,4},{8,6},{10,8},{12,10},{14,12},{16,14},{18,... | collective-permute-start | bytes 1916936 | tf_op jit(solution)/shard_map/ppermute | solution.py:696
  37.0 6.4 %collective-permute-start.35 = (f32[1,2,16,4,128]{4,3,2,1,0:T(4,128)}, f32[1,2,16,4,128]{4,3,2,1,0:T(4,128)S(1)}, u32[]{:S(2)}, u32[]{:S(2)}) collective-permute-start(f32[1,2,16,4,128]{4,3,2,1,0:T(4,128)} %get-tuple-element.115), channel_id=1, source_target_pairs={{0,1},{1,0},{2,3},{3,2},{4,5},{5,4},{6,7},{7,6},{8,9},{9,8},{10,11... | collective-permute-start | bytes 196616 | tf_op jit(solution)/shard_map/ppermute | solution.py:679
  37.9 5.5 %collective-permute-start.20 = (f32[16,128]{1,0:T(8,128)}, f32[16,128]{1,0:T(8,128)}, u32[]{:S(2)}, u32[]{:S(2)}) collective-permute-start(f32[16,128]{1,0:T(8,128)} %param.20), channel_id=1, source_target_pairs={{25,0},{8,1},{27,2},{10,3},{29,4},{12,5},{31,6},{14,7},{1,8},{16,9... | collective-permute-start | bytes 24584 | tf_op jit(solution)/shard_map/cond/branch_4_fun/ppermute | solution.py:606
  45.2 9.1 %collective-permute-start.36 = (f32[2,4,104,128]{3,2,1,0:T(8,128)}, f32[2,4,104,128]{3,2,1,0:T(8,128)S(1)}, u32[]{:S(2)}, u32[]{:S(2)}) collective-permute-start(f32[2,4,104,128]{3,2,1,0:T(8,128)} %get-tuple-element.121), channel_id=1, source_target_pairs={{0,2},{2,4},{4,6},{6,8},{8,10},{10,12},{12,14},{14,16},{16,18},{18... | collective-permute-start | bytes 1277960 | tf_op jit(solution)/shard_map/ppermute | solution.py:695
  46.8 8.1 %collective-permute-start.37 = (f32[2,4,104,128]{3,2,1,0:T(8,128)S(1)}, f32[2,4,104,128]{3,2,1,0:T(8,128)S(1)}, u32[]{:S(2)}, u32[]{:S(2)}) collective-permute-start(f32[2,4,104,128]{3,2,1,0:T(8,128)S(1)} %get-tuple-element.122), channel_id=1, source_target_pairs={{0,30},{2,0},{4,2},{6,4},{8,6},{10,8},{12,10},{14,12},{16,14},{18,... | collective-permute-start | bytes 1277960 | tf_op jit(solution)/shard_map/ppermute | solution.py:696

commit v2 on v1

--- a/solution.py
+++ b/solution.py
@@ -404,7 +404,7 @@
     on_each_side(radial_cells, body)
 
 
-def ghost_response(side, start_ref, w_tile, block_ref, messages, weights, wide, source):
+def ghost_response(side, step, turn_ref, w_tile, block_ref, messages, weights, wide, source):
     facing = side.facing
     cells = w_tile.shape[0]
     reach = SWEEPS - 1
@@ -416,8 +416,11 @@
         wide[2 * cells + i : 2 * cells + i + 1] = messages[1][facing, slot, row : row + 1]
     wide[cells : 2 * cells] = block_ref[...]
     source[...] = jnp.zeros(source.shape, jnp.float32)
+    offset = lax.rem(turn_ref[0] * step, cells * lax.axis_size("az"))
+    rest = offset - lax.div(offset + cells // 2, cells) * cells
+    start = cells - reach + (-rest if side.low else rest)
     for c in range(cells + 2 * reach):
-        source[c, at : at + 1] = wide[pl.ds(start_ref[0] + c, 1), :]
+        source[c, at : at + 1] = wide[pl.ds(start + c, 1), :]
     row = lax.broadcasted_iota(jnp.int32, source.shape[1:], 0)
     weight = [w_tile[j] for j in range(cells)]
     for e in range(2):
@@ -443,7 +446,8 @@
     return response[reach : reach + cells]
 
 
-def finish(known, start_ref, b_ends, w_ends, w_tile, stash, block_ref, tile_in, left_ref, right_ref, *rest):
+def finish(step, turn_ref, b_ends, w_ends, w_tile, stash, block_ref, tile_in, left_ref, right_ref, *rest):
+    known = step > 1
     if known:
         beyond, _, out_ref, *rest = rest
         weights = (beyond.at[0], beyond.at[1])
@@ -528,7 +532,7 @@
         for k in (1 - facing, facing):
             if k == facing:
                 response = ghost_response(
-                    side, start_ref, w_tile, block_ref, messages, weights, wide, source
+                    side, step, turn_ref, w_tile, block_ref, messages, weights, wide, source
                 )
                 for i in range(cells - 2 * SWEEPS):
                     inner_tiles[i] = tile_in[i] + response[SWEEPS + i]
@@ -591,12 +595,10 @@
     return [(2 * i + r, 2 * ((i + (2 * r - 1) * turn) % size) + r) for i in range(size) for r in range(2)]
 
 
-def facing_block(edge, offset, radial_index):
+def facing_block(edge, offset):
     size = lax.axis_size("az")
     cells = edge.shape[0]
-    turn = (offset + cells // 2) // cells
-    rest = offset - turn * cells
-    turn = turn % size
+    turn = (offset + cells // 2) // cells % size
     near = min(size, 16)
 
     def far(t):
@@ -607,14 +609,12 @@
 
     if size > near:
         edge = lax.switch(turn // near, [far(t) for t in range(-(-size // near))], edge)
-    block = lax.switch(turn % near, [branch(t) for t in range(near)], edge)
-    return block, cells - (SWEEPS - 1) + jnp.where(radial_index == 0, -rest, rest)
+    return lax.switch(turn % near, [branch(t) for t in range(near)], edge)
 
 
 def per_device(pressure, source, diagonal, rot_offset):
     _, cells, radial_cells, lanes = pressure.shape
     size = lax.axis_size("az")
-    radial_index = lax.axis_index("rad")
     rows, span = radial_cells + 4 * TILE, radial_cells + TILE
 
     def array(*shape):
@@ -678,8 +678,7 @@
         known = step > 1
         cut = lax.ppermute(cut, "rad", [(0, 1), (1, 0)])
         offset = rot_offset[0] * step % (cells * size)
-        block, start = facing_block(edge, offset, radial_index)
-        place = start.astype(jnp.int32).reshape(1)
+        block = facing_block(edge, offset)
         message = array(2, SWEEPS if known else SLOTS, span, lanes)
         last, first = call(
             later_edges if known else first_edges,
@@ -719,7 +718,7 @@
         if not known:
             inner_cut, b_ends, w_ends, shift, weight = made
         operands = (
-            place,
+            rot_offset,
             b_ends,
             w_ends,
             w_tile,
@@ -740,7 +739,7 @@
                 array(2, 2, 2, span, lanes),
             )
         pressure = call(
-            functools.partial(finish, known),
+            functools.partial(finish, step),
             outs,
             [smem] + [vmem] * (len(operands) - 1) + [hbm],
             hbm if known else [hbm] + [vmem] * 4,

time: 58.7 us -> 55.1 us (0.939); the launches traced: 58.1 us -> 55.6 us
  waiting for transfers between devices: 13.8 us -> 18.7 us
  Pallas kernels: 28.7 us -> 24.9 us
  starting transfers between devices: 14.6 us -> 11 us
    ppermute x2, starting transfers between devices: 5.65 us -> 1.75 us  [per_device(): left = lax.ppermute(last, 'az', ring(size, 1))]
    pallas_call x7, Pallas kernels: 28.7 us -> 24.9 us  [call(): pl.pallas_call(kernel, out_shape=out_shape, in_specs=in_specs, out_specs=...]
    ppermute x2, waiting for transfers between devices: 4.22 us -> 7.12 us  [branch(): return lambda e: lax.ppermute(e, ('az', 'rad'), facing_pairs(size, t))]
    ppermute x2, starting transfers between devices: 5.87 us -> 3.8 us  [branch(): return lambda e: lax.ppermute(e, ('az', 'rad'), facing_pairs(size, t))]
    ppermute x2, starting transfers between devices: 3.06 us -> 5 us  [per_device(): cut = lax.ppermute(cut, 'rad', [(0, 1), (1, 0)])]
    ppermute x2, waiting for transfers between devices: 6.54 us -> 7.84 us  [per_device(): left = lax.ppermute(last, 'az', ring(size, 1))]
    ppermute x2, waiting for transfers between devices: 3.01 us -> 3.72 us  [per_device(): right = lax.ppermute(first, 'az', ring(size, -1))]
  transfers between devices with their start and end apart: 8 -> 8, of which waited for: 5 -> 6; matrix products, arithmetic and copies ran while one was open for 0% -> 0% of each run, Pallas kernels for 27% -> 28%
where the time goes in v2:
time: 55.1 us; the launch traced here: 55.6 us
  Pallas kernels  24.9 us (45%)
  waiting for transfers between devices  18.7 us (34%)
  starting transfers between devices  11 us (20%)
  between operations  0.94 us (2%)
    pallas_call x7, Pallas kernels, call(): pl.pallas_call(kernel, out_shape=out_shape, in_specs=in_specs, out_specs=...  24.9 us
    ppermute x2, waiting for transfers between devices, per_device(): left = lax.ppermute(last, 'az', ring(size, 1))  7.84 us
    ppermute x2, waiting for transfers between devices, branch(): return lambda e: lax.ppermute(e, ('az', 'rad'), facing_pairs(size, t))  7.12 us
    ppermute x2, starting transfers between devices, per_device(): cut = lax.ppermute(cut, 'rad', [(0, 1), (1, 0)])  5 us
    ppermute x2, starting transfers between devices, branch(): return lambda e: lax.ppermute(e, ('az', 'rad'), facing_pairs(size, t))  3.8 us
    ppermute x2, waiting for transfers between devices, per_device(): right = lax.ppermute(first, 'az', ring(size, -1))  3.72 us
    ppermute x2, starting transfers between devices, per_device(): left = lax.ppermute(last, 'az', ring(size, 1))  1.75 us
  transfers between devices with their start and end apart: 8, of which 6 were waited for; matrix products, arithmetic and copies ran while one was open for 0% of the time, Pallas kernels for 28%

profile of v2, /device:TPU:1, one launch (start us, length us, event | category | flops | bytes accessed | tf_op | source)
XLA Modules:
  0.0 55.6 jit_solution(4937680776506051435)
XLA Ops:
  0.0 1.8 %pack.1 = (f32[3,2,16,4,128]{4,3,2,1,0:T(4,128)S(1)}, f32[16,128]{1,0:T(8,128)S(1)}, f32[2,2,4,96,128]{4,3,2,1,0:T(8,128)S(1)}, f32[2,2,3,96,128]{4,3,2,1,0:T(8,128)S(1)}, f32[2,2,3,96,128]{4,3,2,1,0:T(8,128)S(1)}) custom-call(f32[2,16,96,128]{3,2,1,0:T(8,128)} %p_ref.3, f32[2,16,96,128]{3,2,1,0:T(8,128)} %s_ref.3, f32[2,16,96,128]{3,2,1,0:T(8,128)} %d_ref.3), custom_call_target="tpu_custom_call" | custom-call | flops 319488 | bytes 212992 | tf_op jit(solution)/shard_map/pack/pallas_call | solution.py:643
  1.8 2.1 %collective-permute-start.32 = (f32[3,2,16,4,128]{4,3,2,1,0:T(4,128)S(1)}, f32[3,2,16,4,128]{4,3,2,1,0:T(4,128)S(1)}, u32[]{:S(2)}, u32[]{:S(2)}) collective-permute-start(f32[3,2,16,4,128]{4,3,2,1,0:T(4,128)S(1)} %get-tuple-element.98), channel_id=1, source_target_pairs={{0,1},{1,0},{2,3},{3,2},{4,5},{5,4},{6,7},{7,6},{8,9},{9,8},{10,11... | collective-permute-start | bytes 589832 | tf_op jit(solution)/shard_map/ppermute | solution.py:679
  4.7 5.1 %conditional.2 = (f32[16,128]{1,0:T(8,128)}) conditional(s32[]{:T(128)} %clamp.6, f32[16,128]{1,0:T(8,128)S(1)} %get-tuple-element.103, f32[16,128]{1,0:T(8,128)S(1)} %get-tuple-element.103, f32[16,128]{1,0:T(8,128)S(1)} %get-tuple-element.103, f32[16,128]{1,0:T(8,128)S(1)} %get-tuple-element.103, ...), branch_computations={%region_0.1_spmd, %region_1.2_spmd, %region_2.3_spmd, %region_3.4_... | conditional | bytes 32816 | solution.py:612
  4.7 3.1 %collective-permute-start.11 = (f32[16,128]{1,0:T(8,128)S(1)}, f32[16,128]{1,0:T(8,128)}, u32[]{:S(2)}, u32[]{:S(2)}) collective-permute-start(f32[16,128]{1,0:T(8,128)S(1)} %param.11), channel_id=1, source_target_pairs={{11,0},{22,1},{13,2},{24,3},{15,4},{26,5},{17,6},{28,7},{19,8},{30... | collective-permute-start | bytes 24584 | tf_op jit(solution)/shard_map/cond/branch_11_fun/ppermute | solution.py:608
  7.8 2.0 %collective-permute-done.11 = f32[16,128]{1,0:T(8,128)} collective-permute-done((f32[16,128]{1,0:T(8,128)S(1)}, f32[16,128]{1,0:T(8,128)}, u32[]{:S(2)}, u32[]{:S(2)}) %collective-permute-start.11) | collective-permute-done | bytes 8224 | tf_op jit(solution)/shard_map/cond/branch_11_fun/ppermute | solution.py:608
  9.8 0.0 collective-permute-done.32.cut_ref
  9.8 0.9 %edges.2 = (f32[2,6,104,128]{3,2,1,0:T(8,128)S(1)}, f32[2,6,104,128]{3,2,1,0:T(8,128)S(1)}) custom-call(f32[2,2,4,96,128]{4,3,2,1,0:T(8,128)S(1)} %get-tuple-element.105.p_ends, f32[2,2,3,96,128]{4,3,2,1,0:T(8,128)S(1)} %get-tuple-element.106.s_ends, f32[2,2,3,96,128]{4,3,2,1,0:T(8,128)S(1)} %get-tuple-element.107.d_ends, ...), custom_call_target="tpu_custom_call" | custom-call | flops 3833856 | bytes 2555904 | tf_op jit(solution)/shard_map/edges/pallas_call | solution.py:643
  10.7 1.5 %collective-permute-start.33 = (f32[2,6,104,128]{3,2,1,0:T(8,128)S(1)}, f32[2,6,104,128]{3,2,1,0:T(8,128)S(1)}, u32[]{:S(2)}, u32[]{:S(2)}) collective-permute-start(f32[2,6,104,128]{3,2,1,0:T(8,128)S(1)} %get-tuple-element.108), channel_id=1, source_target_pairs={{0,2},{2,4},{4,6},{6,8},{8,10},{10,12},{12,14},{14,16},{16,18},{18... | collective-permute-start | bytes 1916936 | tf_op jit(solution)/shard_map/ppermute | solution.py:694
  12.2 0.0 collective-permute-start.34
  12.2 8.0 %interior.2 = (f32[2,16,96,128]{3,2,1,0:T(8,128)}, f32[2,4,2,2,128,128]{5,4,3,2,1,0:T(8,128)S(1)}, f32[8,8,128]{2,1,0:T(8,128)S(1)}, f32[16,8,128]{2,1,0:T(8,128...) custom-call(f32[2,16,96,128]{3,2,1,0:T(8,128)} %p_ref.3, ...), custom_call_target="tpu_custom_call" | custom-call | flops 14057472 | bytes 9371648 | tf_op jit(solution)/shard_map/interior/pallas_call | solution.py:643
  20.2 6.2 %collective-permute-done.33.left_ref = f32[2,6,104,128]{3,2,1,0:T(8,128)S(1)} collective-permute-done((f32[2,6,104,128]{3,2,1,0:T(8,128)S(1)}, f32[2,6,104,128]{3,2,1,0:T(8,128)S(1)}, u32[]{:S(2)}, u32[]{:S(2)}) %collective-permute-start.33) | collective-permute-done | bytes 639008 | tf_op jit(solution)/shard_map/ppermute | solution.py:694
  26.4 2.5 %collective-permute-done.34.right_ref = f32[2,6,104,128]{3,2,1,0:T(8,128)S(1)} collective-permute-done((f32[2,6,104,128]{3,2,1,0:T(8,128)S(1)}, f32[2,6,104,128]{3,2,1,0:T(8,128)S(1)}, u32[]{:S(2)}, u32[]{:S(2)}) %collective-permute-start.34) | collective-permute-done | bytes 639008 | tf_op jit(solution)/shard_map/ppermute | solution.py:695
  28.9 3.0 %finish.2 = (f32[2,16,96,128]{3,2,1,0:T(8,128)}, f32[1,2,16,4,128]{4,3,2,1,0:T(4,128)S(1)}, f32[16,128]{1,0:T(8,128)S(1)}, f32[2,2,4,96,128]{4,3,2,1,0:T(8,128)S(1)}, f32[2,2,2,104,128]{4,3,2,1,0:T(8,128)S(1)}) custom-call(s32[1]{0:T(128)} %copy.41.turn_ref, f32[2,2,4,104,128]{4,3,2,1,0:T(8,128)S(1)} %get-tuple-element.99.b_ends, ...), custom_call_target="tpu_custom_call", output_to_operand_aliasing={{0}: (10, {})} | custom-call | flops 8306688 | bytes 5537792 | tf_op jit(solution)/shard_map/finish/pallas_call | solution.py:643
  31.9 2.9 %collective-permute-start.35 = (f32[1,2,16,4,128]{4,3,2,1,0:T(4,128)S(1)}, f32[1,2,16,4,128]{4,3,2,1,0:T(4,128)S(1)}, u32[]{:S(2)}, u32[]{:S(2)}) collective-permute-start(f32[1,2,16,4,128]{4,3,2,1,0:T(4,128)S(1)} %get-tuple-element.115), channel_id=1, source_target_pairs={{0,1},{1,0},{2,3},{3,2},{4,5},{5,4},{6,7},{7,6},{8,9},{9,8},{10,11... | collective-permute-start | bytes 196616 | tf_op jit(solution)/shard_map/ppermute | solution.py:679
  34.7 5.9 %conditional.3 = (f32[16,128]{1,0:T(8,128)}) conditional(s32[]{:T(128)} %clamp.7, f32[16,128]{1,0:T(8,128)S(1)} %get-tuple-element.118, f32[16,128]{1,0:T(8,128)S(1)} %get-tuple-element.118, f32[16,128]{1,0:T(8,128)S(1)} %get-tuple-element.118, f32[16,128]{1,0:T(8,128)S(1)} %get-tuple-element.118, ...), branch_computations={%region_16.17_spmd, %region_17.18_spmd, %region_18.19_spmd, %regio... | conditional | bytes 32816 | solution.py:612
  34.7 0.7 %collective-permute-start.23 = (f32[16,128]{1,0:T(8,128)S(1)}, f32[16,128]{1,0:T(8,128)}, u32[]{:S(2)}, u32[]{:S(2)}) collective-permute-start(f32[16,128]{1,0:T(8,128)S(1)} %param.23), channel_id=1, source_target_pairs={{19,0},{14,1},{21,2},{16,3},{23,4},{18,5},{25,6},{20,7},{27,8},{22... | collective-permute-start | bytes 24584 | tf_op jit(solution)/shard_map/cond/branch_7_fun/ppermute | solution.py:608
  35.5 5.2 %collective-permute-done.23 = f32[16,128]{1,0:T(8,128)} collective-permute-done((f32[16,128]{1,0:T(8,128)S(1)}, f32[16,128]{1,0:T(8,128)}, u32[]{:S(2)}, u32[]{:S(2)}) %collective-permute-start.23) | collective-permute-done | bytes 8224 | tf_op jit(solution)/shard_map/cond/branch_7_fun/ppermute | solution.py:608
  40.6 0.8 %edges.3 = (f32[2,4,104,128]{3,2,1,0:T(8,128)S(1)}, f32[2,4,104,128]{3,2,1,0:T(8,128)S(1)}) custom-call(f32[2,2,4,96,128]{4,3,2,1,0:T(8,128)S(1)} %get-tuple-element.120.p_ends, f32[2,2,4,104,128]{4,3,2,1,0:T(8,128)S(1)} %get-tuple-element.99.b_ends, f32[2,2,4,104,128]{4,3,2,1,0:T(8,128)S(1)} %get-tuple-element.100.w_ends, ...), custom_call_target="tpu_custom_call" | custom-call | flops 3833856 | bytes 2555904 | tf_op jit(solution)/shard_map/edges/pallas_call | solution.py:643
  41.5 0.2 collective-permute-start.36
  41.7 0.5 collective-permute-start.37
  42.2 7.5 %interior.3 = (f32[2,16,96,128]{3,2,1,0:T(8,128)}, f32[2,4,2,2,128,128]{5,4,3,2,1,0:T(8,128)S(1)}, f32[8,8,128]{2,1,0:T(8,128)S(1)}, f32[16,8,128]{2,1,0:T(8,128)S(1)}) custom-call(f32[2,16,96,128]{3,2,1,0:T(8,128)} %get-tuple-element.112.p_ref, f32[2,16,104,128]{3,2,1,0:T(8,128)} %get-tuple-element.113.b_ref, f32[2,16,104,128]{3,2,1,0:T(8,128)} %get-tuple-element.114.w_ref, ...), custom_call_target="tpu_custom_call" | custom-call | flops 14057472 | bytes 9371648 | tf_op jit(solution)/shard_map/interior/pallas_call | solution.py:643
  49.7 1.6 %collective-permute-done.36.left_ref = f32[2,4,104,128]{3,2,1,0:T(8,128)S(1)} collective-permute-done((f32[2,4,104,128]{3,2,1,0:T(8,128)S(1)}, f32[2,4,104,128]{3,2,1,0:T(8,128)S(1)}, u32[]{:S(2)}, u32[]{:S(2)}) %collective-permute-start.36) | collective-permute-done | bytes 426016 | tf_op jit(solution)/shard_map/ppermute | solution.py:694
  51.3 1.2 %collective-permute-done.37.right_ref = f32[2,4,104,128]{3,2,1,0:T(8,128)S(1)} collective-permute-done((f32[2,4,104,128]{3,2,1,0:T(8,128)S(1)}, f32[2,4,104,128]{3,2,1,0:T(8,128)S(1)}, u32[]{:S(2)}, u32[]{:S(2)}) %collective-permute-start.37) | collective-permute-done | bytes 426016 | tf_op jit(solution)/shard_map/ppermute | solution.py:695
  52.6 2.9 %finish.3 = f32[2,16,96,128]{3,2,1,0:T(8,128)} custom-call(s32[1]{0:T(128)} %copy.41.turn_ref, f32[2,2,4,104,128]{4,3,2,1,0:T(8,128)S(1)} %get-tuple-element.99.b_ends, f32[2,2,4,104,128]{4,3,2,1,0:T(8,128)S(1)} %get-tuple-element.100.w_ends, f32[16,8,128]{2,1,0:T(8,128)S(1)} %get-tuple-element.116.w_tile, ...), custom_call_target="tpu_custom_call", output_to_operand_aliasing={{}: (10, {})} | custom-call | flops 8306688 | bytes 5537792 | tf_op jit(solution)/shard_map/finish/pallas_call | solution.py:643
  (1 shorter events, 0.0 us)
Async XLA Ops:
  1.8 7.9 %collective-permute-start.32 = (f32[3,2,16,4,128]{4,3,2,1,0:T(4,128)S(1)}, f32[3,2,16,4,128]{4,3,2,1,0:T(4,128)S(1)}, u32[]{:S(2)}, u32[]{:S(2)}) collective-permute-start(f32[3,2,16,4,128]{4,3,2,1,0:T(4,128)S(1)} %get-tuple-element.98), channel_id=1, source_target_pairs={{0,1},{1,0},{2,3},{3,2},{4,5},{5,4},{6,7},{7,6},{8,9},{9,8},{10,11... | collective-permute-start | bytes 589832 | tf_op jit(solution)/shard_map/ppermute | solution.py:679
  4.7 5.0 %collective-permute-start.11 = (f32[16,128]{1,0:T(8,128)S(1)}, f32[16,128]{1,0:T(8,128)}, u32[]{:S(2)}, u32[]{:S(2)}) collective-permute-start(f32[16,128]{1,0:T(8,128)S(1)} %param.11), channel_id=1, source_target_pairs={{11,0},{22,1},{13,2},{24,3},{15,4},{26,5},{17,6},{28,7},{19,8},{30... | collective-permute-start | bytes 24584 | tf_op jit(solution)/shard_map/cond/branch_11_fun/ppermute | solution.py:608
  10.7 15.7 %collective-permute-start.33 = (f32[2,6,104,128]{3,2,1,0:T(8,128)S(1)}, f32[2,6,104,128]{3,2,1,0:T(8,128)S(1)}, u32[]{:S(2)}, u32[]{:S(2)}) collective-permute-start(f32[2,6,104,128]{3,2,1,0:T(8,128)S(1)} %get-tuple-element.108), channel_id=1, source_target_pairs={{0,2},{2,4},{4,6},{6,8},{8,10},{10,12},{12,14},{14,16},{16,18},{18... | collective-permute-start | bytes 1916936 | tf_op jit(solution)/shard_map/ppermute | solution.py:694
  12.2 16.7 %collective-permute-start.34 = (f32[2,6,104,128]{3,2,1,0:T(8,128)S(1)}, f32[2,6,104,128]{3,2,1,0:T(8,128)S(1)}, u32[]{:S(2)}, u32[]{:S(2)}) collective-permute-start(f32[2,6,104,128]{3,2,1,0:T(8,128)S(1)} %get-tuple-element.109), channel_id=1, source_target_pairs={{0,30},{2,0},{4,2},{6,4},{8,6},{10,8},{12,10},{14,12},{16,14},{18,... | collective-permute-start | bytes 1916936 | tf_op jit(solution)/shard_map/ppermute | solution.py:695
  31.9 8.8 %collective-permute-start.35 = (f32[1,2,16,4,128]{4,3,2,1,0:T(4,128)S(1)}, f32[1,2,16,4,128]{4,3,2,1,0:T(4,128)S(1)}, u32[]{:S(2)}, u32[]{:S(2)}) collective-permute-start(f32[1,2,16,4,128]{4,3,2,1,0:T(4,128)S(1)} %get-tuple-element.115), channel_id=1, source_target_pairs={{0,1},{1,0},{2,3},{3,2},{4,5},{5,4},{6,7},{7,6},{8,9},{9,8},{10,11... | collective-permute-start | bytes 196616 | tf_op jit(solution)/shard_map/ppermute | solution.py:679
  34.7 5.9 %collective-permute-start.23 = (f32[16,128]{1,0:T(8,128)S(1)}, f32[16,128]{1,0:T(8,128)}, u32[]{:S(2)}, u32[]{:S(2)}) collective-permute-start(f32[16,128]{1,0:T(8,128)S(1)} %param.23), channel_id=1, source_target_pairs={{19,0},{14,1},{21,2},{16,3},{23,4},{18,5},{25,6},{20,7},{27,8},{22... | collective-permute-start | bytes 24584 | tf_op jit(solution)/shard_map/cond/branch_7_fun/ppermute | solution.py:608
  41.5 9.9 %collective-permute-start.36 = (f32[2,4,104,128]{3,2,1,0:T(8,128)S(1)}, f32[2,4,104,128]{3,2,1,0:T(8,128)S(1)}, u32[]{:S(2)}, u32[]{:S(2)}) collective-permute-start(f32[2,4,104,128]{3,2,1,0:T(8,128)S(1)} %get-tuple-element.121), channel_id=1, source_target_pairs={{0,2},{2,4},{4,6},{6,8},{8,10},{10,12},{12,14},{14,16},{16,18},{18... | collective-permute-start | bytes 1277960 | tf_op jit(solution)/shard_map/ppermute | solution.py:694
  41.7 10.9 %collective-permute-start.37 = (f32[2,4,104,128]{3,2,1,0:T(8,128)S(1)}, f32[2,4,104,128]{3,2,1,0:T(8,128)S(1)}, u32[]{:S(2)}, u32[]{:S(2)}) collective-permute-start(f32[2,4,104,128]{3,2,1,0:T(8,128)S(1)} %get-tuple-element.122), channel_id=1, source_target_pairs={{0,30},{2,0},{4,2},{6,4},{8,6},{10,8},{12,10},{14,12},{16,14},{18,... | collective-permute-start | bytes 1277960 | tf_op jit(solution)/shard_map/ppermute | solution.py:695

commit v3 on v2

--- a/solution.py
+++ b/solution.py
@@ -12,7 +12,11 @@
 OMEGA = 0.8
 TILE = 8
 OWN = 2 * TILE
-SLOTS = SWEEPS + 2
+EARLY = False
+LEVELS = tuple(range(SWEEPS))
+WEIGHTS = (SWEEPS, SWEEPS + 1)
+FIRST_EARLY = (0, *WEIGHTS) if EARLY else ()
+FIRST_LATE = LEVELS[1:] if EARLY else LEVELS + WEIGHTS
 
 
 class Side:
@@ -27,11 +31,15 @@
         self.tile = slice(end, end + TILE) if low else slice(TILE, OWN)
         self.ghost = OWN - 1 if low else end
         self.edge = OWN if low else end - 1
-        self.spare = self.count - TILE + SWEEPS if low else 0
+        self.spare = self.count - 1 if low else 0
+        self.inside = shifted(self.own, -self.first)
         self.facing = 1 if low else 0
         self.sent = slice(radial_cells - SWEEPS, radial_cells) if low else slice(0, SWEEPS)
         self.sent_tile = radial_cells - TILE if low else 0
         self.edge_tile = 0 if low else radial_cells - TILE
+
+    def beyond(self, distance):
+        return self.inside.stop - 1 + distance if self.low else self.inside.start - distance
 
 
 def shifted(s, by):
@@ -101,8 +109,49 @@
     return slice(0, count) if edge == 0 else slice(cells - count, cells)
 
 
-def spare_rows(side):
-    return [(slot, side.spare + i) for slot in range(SWEEPS) for i in range(TILE - SWEEPS)]
+def block_rows(cells):
+    return cells // 2 + SWEEPS - 1
+
+
+class Message:
+    def __init__(self, slots, radial_cells, cells, weights):
+        self.slots = slots
+        self.radial_cells = radial_cells
+        tail = []
+        if 1 in slots:
+            needed = [(n, SWEEPS - 1 - n) for n in LEVELS] + [(SWEEPS, 2)] * weights
+            tail += [(slot, k, h) for slot, n in needed for k in range(2) for h in range(1, n + 1)]
+            tail += [("block", i) for i in range(block_rows(cells))]
+            tail += ["third"] * weights
+        start = 2 * len(slots) * radial_cells
+        self.tail = {what: start + i for i, what in enumerate(tail)}
+        self.rows = start + -(-len(tail) // TILE) * TILE
+
+    def block(self, slot, k):
+        start = (2 * self.slots.index(slot) + k) * self.radial_cells
+        return slice(start, start + self.radial_cells)
+
+    def row(self, *what):
+        at = self.tail[what if len(what) > 1 else what[0]]
+        return slice(at, at + 1)
+
+    def beyond(self, slot, k):
+        return [w[2] for w in self.tail if w != "third" and w[:2] == (slot, k) and len(w) == 3]
+
+    def put(self, ref, side, slot, k, value):
+        if slot in self.slots:
+            ref[self.block(slot, k)] = value[side.inside]
+        for h in self.beyond(slot, k):
+            at = side.beyond(h)
+            ref[self.row(slot, k, h)] = value[at : at + 1]
+
+
+def messages_of(step, radial_cells, cells):
+    late = FIRST_LATE if step == 1 else LEVELS
+    return (
+        Message(FIRST_EARLY if step == 1 else (), radial_cells, cells, False),
+        Message(late, radial_cells, cells, step == 1),
+    )
 
 
 def close(column, side, facing):
@@ -113,7 +162,7 @@
         column[row] = column[side.edge : side.edge + 1]
 
 
-def trajectories(side, field, other, weight, shift, messages):
+def trajectories(side, field, other, weight, shift, layout, messages, weights):
     bufs = (field, other)
     matrix = neighbour_matrix(field.shape[-1])
 
@@ -129,7 +178,9 @@
         items = []
         for edge, message in enumerate(messages):
             for k in range(2):
-                message[k, sweep] = src[edge, k, at(edge, 1, SWEEPS), side.rows]
+                layout.put(
+                    message, side, sweep, k, src[edge, k, at(edge, 1, SWEEPS), side.rows]
+                )
                 for j in range(1, SWEEPS - sweep):
                     i = at(edge, j, SWEEPS - 1)
 
@@ -154,21 +205,24 @@
                         )
                     )
         relax_all(side, matrix, items)
+    if not weights:
+        return
     for edge, message in enumerate(messages):
-        if message.shape[1] == SWEEPS:
-            continue
         for k in range(2):
             for i in range(2):
-                message[k, SWEEPS + i] = weight(edge, k, at(edge, 1 + i, SWEEPS - 1))
-            if k == side.facing:
-                row = side.edge - side.first
-                message[k, SWEEPS + 1, side.spare : side.spare + 1] = weight(
-                    edge, k, at(edge, 3, SWEEPS - 1)
-                )[row : row + 1]
-
-
-def pack(p_ref, s_ref, d_ref, cut_ref, edge_ref, p_ends, s_ends, d_ends, tiles, edge_tiles, sems):
+                layout.put(
+                    message, side, SWEEPS + i, k, weight(edge, k, at(edge, 1 + i, SWEEPS - 1))
+                )
+        row = side.edge - side.first
+        message[layout.row("third")] = weight(edge, side.facing, at(edge, 3, SWEEPS - 1))[
+            row : row + 1
+        ]
+
+
+def pack(p_ref, s_ref, d_ref, cut_ref, edge_ref, p_ends, s_ends, d_ends, *rest):
+    *early, tiles, edge_tiles, sems = rest
     cells, radial_cells = p_ref.shape[1:3]
+    layout, _ = messages_of(1, radial_cells, cells)
 
     def body(side):
         copies = []
@@ -186,6 +240,13 @@
                 span = pl.ds(end_columns(edge, cells, count).start, count)
                 fetch(source.at[:, span], target.at[edge])
         copy_all(copies)
+        for edge, message in enumerate(early[::-1]):
+            for k in range(2):
+                i = 0 if edge == 0 else SWEEPS - 1
+                message[layout.block(0, k)] = p_ends[edge, k, i]
+                for j in range(2):
+                    i = j if edge == 0 else SWEEPS - 2 - j
+                    message[layout.block(SWEEPS + j, k)] = OMEGA / (6.0 + d_ends[edge, k, i])
         cut_ref[...] = tiles[:, :, :, shifted(side.sent, -side.sent_tile), :]
         at = side.edge - OWN - side.edge_tile
         for j in range(cells):
@@ -203,11 +264,14 @@
                 field[edge, k, i, side.cut] = cut_ref[0, k, columns.start + i]
 
 
-def send_block(side, arriving, block_ref, messages):
+def send_block(layout, arriving, block, messages):
     arriving.wait()
-    for message in messages:
-        for i, (slot, row) in enumerate(spare_rows(side)):
-            message[side.facing, slot, row : row + 1] = block_ref[i : i + 1]
+    cells = block.shape[0]
+    count = block_rows(cells)
+    for edge, message in enumerate(messages):
+        for i in range(count):
+            at = i if edge == 0 else cells - count + i
+            message[layout.row("block", i)] = block[at : at + 1]
 
 
 def first_edges(
@@ -216,6 +280,7 @@
     radial_cells = p_ends.shape[3]
     cells = cut_ref.shape[2]
     n = SWEEPS - 1
+    _, layout = messages_of(1, radial_cells, cells)
 
     def body(side):
         arriving = pltpu.make_async_copy(block_ref, block, sem)
@@ -240,15 +305,18 @@
             other,
             lambda e, k, i: weight[e, k, i],
             lambda e, k, i: shift[e, k, i],
+            layout,
             (first, last),
+            True,
         )
-        send_block(side, arriving, block, (first, last))
+        send_block(layout, arriving, block, (first, last))
 
     on_each_side(radial_cells, body)
 
 
 def later_edges(p_ends, b_ends, w_ends, cut_ref, block_ref, last, first, block, sem, field, other):
     cells, radial_cells = cut_ref.shape[2], p_ends.shape[3]
+    _, layout = messages_of(2, radial_cells, cells)
 
     def body(side):
         arriving = pltpu.make_async_copy(block_ref, block, sem)
@@ -260,9 +328,11 @@
             other,
             lambda e, k, i: w_ends[e, k, i + e],
             lambda e, k, i: b_ends[e, k, i + e],
+            layout,
             (first, last),
+            False,
         )
-        send_block(side, arriving, block, (first, last))
+        send_block(layout, arriving, block, (first, last))
 
     on_each_side(radial_cells, body)
 
@@ -404,16 +474,16 @@
     on_each_side(radial_cells, body)
 
 
-def ghost_response(side, step, turn_ref, w_tile, block_ref, messages, weights, wide, source):
+def ghost_response(side, step, turn_ref, w_tile, block_ref, layout, messages, weights, wide, source):
     facing = side.facing
     cells = w_tile.shape[0]
     reach = SWEEPS - 1
     tile = slice(side.edge_tile + OWN - side.first, side.edge_tile + OWN - side.first + TILE)
     at = side.edge - OWN - side.edge_tile
-    rows = spare_rows(side)
-    for i, (slot, row) in enumerate(rows):
-        wide[i : i + 1] = messages[0][facing, slot, row : row + 1]
-        wide[2 * cells + i : 2 * cells + i + 1] = messages[1][facing, slot, row : row + 1]
+    count = block_rows(cells)
+    for i in range(count):
+        for message, to in zip(messages, (cells - count + i, 2 * cells + i)):
+            wide[to : to + 1] = message[layout.row("block", i)]
     wide[cells : 2 * cells] = block_ref[...]
     source[...] = jnp.zeros(source.shape, jnp.float32)
     offset = lax.rem(turn_ref[0] * step, cells * lax.axis_size("az"))
@@ -450,13 +520,21 @@
     known = step > 1
     if known:
         beyond, _, out_ref, *rest = rest
-        weights = (beyond.at[0], beyond.at[1])
+        early = ()
     else:
-        cut_in, _, out_ref, cut_out, edge_out, ends_out, beyond_out, *rest = rest
-        weights = tuple(x.at[:, pl.ds(SWEEPS, 2)] for x in (left_ref, right_ref))
+        early = rest[1:3] if EARLY else ()
+        cut_in, rest = rest[0], rest[1 + len(early) :]
+        _, out_ref, cut_out, edge_out, ends_out, beyond, *rest = rest
+    weights = (beyond.at[0], beyond.at[1])
     levels, last, inner_tiles, near, near2, wide, source, sems = rest
     messages = (left_ref, right_ref)
     cells, radial_cells = out_ref.shape[1:3]
+    early_layout, layout = messages_of(step, radial_cells, cells)
+
+    def given(e, k, slot):
+        if slot in layout.slots:
+            return messages[e][layout.block(slot, k)]
+        return early[e][early_layout.block(slot, k)]
 
     def column(e, d):
         return d - 1 if e == 0 else cells - d
@@ -469,9 +547,31 @@
                 return levels.at[n, e, k, d]
             return stash.at[e, n, k, d - n - 1 if e == 0 else n + 2 - d]
 
+        def meet(e, k, n, response):
+            target = levels.at[n, e, k, 0]
+            value = given(e, k, n)
+            target[side.own] = value if response is None else value + response[side.inside]
+            for h in layout.beyond(n, k):
+                at = side.beyond(h)
+                value = messages[e][layout.row(n, k, h)]
+                if response is not None:
+                    value = value + response[at : at + 1]
+                target[side.first + at : side.first + at + 1] = value
+
         for e in range(2):
+            if not known:
+                for k in range(2):
+                    for i in range(2):
+                        target = beyond.at[e, k, i]
+                        target[side.inside] = given(e, k, SWEEPS + i)
+                        for h in layout.beyond(SWEEPS + i, k):
+                            row = side.beyond(h)
+                            target[row : row + 1] = messages[e][layout.row(SWEEPS + i, k, h)]
+                beyond[e, facing, 1, side.spare : side.spare + 1] = messages[e][
+                    layout.row("third")
+                ]
             for k in range(2):
-                levels[0, e, k, 0, side.rows] = messages[e][k, 0]
+                meet(e, k, 0, None)
                 for buf in (near, near2):
                     buf[e, k] = jnp.zeros(buf.shape[2:], jnp.float32)
         nears = (near, near2)
@@ -503,7 +603,7 @@
 
                     def take(new, e=e, k=k):
                         dst[e, k, 0, side.rows] = new
-                        levels[n + 1, e, k, 0, side.rows] = messages[e][k, n + 1] + new
+                        meet(e, k, n + 1, new)
                         close(dst.at[e, k, 0], side, k == facing)
 
                     if n == 0:
@@ -532,7 +632,7 @@
         for k in (1 - facing, facing):
             if k == facing:
                 response = ghost_response(
-                    side, step, turn_ref, w_tile, block_ref, messages, weights, wide, source
+                    side, step, turn_ref, w_tile, block_ref, layout, messages, weights, wide, source
                 )
                 for i in range(cells - 2 * SWEEPS):
                     inner_tiles[i] = tile_in[i] + response[SWEEPS + i]
@@ -571,8 +671,6 @@
                 for i in range(SWEEPS):
                     edge_out[first + i : first + i + 1] = last[e, facing, i, row : row + 1]
             ends_out[...] = last[...]
-            for e in range(2):
-                beyond_out[e] = weights[e][...]
         for c in copies:
             c.wait()
 
@@ -654,6 +752,8 @@
         )(*operands)
 
     fields = tuple(pinned(x) for x in (pressure, source, diagonal))
+    layout, _ = messages_of(1, radial_cells, cells)
+    early_message = array(layout.rows, lanes)
     cut, edge, *ends = call(
         pack,
         (
@@ -662,9 +762,10 @@
             array(2, 2, SWEEPS, radial_cells, lanes),
             array(2, 2, SWEEPS - 1, radial_cells, lanes),
             array(2, 2, SWEEPS - 1, radial_cells, lanes),
+            *([early_message] * 2 if EARLY else []),
         ),
         [hbm] * 3,
-        [vmem] * 2 + [anywhere] * 3,
+        [vmem] * (7 if EARLY else 5),
         [
             scratch(3, 2, cells, TILE, lanes),
             scratch(cells, TILE, lanes),
@@ -674,12 +775,20 @@
         1,
         name="pack",
     )
+    early = []
+    if EARLY:
+        *ends, last, first = ends
+        early = [
+            lax.ppermute(last, "az", ring(size, 1)),
+            lax.ppermute(first, "az", ring(size, -1)),
+        ]
     for step in range(1, STEPS + 1):
         known = step > 1
         cut = lax.ppermute(cut, "rad", [(0, 1), (1, 0)])
         offset = rot_offset[0] * step % (cells * size)
         block = facing_block(edge, offset)
-        message = array(2, SWEEPS if known else SLOTS, span, lanes)
+        _, layout = messages_of(step, radial_cells, cells)
+        message = array(layout.rows, lanes)
         last, first = call(
             later_edges if known else first_edges,
             (message, message),
@@ -728,7 +837,7 @@
             left,
             right,
         )
-        operands += (beyond,) if known else (inner_cut,)
+        operands += (beyond,) if known else (inner_cut, *early)
         outs = result
         if not known:
             outs = (

time: 55.1 us -> 55.6 us (level); the launches traced: 55.6 us -> 55.2 us
  starting transfers between devices: 11 us -> 9.58 us
  Pallas kernels: 24.9 us -> 25.5 us
    ppermute x2, waiting for transfers between devices: 7.84 us -> 5.28 us  [per_device(): left = lax.ppermute(last, 'az', ring(size, 1))]
    ppermute x2, waiting for transfers between devices: 7.12 us -> 8.77 us  [branch(): return lambda e: lax.ppermute(e, ('az', 'rad'), facing_pairs(size, t))]
    ppermute x2, starting transfers between devices: 3.8 us -> 2.15 us  [branch(): return lambda e: lax.ppermute(e, ('az', 'rad'), facing_pairs(size, t))]
    ppermute x2, starting transfers between devices: 5 us -> 3.5 us  [per_device(): cut = lax.ppermute(cut, 'rad', [(0, 1), (1, 0)])]
    ppermute x2, waiting for transfers between devices: 3.72 us -> 5.11 us  [per_device(): right = lax.ppermute(first, 'az', ring(size, -1))]
    ppermute x2, starting transfers between devices: 0.5 us -> 1.84 us  [per_device(): right = lax.ppermute(first, 'az', ring(size, -1))]
    pallas_call x7, Pallas kernels: 24.9 us -> 25.5 us  [call(): pl.pallas_call(kernel, out_shape=out_shape, in_specs=in_specs, out_specs=...]
where the time goes in v3:
time: 55.6 us; the launch traced here: 55.2 us
  Pallas kernels  25.5 us (46%)
  waiting for transfers between devices  19.2 us (35%)
  starting transfers between devices  9.58 us (17%)
  between operations  0.94 us (2%)
    pallas_call x7, Pallas kernels, call(): pl.pallas_call(kernel, out_shape=out_shape, in_specs=in_specs, out_specs=...  25.5 us
    ppermute x2, waiting for transfers between devices, branch(): return lambda e: lax.ppermute(e, ('az', 'rad'), facing_pairs(size, t))  8.77 us
    ppermute x2, waiting for transfers between devices, per_device(): left = lax.ppermute(last, 'az', ring(size, 1))  5.28 us
    ppermute x2, waiting for transfers between devices, per_device(): right = lax.ppermute(first, 'az', ring(size, -1))  5.11 us
    ppermute x2, starting transfers between devices, per_device(): cut = lax.ppermute(cut, 'rad', [(0, 1), (1, 0)])  3.5 us
    ppermute x2, starting transfers between devices, branch(): return lambda e: lax.ppermute(e, ('az', 'rad'), facing_pairs(size, t))  2.15 us
    ppermute x2, starting transfers between devices, per_device(): left = lax.ppermute(last, 'az', ring(size, 1))  2.09 us
    ppermute x2, starting transfers between devices, per_device(): right = lax.ppermute(first, 'az', ring(size, -1))  1.84 us
  transfers between devices with their start and end apart: 8, of which 6 were waited for; matrix products, arithmetic and copies ran while one was open for 0% of the time, Pallas kernels for 28%

profile of v3, /device:TPU:1, one launch (start us, length us, event | category | flops | bytes accessed | tf_op | source)
XLA Modules:
  0.0 55.2 jit_solution(9748074107060841306)
XLA Ops:
  0.0 1.8 %pack.1 = (f32[3,2,16,4,128]{4,3,2,1,0:T(4,128)S(1)}, f32[16,128]{1,0:T(8,128)S(1)}, f32[2,2,4,96,128]{4,3,2,1,0:T(8,128)S(1)}, f32[2,2,3,96,128]{4,3,2,1,0:T(8,128)S(1)}, f32[2,2,3,96,128]{4,3,2,1,0:T(8,128)S(1)}) custom-call(f32[2,16,96,128]{3,2,1,0:T(8,128)} %p_ref.3, f32[2,16,96,128]{3,2,1,0:T(8,128)} %s_ref.3, f32[2,16,96,128]{3,2,1,0:T(8,128)} %d_ref.3), custom_call_target="tpu_custom_call" | custom-call | flops 319488 | bytes 212992 | tf_op jit(solution)/shard_map/pack/pallas_call | solution.py:741
  1.8 2.1 %collective-permute-start.32 = (f32[3,2,16,4,128]{4,3,2,1,0:T(4,128)S(1)}, f32[3,2,16,4,128]{4,3,2,1,0:T(4,128)S(1)}, u32[]{:S(2)}, u32[]{:S(2)}) collective-permute-start(f32[3,2,16,4,128]{4,3,2,1,0:T(4,128)S(1)} %get-tuple-element.98), channel_id=1, source_target_pairs={{0,1},{1,0},{2,3},{3,2},{4,5},{5,4},{6,7},{7,6},{8,9},{9,8},{10,11... | collective-permute-start | bytes 589832 | tf_op jit(solution)/shard_map/ppermute | solution.py:787
  4.7 4.7 %conditional.2 = (f32[16,128]{1,0:T(8,128)}) conditional(s32[]{:T(128)} %clamp.6, f32[16,128]{1,0:T(8,128)S(1)} %get-tuple-element.103, f32[16,128]{1,0:T(8,128)S(1)} %get-tuple-element.103, f32[16,128]{1,0:T(8,128)S(1)} %get-tuple-element.103, f32[16,128]{1,0:T(8,128)S(1)} %get-tuple-element.103, ...), branch_computations={%region_0.1_spmd, %region_1.2_spmd, %region_2.3_spmd, %region_3.4_... | conditional | bytes 32816 | solution.py:710
  4.7 0.6 %collective-permute-start.1 = (f32[16,128]{1,0:T(8,128)S(1)}, f32[16,128]{1,0:T(8,128)}, u32[]{:S(2)}, u32[]{:S(2)}) collective-permute-start(f32[16,128]{1,0:T(8,128)S(1)} %param.1), channel_id=1, source_target_pairs={{31,0},{2,1},{1,2},{4,3},{3,4},{6,5},{5,6},{8,7},{7,8},{10,9},{9,1... | collective-permute-start | bytes 24584 | tf_op jit(solution)/shard_map/cond/branch_1_fun/ppermute | solution.py:706
  5.3 4.1 %collective-permute-done.1 = f32[16,128]{1,0:T(8,128)} collective-permute-done((f32[16,128]{1,0:T(8,128)S(1)}, f32[16,128]{1,0:T(8,128)}, u32[]{:S(2)}, u32[]{:S(2)}) %collective-permute-start.1) | collective-permute-done | bytes 8224 | tf_op jit(solution)/shard_map/cond/branch_1_fun/ppermute | solution.py:706
  9.4 1.3 %edges.2 = (f32[1184,128]{1,0:T(8,128)S(1)}, f32[1184,128]{1,0:T(8,128)S(1)}) custom-call(f32[2,2,4,96,128]{4,3,2,1,0:T(8,128)S(1)} %get-tuple-element.105.p_ends, f32[2,2,3,96,128]{4,3,2,1,0:T(8,128)S(1)} %get-tuple-element.106.s_ends, f32[2,2,3,96,128]{4,3,2,1,0:T(8,128)S(1)} %get-tuple-element.107.d_ends, ...), custom_call_target="tpu_custom_call" | custom-call | flops 3833856 | bytes 2555904 | tf_op jit(solution)/shard_map/edges/pallas_call | solution.py:741
  10.7 1.8 %collective-permute-start.33 = (f32[1184,128]{1,0:T(8,128)S(1)}, f32[1184,128]{1,0:T(8,128)S(1)}, u32[]{:S(2)}, u32[]{:S(2)}) collective-permute-start(f32[1184,128]{1,0:T(8,128)S(1)} %get-tuple-element.108), channel_id=1, source_target_pairs={{0,2},{2,4},{4,6},{6,8},{8,10},{10,12},{12,14},{14,16},{16,18},{18... | collective-permute-start | bytes 1818632 | tf_op jit(solution)/shard_map/ppermute | solution.py:803
  12.6 1.3 %collective-permute-start.34 = (f32[1184,128]{1,0:T(8,128)S(1)}, f32[1184,128]{1,0:T(8,128)S(1)}, u32[]{:S(2)}, u32[]{:S(2)}) collective-permute-start(f32[1184,128]{1,0:T(8,128)S(1)} %get-tuple-element.109), channel_id=1, source_target_pairs={{0,30},{2,0},{4,2},{6,4},{8,6},{10,8},{12,10},{14,12},{16,14},{18,... | collective-permute-start | bytes 1818632 | tf_op jit(solution)/shard_map/ppermute | solution.py:804
  13.9 8.0 %interior.2 = (f32[2,16,96,128]{3,2,1,0:T(8,128)}, f32[2,4,2,2,128,128]{5,4,3,2,1,0:T(8,128)S(1)}, f32[8,8,128]{2,1,0:T(8,128)S(1)}, f32[16,8,128]{2,1,0:T(8,128...) custom-call(f32[2,16,96,128]{3,2,1,0:T(8,128)} %p_ref.3, ...), custom_call_target="tpu_custom_call" | custom-call | flops 14057472 | bytes 9371648 | tf_op jit(solution)/shard_map/interior/pallas_call | solution.py:741
  21.9 4.2 %collective-permute-done.33.left_ref = f32[1184,128]{1,0:T(8,128)S(1)} collective-permute-done((f32[1184,128]{1,0:T(8,128)S(1)}, f32[1184,128]{1,0:T(8,128)S(1)}, u32[]{:S(2)}, u32[]{:S(2)}) %collective-permute-start.33) | collective-permute-done | bytes 606240 | tf_op jit(solution)/shard_map/ppermute | solution.py:803
  26.1 2.5 %collective-permute-done.34.right_ref = f32[1184,128]{1,0:T(8,128)S(1)} collective-permute-done((f32[1184,128]{1,0:T(8,128)S(1)}, f32[1184,128]{1,0:T(8,128)S(1)}, u32[]{:S(2)}, u32[]{:S(2)}) %collective-permute-start.34) | collective-permute-done | bytes 606240 | tf_op jit(solution)/shard_map/ppermute | solution.py:804
  28.6 3.0 %finish.2 = (f32[2,16,96,128]{3,2,1,0:T(8,128)}, f32[1,2,16,4,128]{4,3,2,1,0:T(4,128)S(1)}, f32[16,128]{1,0:T(8,128)S(1)}, f32[2,2,4,96,128]{4,3,2,1,0:T(8,128)S(1)}, f32[2,2,2,104,128]{4,3,2,1,0:T(8,128)S(1)}) custom-call(s32[1]{0:T(128)} %copy.41.turn_ref, f32[2,2,4,104,128]{4,3,2,1,0:T(8,128)S(1)} %get-tuple-element.99.b_ends, ...), custom_call_target="tpu_custom_call", output_to_operand_aliasing={{0}: (10, {})} | custom-call | flops 8306688 | bytes 5537792 | tf_op jit(solution)/shard_map/finish/pallas_call | solution.py:741
  31.6 1.4 %collective-permute-start.35 = (f32[1,2,16,4,128]{4,3,2,1,0:T(4,128)S(1)}, f32[1,2,16,4,128]{4,3,2,1,0:T(4,128)S(1)}, u32[]{:S(2)}, u32[]{:S(2)}) collective-permute-start(f32[1,2,16,4,128]{4,3,2,1,0:T(4,128)S(1)} %get-tuple-element.115), channel_id=1, source_target_pairs={{0,1},{1,0},{2,3},{3,2},{4,5},{5,4},{6,7},{7,6},{8,9},{9,8},{10,11... | collective-permute-start | bytes 196616 | tf_op jit(solution)/shard_map/ppermute | solution.py:787
  32.9 6.2 %conditional.3 = (f32[16,128]{1,0:T(8,128)}) conditional(s32[]{:T(128)} %clamp.7, f32[16,128]{1,0:T(8,128)S(1)} %get-tuple-element.118, f32[16,128]{1,0:T(8,128)S(1)} %get-tuple-element.118, f32[16,128]{1,0:T(8,128)S(1)} %get-tuple-element.118, f32[16,128]{1,0:T(8,128)S(1)} %get-tuple-element.118, ...), branch_computations={%region_16.17_spmd, %region_17.18_spmd, %region_18.19_spmd, %regio... | conditional | bytes 32816 | solution.py:710
  32.9 1.5 %collective-permute-start.18 = (f32[16,128]{1,0:T(8,128)S(1)}, f32[16,128]{1,0:T(8,128)}, u32[]{:S(2)}, u32[]{:S(2)}) collective-permute-start(f32[16,128]{1,0:T(8,128)S(1)} %param.18), channel_id=1, source_target_pairs={{29,0},{4,1},{31,2},{6,3},{1,4},{8,5},{3,6},{10,7},{5,8},{12,9},{7... | collective-permute-start | bytes 24584 | tf_op jit(solution)/shard_map/cond/branch_2_fun/ppermute | solution.py:706
  34.4 4.7 %collective-permute-done.18 = f32[16,128]{1,0:T(8,128)} collective-permute-done((f32[16,128]{1,0:T(8,128)S(1)}, f32[16,128]{1,0:T(8,128)}, u32[]{:S(2)}, u32[]{:S(2)}) %collective-permute-start.18) | collective-permute-done | bytes 8224 | tf_op jit(solution)/shard_map/cond/branch_2_fun/ppermute | solution.py:706
  39.1 0.0 collective-permute-done.35.cut_ref
  39.1 0.8 %edges.3 = (f32[792,128]{1,0:T(8,128)S(1)}, f32[792,128]{1,0:T(8,128)S(1)}) custom-call(f32[2,2,4,96,128]{4,3,2,1,0:T(8,128)S(1)} %get-tuple-element.120.p_ends, f32[2,2,4,104,128]{4,3,2,1,0:T(8,128)S(1)} %get-tuple-element.99.b_ends, f32[2,2,4,104,128]{4,3,2,1,0:T(8,128)S(1)} %get-tuple-element.100.w_ends, ...), custom_call_target="tpu_custom_call" | custom-call | flops 3833856 | bytes 2555904 | tf_op jit(solution)/shard_map/edges/pallas_call | solution.py:741
  40.0 0.2 collective-permute-start.36
  40.2 0.5 collective-permute-start.37
  40.7 7.5 %interior.3 = (f32[2,16,96,128]{3,2,1,0:T(8,128)}, f32[2,4,2,2,128,128]{5,4,3,2,1,0:T(8,128)S(1)}, f32[8,8,128]{2,1,0:T(8,128)S(1)}, f32[16,8,128]{2,1,0:T(8,128)S(1)}) custom-call(f32[2,16,96,128]{3,2,1,0:T(8,128)} %get-tuple-element.112.p_ref, f32[2,16,104,128]{3,2,1,0:T(8,128)} %get-tuple-element.113.b_ref, f32[2,16,104,128]{3,2,1,0:T(8,128)} %get-tuple-element.114.w_ref, ...), custom_call_target="tpu_custom_call" | custom-call | flops 14057472 | bytes 9371648 | tf_op jit(solution)/shard_map/interior/pallas_call | solution.py:741
  48.2 1.1 %collective-permute-done.36.left_ref = f32[792,128]{1,0:T(8,128)S(1)} collective-permute-done((f32[792,128]{1,0:T(8,128)S(1)}, f32[792,128]{1,0:T(8,128)S(1)}, u32[]{:S(2)}, u32[]{:S(2)}) %collective-permute-start.36) | collective-permute-done | bytes 405536 | tf_op jit(solution)/shard_map/ppermute | solution.py:803
  49.3 2.6 %collective-permute-done.37.right_ref = f32[792,128]{1,0:T(8,128)S(1)} collective-permute-done((f32[792,128]{1,0:T(8,128)S(1)}, f32[792,128]{1,0:T(8,128)S(1)}, u32[]{:S(2)}, u32[]{:S(2)}) %collective-permute-start.37) | collective-permute-done | bytes 405536 | tf_op jit(solution)/shard_map/ppermute | solution.py:804
  51.9 3.1 %finish.3 = f32[2,16,96,128]{3,2,1,0:T(8,128)} custom-call(s32[1]{0:T(128)} %copy.41.turn_ref, f32[2,2,4,104,128]{4,3,2,1,0:T(8,128)S(1)} %get-tuple-element.99.b_ends, f32[2,2,4,104,128]{4,3,2,1,0:T(8,128)S(1)} %get-tuple-element.100.w_ends, f32[16,8,128]{2,1,0:T(8,128)S(1)} %get-tuple-element.116.w_tile, ...), custom_call_target="tpu_custom_call", output_to_operand_aliasing={{}: (10, {})} | custom-call | flops 8306688 | bytes 5537792 | tf_op jit(solution)/shard_map/finish/pallas_call | solution.py:741
  (1 shorter events, 0.0 us)
Async XLA Ops:
  1.8 7.6 %collective-permute-start.32 = (f32[3,2,16,4,128]{4,3,2,1,0:T(4,128)S(1)}, f32[3,2,16,4,128]{4,3,2,1,0:T(4,128)S(1)}, u32[]{:S(2)}, u32[]{:S(2)}) collective-permute-start(f32[3,2,16,4,128]{4,3,2,1,0:T(4,128)S(1)} %get-tuple-element.98), channel_id=1, source_target_pairs={{0,1},{1,0},{2,3},{3,2},{4,5},{5,4},{6,7},{7,6},{8,9},{9,8},{10,11... | collective-permute-start | bytes 589832 | tf_op jit(solution)/shard_map/ppermute | solution.py:787
  4.7 4.7 %collective-permute-start.1 = (f32[16,128]{1,0:T(8,128)S(1)}, f32[16,128]{1,0:T(8,128)}, u32[]{:S(2)}, u32[]{:S(2)}) collective-permute-start(f32[16,128]{1,0:T(8,128)S(1)} %param.1), channel_id=1, source_target_pairs={{31,0},{2,1},{1,2},{4,3},{3,4},{6,5},{5,6},{8,7},{7,8},{10,9},{9,1... | collective-permute-start | bytes 24584 | tf_op jit(solution)/shard_map/cond/branch_1_fun/ppermute | solution.py:706
  10.7 15.3 %collective-permute-start.33 = (f32[1184,128]{1,0:T(8,128)S(1)}, f32[1184,128]{1,0:T(8,128)S(1)}, u32[]{:S(2)}, u32[]{:S(2)}) collective-permute-start(f32[1184,128]{1,0:T(8,128)S(1)} %get-tuple-element.108), channel_id=1, source_target_pairs={{0,2},{2,4},{4,6},{6,8},{8,10},{10,12},{12,14},{14,16},{16,18},{18... | collective-permute-start | bytes 1818632 | tf_op jit(solution)/shard_map/ppermute | solution.py:803
  12.6 16.0 %collective-permute-start.34 = (f32[1184,128]{1,0:T(8,128)S(1)}, f32[1184,128]{1,0:T(8,128)S(1)}, u32[]{:S(2)}, u32[]{:S(2)}) collective-permute-start(f32[1184,128]{1,0:T(8,128)S(1)} %get-tuple-element.109), channel_id=1, source_target_pairs={{0,30},{2,0},{4,2},{6,4},{8,6},{10,8},{12,10},{14,12},{16,14},{18,... | collective-permute-start | bytes 1818632 | tf_op jit(solution)/shard_map/ppermute | solution.py:804
  31.6 7.6 %collective-permute-start.35 = (f32[1,2,16,4,128]{4,3,2,1,0:T(4,128)S(1)}, f32[1,2,16,4,128]{4,3,2,1,0:T(4,128)S(1)}, u32[]{:S(2)}, u32[]{:S(2)}) collective-permute-start(f32[1,2,16,4,128]{4,3,2,1,0:T(4,128)S(1)} %get-tuple-element.115), channel_id=1, source_target_pairs={{0,1},{1,0},{2,3},{3,2},{4,5},{5,4},{6,7},{7,6},{8,9},{9,8},{10,11... | collective-permute-start | bytes 196616 | tf_op jit(solution)/shard_map/ppermute | solution.py:787
  32.9 6.2 %collective-permute-start.18 = (f32[16,128]{1,0:T(8,128)S(1)}, f32[16,128]{1,0:T(8,128)}, u32[]{:S(2)}, u32[]{:S(2)}) collective-permute-start(f32[16,128]{1,0:T(8,128)S(1)} %param.18), channel_id=1, source_target_pairs={{29,0},{4,1},{31,2},{6,3},{1,4},{8,5},{3,6},{10,7},{5,8},{12,9},{7... | collective-permute-start | bytes 24584 | tf_op jit(solution)/shard_map/cond/branch_2_fun/ppermute | solution.py:706
  40.0 9.3 %collective-permute-start.36 = (f32[792,128]{1,0:T(8,128)S(1)}, f32[792,128]{1,0:T(8,128)S(1)}, u32[]{:S(2)}, u32[]{:S(2)}) collective-permute-start(f32[792,128]{1,0:T(8,128)S(1)} %get-tuple-element.121), channel_id=1, source_target_pairs={{0,2},{2,4},{4,6},{6,8},{8,10},{10,12},{12,14},{14,16},{16,18},{18... | collective-permute-start | bytes 1216520 | tf_op jit(solution)/shard_map/ppermute | solution.py:803
  40.2 11.7 %collective-permute-start.37 = (f32[792,128]{1,0:T(8,128)S(1)}, f32[792,128]{1,0:T(8,128)S(1)}, u32[]{:S(2)}, u32[]{:S(2)}) collective-permute-start(f32[792,128]{1,0:T(8,128)S(1)} %get-tuple-element.122), channel_id=1, source_target_pairs={{0,30},{2,0},{4,2},{6,4},{8,6},{10,8},{12,10},{14,12},{16,14},{18,... | collective-permute-start | bytes 1216520 | tf_op jit(solution)/shard_map/ppermute | solution.py:804

commit v4 on v3

--- a/solution.py
+++ b/solution.py
@@ -12,7 +12,7 @@
 OMEGA = 0.8
 TILE = 8
 OWN = 2 * TILE
-EARLY = False
+EARLY = True
 LEVELS = tuple(range(SWEEPS))
 WEIGHTS = (SWEEPS, SWEEPS + 1)
 FIRST_EARLY = (0, *WEIGHTS) if EARLY else ()

time: 55.6 us -> 55.1 us (level)
  the two profiles are of different devices: /device:TPU:1 before, /device:TPU:4 now
where the time goes in v4:
time: 55.1 us; the launch traced here: 54.4 us
  Pallas kernels  26.1 us (47%)
  starting transfers between devices  18.9 us (34%)
  waiting for transfers between devices  8.5 us (15%)
  between operations  1 us (2%)
    pallas_call x7, Pallas kernels, call(): pl.pallas_call(kernel, out_shape=out_shape, in_specs=in_specs, out_specs=...  26.1 us
    ppermute x2, starting transfers between devices, per_device(): right = lax.ppermute(first, 'az', ring(size, -1))  8.86 us
    ppermute x2, waiting for transfers between devices, branch(): return lambda e: lax.ppermute(e, ('az', 'rad'), facing_pairs(size, t))  7.58 us
    ppermute x1, starting transfers between devices, per_device(): lax.ppermute(first, 'az', ring(size, -1))  4.44 us
    ppermute x2, starting transfers between devices, branch(): return lambda e: lax.ppermute(e, ('az', 'rad'), facing_pairs(size, t))  4.35 us
  transfers between devices with their start and end apart: 10, of which 3 were waited for; matrix products, arithmetic and copies ran while one was open for 0% of the time, Pallas kernels for 28%

profile of v4, /device:TPU:4, one launch (start us, length us, event | category | flops | bytes accessed | tf_op | source)
XLA Modules:
  0.0 54.4 jit_solution(13261688157486355111)
XLA Ops:
  0.0 1.9 %pack.1 = (f32[3,2,16,4,128]{4,3,2,1,0:T(4,128)S(1)}, f32[16,128]{1,0:T(8,128)S(1)}, f32[2,2,4,96,128]{4,3,2,1,0:T(8,128)S(1)}, f32[2,2,3,96,128]{4,3,2,1,0:T(8,...) custom-call(f32[2,16,96,128]{3,2,1,0:T(8,128)} %p_ref.3, ...), custom_call_target="tpu_custom_call" | custom-call | flops 319488 | bytes 212992 | tf_op jit(solution)/shard_map/pack/pallas_call | solution.py:741
  1.9 0.1 collective-permute-start.32
  2.7 5.2 %conditional.2 = (f32[16,128]{1,0:T(8,128)}) conditional(s32[]{:T(128)} %clamp.6, f32[16,128]{1,0:T(8,128)S(1)} %get-tuple-element.105, f32[16,128]{1,0:T(8,128)S(1)} %get-tuple-element.105, f32[16,128]{1,0:T(8,128)S(1)} %get-tuple-element.105, f32[16,128]{1,0:T(8,128)S(1)} %get-tuple-element.105, ...), branch_computations={%region_0.1_spmd, %region_1.2_spmd, %region_2.3_spmd, %region_3.4_... | conditional | bytes 32816 | solution.py:710
  2.7 3.2 %collective-permute-start.7 = (f32[16,128]{1,0:T(8,128)S(1)}, f32[16,128]{1,0:T(8,128)}, u32[]{:S(2)}, u32[]{:S(2)}) collective-permute-start(f32[16,128]{1,0:T(8,128)S(1)} %param.7), channel_id=1, source_target_pairs={{19,0},{14,1},{21,2},{16,3},{23,4},{18,5},{25,6},{20,7},{27,8},{22... | collective-permute-start | bytes 24584 | tf_op jit(solution)/shard_map/cond/branch_7_fun/ppermute | solution.py:706
  5.9 2.0 %collective-permute-done.7 = f32[16,128]{1,0:T(8,128)} collective-permute-done((f32[16,128]{1,0:T(8,128)S(1)}, f32[16,128]{1,0:T(8,128)}, u32[]{:S(2)}, u32[]{:S(2)}) %collective-permute-start.7) | collective-permute-done | bytes 8224 | tf_op jit(solution)/shard_map/cond/branch_7_fun/ppermute | solution.py:706
  7.9 0.9 %collective-permute-done.32.cut_ref = f32[3,2,16,4,128]{4,3,2,1,0:T(4,128)S(1)} collective-permute-done((f32[3,2,16,4,128]{4,3,2,1,0:T(4,128)S(1)}, f32[3,2,16,4,128]{4,3,2,1,0:T(4,128)S(1)}, u32[]{:S(2)}, u32[]{:S(2)}) %collective-permute-start.32) | collective-permute-done | bytes 196640 | tf_op jit(solution)/shard_map/ppermute | solution.py:787
  8.8 1.3 %edges.2 = (f32[608,128]{1,0:T(8,128)S(1)}, f32[608,128]{1,0:T(8,128)S(1)}) custom-call(f32[2,2,4,96,128]{4,3,2,1,0:T(8,128)S(1)} %get-tuple-element.107.p_ends, f32[2,2,3,96,128]{4,3,2,1,0:T(8,128)S(1)} %get-tuple-element.108.s_ends, f32[2,2,3,96,128]{4,3,2,1,0:T(8,128)S(1)} %get-tuple-element.109.d_ends, ...), custom_call_target="tpu_custom_call" | custom-call | flops 3833856 | bytes 2555904 | tf_op jit(solution)/shard_map/edges/pallas_call | solution.py:741
  10.1 0.1 collective-permute-start.33
  10.1 4.4 %collective-permute-start.34 = (f32[608,128]{1,0:T(8,128)S(1)}, f32[608,128]{1,0:T(8,128)S(1)}, u32[]{:S(2)}, u32[]{:S(2)}) collective-permute-start(f32[608,128]{1,0:T(8,128)S(1)} %get-tuple-element.111), channel_id=1, source_target_pairs={{0,30},{2,0},{4,2},{6,4},{8,6},{10,8},{12,10},{14,12},{16,14},{18,... | collective-permute-start | bytes 933896 | tf_op jit(solution)/shard_map/ppermute | solution.py:804
  14.6 4.4 %collective-permute-start.36 = (f32[576,128]{1,0:T(8,128)S(1)}, f32[576,128]{1,0:T(8,128)S(1)}, u32[]{:S(2)}, u32[]{:S(2)}) collective-permute-start(f32[576,128]{1,0:T(8,128)S(1)} %get-tuple-element.114), channel_id=1, source_target_pairs={{0,30},{2,0},{4,2},{6,4},{8,6},{10,8},{12,10},{14,12},{16,14},{18,... | collective-permute-start | bytes 884744 | tf_op jit(solution)/shard_map/ppermute | solution.py:783
  19.0 8.0 %interior.2 = (f32[2,16,96,128]{3,2,1,0:T(8,128)}, f32[2,4,2,2,128,128]{5,4,3,2,1,0:T(8,128)S(1)}, f32[8,8,128]{2,1,0:T(8,128)S(1)}, f32[16,8,128]{2,1,0:T(8,128...) custom-call(f32[2,16,96,128]{3,2,1,0:T(8,128)} %p_ref.3, ...), custom_call_target="tpu_custom_call" | custom-call | flops 14057472 | bytes 9371648 | tf_op jit(solution)/shard_map/interior/pallas_call | solution.py:741
  27.0 0.0 collective-permute-done.35.rest_1_
  27.0 0.0 collective-permute-done.36.rest_2_
  27.0 3.1 %finish.2 = (f32[2,16,96,128]{3,2,1,0:T(8,128)}, f32[1,2,16,4,128]{4,3,2,1,0:T(4,128)S(1)}, f32[16,128]{1,0:T(8,128)S(1)}, f32[2,2,4,96,128]{4,3,2,1,0:T(8,128)S(1)}, f32[2,2,2,104,128]{4,3,2,1,0:T(8,128)S(1)}) custom-call(s32[1]{0:T(128)} %copy.41.turn_ref, f32[2,2,4,104,128]{4,3,2,1,0:T(8,128)S(1)} %get-tuple-element.101.b_ends, ...), custom_call_target="tpu_custom_call", output_to_operand_aliasing={{0}: (12, {})} | custom-call | flops 8306688 | bytes 5537792 | tf_op jit(solution)/shard_map/finish/pallas_call | solution.py:741
  30.1 1.0 %collective-permute-start.37 = (f32[1,2,16,4,128]{4,3,2,1,0:T(4,128)S(1)}, f32[1,2,16,4,128]{4,3,2,1,0:T(4,128)S(1)}, u32[]{:S(2)}, u32[]{:S(2)}) collective-permute-start(f32[1,2,16,4,128]{4,3,2,1,0:T(4,128)S(1)} %get-tuple-element.119), channel_id=1, source_target_pairs={{0,1},{1,0},{2,3},{3,2},{4,5},{5,4},{6,7},{7,6},{8,9},{9,8},{10,11... | collective-permute-start | bytes 196616 | tf_op jit(solution)/shard_map/ppermute | solution.py:787
  31.1 6.8 %conditional.3 = (f32[16,128]{1,0:T(8,128)}) conditional(s32[]{:T(128)} %clamp.7, f32[16,128]{1,0:T(8,128)S(1)} %get-tuple-element.122, f32[16,128]{1,0:T(8,128)S(1)} %get-tuple-element.122, f32[16,128]{1,0:T(8,128)S(1)} %get-tuple-element.122, f32[16,128]{1,0:T(8,128)S(1)} %get-tuple-element.122, ...), branch_computations={%region_16.17_spmd, %region_17.18_spmd, %region_18.19_spmd, %regio... | conditional | bytes 32816 | solution.py:710
  31.1 1.2 %collective-permute-start.31 = (f32[16,128]{1,0:T(8,128)S(1)}, f32[16,128]{1,0:T(8,128)}, u32[]{:S(2)}, u32[]{:S(2)}) collective-permute-start(f32[16,128]{1,0:T(8,128)S(1)} %param.31), channel_id=1, source_target_pairs={{3,0},{30,1},{5,2},{0,3},{7,4},{2,5},{9,6},{4,7},{11,8},{6,9},{13,... | collective-permute-start | bytes 24584 | tf_op jit(solution)/shard_map/cond/branch_15_fun/ppermute | solution.py:706
  32.3 5.6 %collective-permute-done.31 = f32[16,128]{1,0:T(8,128)} collective-permute-done((f32[16,128]{1,0:T(8,128)S(1)}, f32[16,128]{1,0:T(8,128)}, u32[]{:S(2)}, u32[]{:S(2)}) %collective-permute-start.31) | collective-permute-done | bytes 8224 | tf_op jit(solution)/shard_map/cond/branch_15_fun/ppermute | solution.py:706
  37.9 1.2 %edges.3 = (f32[792,128]{1,0:T(8,128)S(1)}, f32[792,128]{1,0:T(8,128)S(1)}) custom-call(f32[2,2,4,96,128]{4,3,2,1,0:T(8,128)S(1)} %get-tuple-element.124.p_ends, f32[2,2,4,104,128]{4,3,2,1,0:T(8,128)S(1)} %get-tuple-element.101.b_ends, f32[2,2,4,104,128]{4,3,2,1,0:T(8,128)S(1)} %get-tuple-element.102.w_ends, ...), custom_call_target="tpu_custom_call" | custom-call | flops 3833856 | bytes 2555904 | tf_op jit(solution)/shard_map/edges/pallas_call | solution.py:741
  39.1 0.1 collective-permute-start.38
  39.2 4.4 %collective-permute-start.39 = (f32[792,128]{1,0:T(8,128)S(1)}, f32[792,128]{1,0:T(8,128)S(1)}, u32[]{:S(2)}, u32[]{:S(2)}) collective-permute-start(f32[792,128]{1,0:T(8,128)S(1)} %get-tuple-element.126), channel_id=1, source_target_pairs={{0,30},{2,0},{4,2},{6,4},{8,6},{10,8},{12,10},{14,12},{16,14},{18,... | collective-permute-start | bytes 1216520 | tf_op jit(solution)/shard_map/ppermute | solution.py:804
  43.6 7.5 %interior.3 = (f32[2,16,96,128]{3,2,1,0:T(8,128)}, f32[2,4,2,2,128,128]{5,4,3,2,1,0:T(8,128)S(1)}, f32[8,8,128]{2,1,0:T(8,128)S(1)}, f32[16,8,128]{2,1,0:T(8,128)S(1)}) custom-call(f32[2,16,96,128]{3,2,1,0:T(8,128)} %get-tuple-element.116.p_ref, f32[2,16,104,128]{3,2,1,0:T(8,128)} %get-tuple-element.117.b_ref, f32[2,16,104,128]{3,2,1,0:T(8,128)} %get-tuple-element.118.w_ref, ...), custom_call_target="tpu_custom_call" | custom-call | flops 14057472 | bytes 9371648 | tf_op jit(solution)/shard_map/interior/pallas_call | solution.py:741
  51.1 0.0 collective-permute-done.38.left_ref
  51.1 3.2 %finish.3 = f32[2,16,96,128]{3,2,1,0:T(8,128)} custom-call(s32[1]{0:T(128)} %copy.41.turn_ref, f32[2,2,4,104,128]{4,3,2,1,0:T(8,128)S(1)} %get-tuple-element.101.b_ends, f32[2,2,4,104,128]{4,3,2,1,0:T(8,128)S(1)} %get-tuple-element.102.w_ends, f32[16,8,128]{2,1,0:T(8,128)S(1)} %get-tuple-element.120.w_tile, ...), custom_call_target="tpu_custom_call", output_to_operand_aliasing={{}: (10, {})} | custom-call | flops 8306688 | bytes 5537792 | tf_op jit(solution)/shard_map/finish/pallas_call | solution.py:741
  (5 shorter events, 0.0 us)
Async XLA Ops:
  1.9 6.9 %collective-permute-start.32 = (f32[3,2,16,4,128]{4,3,2,1,0:T(4,128)S(1)}, f32[3,2,16,4,128]{4,3,2,1,0:T(4,128)S(1)}, u32[]{:S(2)}, u32[]{:S(2)}) collective-permute-start(f32[3,2,16,4,128]{4,3,2,1,0:T(4,128)S(1)} %get-tuple-element.100), channel_id=1, source_target_pairs={{0,1},{1,0},{2,3},{3,2},{4,5},{5,4},{6,7},{7,6},{8,9},{9,8},{10,11... | collective-permute-start | bytes 589832 | tf_op jit(solution)/shard_map/ppermute | solution.py:787
  2.7 5.2 %collective-permute-start.7 = (f32[16,128]{1,0:T(8,128)S(1)}, f32[16,128]{1,0:T(8,128)}, u32[]{:S(2)}, u32[]{:S(2)}) collective-permute-start(f32[16,128]{1,0:T(8,128)S(1)} %param.7), channel_id=1, source_target_pairs={{19,0},{14,1},{21,2},{16,3},{23,4},{18,5},{25,6},{20,7},{27,8},{22... | collective-permute-start | bytes 24584 | tf_op jit(solution)/shard_map/cond/branch_7_fun/ppermute | solution.py:706
  10.1 16.9 %collective-permute-start.33 = (f32[608,128]{1,0:T(8,128)S(1)}, f32[608,128]{1,0:T(8,128)S(1)}, u32[]{:S(2)}, u32[]{:S(2)}) collective-permute-start(f32[608,128]{1,0:T(8,128)S(1)} %get-tuple-element.110), channel_id=1, source_target_pairs={{0,2},{2,4},{4,6},{6,8},{8,10},{10,12},{12,14},{14,16},{16,18},{18... | collective-permute-start | bytes 933896 | tf_op jit(solution)/shard_map/ppermute | solution.py:803
  10.1 16.9 %collective-permute-start.34 = (f32[608,128]{1,0:T(8,128)S(1)}, f32[608,128]{1,0:T(8,128)S(1)}, u32[]{:S(2)}, u32[]{:S(2)}) collective-permute-start(f32[608,128]{1,0:T(8,128)S(1)} %get-tuple-element.111), channel_id=1, source_target_pairs={{0,30},{2,0},{4,2},{6,4},{8,6},{10,8},{12,10},{14,12},{16,14},{18,... | collective-permute-start | bytes 933896 | tf_op jit(solution)/shard_map/ppermute | solution.py:804
  14.6 12.4 %collective-permute-start.35 = (f32[576,128]{1,0:T(8,128)S(1)}, f32[576,128]{1,0:T(8,128)S(1)}, u32[]{:S(2)}, u32[]{:S(2)}) collective-permute-start(f32[576,128]{1,0:T(8,128)S(1)} %get-tuple-element.113), channel_id=1, source_target_pairs={{0,2},{2,4},{4,6},{6,8},{8,10},{10,12},{12,14},{14,16},{16,18},{18... | collective-permute-start | bytes 884744 | tf_op jit(solution)/shard_map/ppermute | solution.py:782
  14.6 12.4 %collective-permute-start.36 = (f32[576,128]{1,0:T(8,128)S(1)}, f32[576,128]{1,0:T(8,128)S(1)}, u32[]{:S(2)}, u32[]{:S(2)}) collective-permute-start(f32[576,128]{1,0:T(8,128)S(1)} %get-tuple-element.114), channel_id=1, source_target_pairs={{0,30},{2,0},{4,2},{6,4},{8,6},{10,8},{12,10},{14,12},{16,14},{18,... | collective-permute-start | bytes 884744 | tf_op jit(solution)/shard_map/ppermute | solution.py:783
  30.1 7.8 %collective-permute-start.37 = (f32[1,2,16,4,128]{4,3,2,1,0:T(4,128)S(1)}, f32[1,2,16,4,128]{4,3,2,1,0:T(4,128)S(1)}, u32[]{:S(2)}, u32[]{:S(2)}) collective-permute-start(f32[1,2,16,4,128]{4,3,2,1,0:T(4,128)S(1)} %get-tuple-element.119), channel_id=1, source_target_pairs={{0,1},{1,0},{2,3},{3,2},{4,5},{5,4},{6,7},{7,6},{8,9},{9,8},{10,11... | collective-permute-start | bytes 196616 | tf_op jit(solution)/shard_map/ppermute | solution.py:787
  31.1 6.8 %collective-permute-start.31 = (f32[16,128]{1,0:T(8,128)S(1)}, f32[16,128]{1,0:T(8,128)}, u32[]{:S(2)}, u32[]{:S(2)}) collective-permute-start(f32[16,128]{1,0:T(8,128)S(1)} %param.31), channel_id=1, source_target_pairs={{3,0},{30,1},{5,2},{0,3},{7,4},{2,5},{9,6},{4,7},{11,8},{6,9},{13,... | collective-permute-start | bytes 24584 | tf_op jit(solution)/shard_map/cond/branch_15_fun/ppermute | solution.py:706
  39.1 12.0 %collective-permute-start.38 = (f32[792,128]{1,0:T(8,128)S(1)}, f32[792,128]{1,0:T(8,128)S(1)}, u32[]{:S(2)}, u32[]{:S(2)}) collective-permute-start(f32[792,128]{1,0:T(8,128)S(1)} %get-tuple-element.125), channel_id=1, source_target_pairs={{0,2},{2,4},{4,6},{6,8},{8,10},{10,12},{12,14},{14,16},{16,18},{18... | collective-permute-start | bytes 1216520 | tf_op jit(solution)/shard_map/ppermute | solution.py:803
  39.2 12.0 %collective-permute-start.39 = (f32[792,128]{1,0:T(8,128)S(1)}, f32[792,128]{1,0:T(8,128)S(1)}, u32[]{:S(2)}, u32[]{:S(2)}) collective-permute-start(f32[792,128]{1,0:T(8,128)S(1)} %get-tuple-element.126), channel_id=1, source_target_pairs={{0,30},{2,0},{4,2},{6,4},{8,6},{10,8},{12,10},{14,12},{16,14},{18,... | collective-permute-start | bytes 1216520 | tf_op jit(solution)/shard_map/ppermute | solution.py:804

commit v5 on v4

--- a/solution.py
+++ b/solution.py
@@ -12,11 +12,8 @@
 OMEGA = 0.8
 TILE = 8
 OWN = 2 * TILE
-EARLY = True
 LEVELS = tuple(range(SWEEPS))
 WEIGHTS = (SWEEPS, SWEEPS + 1)
-FIRST_EARLY = (0, *WEIGHTS) if EARLY else ()
-FIRST_LATE = LEVELS[1:] if EARLY else LEVELS + WEIGHTS
 
 
 class Side:
@@ -118,11 +115,10 @@
         self.slots = slots
         self.radial_cells = radial_cells
         tail = []
-        if 1 in slots:
-            needed = [(n, SWEEPS - 1 - n) for n in LEVELS] + [(SWEEPS, 2)] * weights
-            tail += [(slot, k, h) for slot, n in needed for k in range(2) for h in range(1, n + 1)]
-            tail += [("block", i) for i in range(block_rows(cells))]
-            tail += ["third"] * weights
+        needed = [(n, SWEEPS - 1 - n) for n in LEVELS] + [(SWEEPS, 2)] * weights
+        tail += [(slot, k, h) for slot, n in needed for k in range(2) for h in range(1, n + 1)]
+        tail += [("block", i) for i in range(block_rows(cells))]
+        tail += ["third"] * weights
         start = 2 * len(slots) * radial_cells
         self.tail = {what: start + i for i, what in enumerate(tail)}
         self.rows = start + -(-len(tail) // TILE) * TILE
@@ -139,19 +135,14 @@
         return [w[2] for w in self.tail if w != "third" and w[:2] == (slot, k) and len(w) == 3]
 
     def put(self, ref, side, slot, k, value):
-        if slot in self.slots:
-            ref[self.block(slot, k)] = value[side.inside]
+        ref[self.block(slot, k)] = value[side.inside]
         for h in self.beyond(slot, k):
             at = side.beyond(h)
             ref[self.row(slot, k, h)] = value[at : at + 1]
 
 
-def messages_of(step, radial_cells, cells):
-    late = FIRST_LATE if step == 1 else LEVELS
-    return (
-        Message(FIRST_EARLY if step == 1 else (), radial_cells, cells, False),
-        Message(late, radial_cells, cells, step == 1),
-    )
+def message_of(step, radial_cells, cells):
+    return Message(LEVELS + WEIGHTS if step == 1 else LEVELS, radial_cells, cells, step == 1)
 
 
 def close(column, side, facing):
@@ -220,9 +211,8 @@
 
 
 def pack(p_ref, s_ref, d_ref, cut_ref, edge_ref, p_ends, s_ends, d_ends, *rest):
-    *early, tiles, edge_tiles, sems = rest
+    tiles, edge_tiles, sems = rest
     cells, radial_cells = p_ref.shape[1:3]
-    layout, _ = messages_of(1, radial_cells, cells)
 
     def body(side):
         copies = []
@@ -240,13 +230,6 @@
                 span = pl.ds(end_columns(edge, cells, count).start, count)
                 fetch(source.at[:, span], target.at[edge])
         copy_all(copies)
-        for edge, message in enumerate(early[::-1]):
-            for k in range(2):
-                i = 0 if edge == 0 else SWEEPS - 1
-                message[layout.block(0, k)] = p_ends[edge, k, i]
-                for j in range(2):
-                    i = j if edge == 0 else SWEEPS - 2 - j
-                    message[layout.block(SWEEPS + j, k)] = OMEGA / (6.0 + d_ends[edge, k, i])
         cut_ref[...] = tiles[:, :, :, shifted(side.sent, -side.sent_tile), :]
         at = side.edge - OWN - side.edge_tile
         for j in range(cells):
@@ -280,7 +263,7 @@
     radial_cells = p_ends.shape[3]
     cells = cut_ref.shape[2]
     n = SWEEPS - 1
-    _, layout = messages_of(1, radial_cells, cells)
+    layout = message_of(1, radial_cells, cells)
 
     def body(side):
         arriving = pltpu.make_async_copy(block_ref, block, sem)
@@ -316,7 +299,7 @@
 
 def later_edges(p_ends, b_ends, w_ends, cut_ref, block_ref, last, first, block, sem, field, other):
     cells, radial_cells = cut_ref.shape[2], p_ends.shape[3]
-    _, layout = messages_of(2, radial_cells, cells)
+    layout = message_of(2, radial_cells, cells)
 
     def body(side):
         arriving = pltpu.make_async_copy(block_ref, block, sem)
@@ -337,7 +320,7 @@
     on_each_side(radial_cells, body)
 
 
-def inner_sweeps(side, levels, weight, shift, last, out_ref, stash, tile_out, w_tile, sems):
+def inner_sweeps(side, levels, weight, shift, last, stash, tile_out, w_tile):
     cells = levels.shape[2]
     radial_cells = side.own.stop - side.own.start
     for j in range(cells):
@@ -388,20 +371,15 @@
                 for k in range(2):
                     for i in range(2):
                         stash[e, n + 1, k, i] = levels[n + 1, k, first + i]
-    inner = pltpu.make_async_copy(
-        last, out_ref.at[:, pl.ds(SWEEPS, cells - 2 * SWEEPS)], sems.at[0]
-    )
-    inner.start()
     tile_out[...] = last[side.facing, :, side.edge_tile : side.edge_tile + TILE, :]
     first = side.edge_tile + OWN - side.first
     w_tile[...] = weight[side.facing, :, first : first + TILE, :]
-    return inner
 
 
 def first_interior(
     p_ref, s_ref, d_ref, cut_ref,
-    out_ref, stash, tile_out, w_tile, cut_out, b_ends, w_ends, b_out, w_out,
-    levels, last, shift, weight, sems,
+    last, stash, tile_out, w_tile, cut_out, b_ends, w_ends, b_out, w_out,
+    levels, shift, weight, sems,
 ):
     cells, radial_cells = p_ref.shape[1:3]
 
@@ -439,11 +417,7 @@
             columns = end_columns(e, cells, SWEEPS)
             b_ends[e] = shift[:, columns]
             w_ends[e] = weight[:, columns]
-        pending.append(
-            inner_sweeps(
-                side, levels, weight, shift, last, out_ref, stash, tile_out, w_tile, sems
-            )
-        )
+        inner_sweeps(side, levels, weight, shift, last, stash, tile_out, w_tile)
         cut_out[...] = last[:, :, side.sent, :]
         for c in pending:
             c.wait()
@@ -452,24 +426,30 @@
 
 
 def later_interior(
-    p_ref, b_ref, w_ref, cut_ref, out_ref, stash, tile_out, w_tile, levels, last, shift, weight, sems
+    inner_ref, tile_ref, p_ends, b_ref, w_ref, cut_ref,
+    out_ref, stash, tile_out, w_tile,
+    levels, last, shift, weight, sems,
 ):
-    cells, radial_cells = p_ref.shape[1:3]
+    cells, radial_cells = out_ref.shape[1:3]
+    inner = slice(SWEEPS, cells - SWEEPS)
 
     def body(side):
-        copy_all(
-            [
-                pltpu.make_async_copy(
-                    p_ref, levels.at[0, :, :, pl.ds(OWN, radial_cells), :], sems.at[0]
-                ),
-                pltpu.make_async_copy(b_ref, shift, sems.at[1]),
-                pltpu.make_async_copy(w_ref, weight, sems.at[2]),
-            ]
-        )
+        copies = [
+            pltpu.make_async_copy(b_ref, shift, sems.at[0]),
+            pltpu.make_async_copy(w_ref, weight, sems.at[1]),
+        ]
+        for c in copies:
+            c.start()
+        start = OWN + side.edge_tile
+        levels[0, :, inner, side.own, :] = inner_ref[...]
+        levels[0, side.facing, inner, start : start + TILE, :] = tile_ref[...]
+        for e in range(2):
+            levels[0, :, end_columns(e, cells, SWEEPS), side.own, :] = p_ends[e]
         levels[0, :, :, side.cut, :] = cut_ref[0]
-        inner_sweeps(
-            side, levels, weight, shift, last, out_ref, stash, tile_out, w_tile, sems
-        ).wait()
+        for c in copies:
+            c.wait()
+        inner_sweeps(side, levels, weight, shift, last, stash, tile_out, w_tile)
+        copy_all([pltpu.make_async_copy(last, out_ref.at[:, pl.ds(SWEEPS, cells - 2 * SWEEPS)], sems.at[0])])
 
     on_each_side(radial_cells, body)
 
@@ -519,22 +499,17 @@
 def finish(step, turn_ref, b_ends, w_ends, w_tile, stash, block_ref, tile_in, left_ref, right_ref, *rest):
     known = step > 1
     if known:
-        beyond, _, out_ref, *rest = rest
-        early = ()
+        beyond, _, out_ref, levels, last, inner_tiles, near, near2, wide, source, sems = rest
     else:
-        early = rest[1:3] if EARLY else ()
-        cut_in, rest = rest[0], rest[1 + len(early) :]
-        _, out_ref, cut_out, edge_out, ends_out, beyond, *rest = rest
+        cut_in, cut_out, edge_out, last, inner_tiles, beyond, *rest = rest
+        levels, near, near2, wide, source = rest
     weights = (beyond.at[0], beyond.at[1])
-    levels, last, inner_tiles, near, near2, wide, source, sems = rest
     messages = (left_ref, right_ref)
-    cells, radial_cells = out_ref.shape[1:3]
-    early_layout, layout = messages_of(step, radial_cells, cells)
+    cells, radial_cells = block_ref.shape[0], last.shape[3]
+    layout = message_of(step, radial_cells, cells)
 
     def given(e, k, slot):
-        if slot in layout.slots:
-            return messages[e][layout.block(slot, k)]
-        return early[e][early_layout.block(slot, k)]
+        return messages[e][layout.block(slot, k)]
 
     def column(e, d):
         return d - 1 if e == 0 else cells - d
@@ -623,9 +598,11 @@
             relax_all(side, matrix, items)
         copies = []
 
-        def store(source, target):
-            copies.append(pltpu.make_async_copy(source, target, sems.at[len(copies)]))
-            copies[-1].start()
+        def store(source, k, columns, rows):
+            if known:
+                target = out_ref.at[k, pl.ds(*columns), pl.ds(*rows), :]
+                copies.append(pltpu.make_async_copy(source, target, sems.at[len(copies)]))
+                copies[-1].start()
 
         response = None
         tile = slice(side.edge_tile, side.edge_tile + TILE)
@@ -636,12 +613,8 @@
                 )
                 for i in range(cells - 2 * SWEEPS):
                     inner_tiles[i] = tile_in[i] + response[SWEEPS + i]
-                store(
-                    inner_tiles,
-                    out_ref.at[
-                        k, pl.ds(SWEEPS, cells - 2 * SWEEPS), pl.ds(side.edge_tile, TILE), :
-                    ],
-                )
+                columns = (SWEEPS, cells - 2 * SWEEPS)
+                store(inner_tiles, k, columns, (side.edge_tile, TILE))
             items = []
             for d in range(1, SWEEPS + 1):
                 for e in range(2):
@@ -657,7 +630,7 @@
             relax_all(side, matrix, items)
             for e in range(2):
                 first = end_columns(e, cells, SWEEPS).start
-                store(last.at[e, k], out_ref.at[k, pl.ds(first, SWEEPS)])
+                store(last.at[e, k], k, (first, SWEEPS), (0, radial_cells))
         if not known:
             row = side.edge - OWN
             cut_out[0, :, SWEEPS : cells - SWEEPS] = cut_in[...]
@@ -670,7 +643,6 @@
                 cut_out[0, :, first : first + SWEEPS] = last[e, :, :, side.sent, :]
                 for i in range(SWEEPS):
                     edge_out[first + i : first + i + 1] = last[e, facing, i, row : row + 1]
-            ends_out[...] = last[...]
         for c in copies:
             c.wait()
 
@@ -752,8 +724,6 @@
         )(*operands)
 
     fields = tuple(pinned(x) for x in (pressure, source, diagonal))
-    layout, _ = messages_of(1, radial_cells, cells)
-    early_message = array(layout.rows, lanes)
     cut, edge, *ends = call(
         pack,
         (
@@ -762,10 +732,9 @@
             array(2, 2, SWEEPS, radial_cells, lanes),
             array(2, 2, SWEEPS - 1, radial_cells, lanes),
             array(2, 2, SWEEPS - 1, radial_cells, lanes),
-            *([early_message] * 2 if EARLY else []),
         ),
         [hbm] * 3,
-        [vmem] * (7 if EARLY else 5),
+        [vmem] * 5,
         [
             scratch(3, 2, cells, TILE, lanes),
             scratch(cells, TILE, lanes),
@@ -775,20 +744,12 @@
         1,
         name="pack",
     )
-    early = []
-    if EARLY:
-        *ends, last, first = ends
-        early = [
-            lax.ppermute(last, "az", ring(size, 1)),
-            lax.ppermute(first, "az", ring(size, -1)),
-        ]
     for step in range(1, STEPS + 1):
         known = step > 1
         cut = lax.ppermute(cut, "rad", [(0, 1), (1, 0)])
         offset = rot_offset[0] * step % (cells * size)
         block = facing_block(edge, offset)
-        _, layout = messages_of(step, radial_cells, cells)
-        message = array(layout.rows, lanes)
+        message = array(message_of(step, radial_cells, cells).rows, lanes)
         last, first = call(
             later_edges if known else first_edges,
             (message, message),
@@ -803,29 +764,38 @@
         left = lax.ppermute(last, "az", ring(size, 1))
         right = lax.ppermute(first, "az", ring(size, -1))
         result = pltpu.HBM(pressure.shape, jnp.float32)
-        outs = (result, stash, tiles, array(cells, TILE, lanes))
-        out_specs = [hbm] + [vmem] * 3
+        inner_shape = (2, cells_in, radial_cells, lanes)
+        outs = (stash, tiles, array(cells, TILE, lanes))
+        levels = scratch(SWEEPS, 2, cells, rows, lanes)
+        whole = [scratch(*kept.shape), scratch(*kept.shape), pltpu.SemaphoreType.DMA((3,))]
         if not known:
-            outs += (array(2, cells_in, SWEEPS, lanes), kept_ends, kept_ends, kept, kept)
-            out_specs += [vmem] * 3 + [hbm] * 2
-        inner, saved, inner_tiles, w_tile, *made = call(
-            later_interior if known else first_interior,
-            outs,
-            [hbm] * 3 + [vmem],
-            out_specs,
-            [
-                scratch(SWEEPS, 2, cells, rows, lanes),
-                scratch(2, cells_in, radial_cells, lanes),
-                scratch(*kept.shape),
-                scratch(*kept.shape),
-                pltpu.SemaphoreType.DMA((3,)),
-            ],
-            (*fields, cut),
-            44,
-            name="interior",
-        )
-        if not known:
-            inner_cut, b_ends, w_ends, shift, weight = made
+            inner, saved, inner_tiles, w_tile, inner_cut, b_ends, w_ends, shift, weight = call(
+                first_interior,
+                (
+                    array(*inner_shape),
+                    *outs,
+                    array(2, cells_in, SWEEPS, lanes),
+                    *[kept_ends] * 2,
+                    *[kept] * 2,
+                ),
+                [hbm] * 3 + [vmem],
+                [vmem] * 7 + [hbm] * 2,
+                [levels, *whole],
+                (*fields, cut),
+                44,
+                name="interior",
+            )
+        else:
+            done, saved, inner_tiles, w_tile = call(
+                later_interior,
+                (result, *outs),
+                [vmem] * 3 + [hbm] * 2 + [vmem],
+                [hbm] + [vmem] * 3,
+                [levels, scratch(*inner_shape), *whole],
+                (inner, fixed_tiles, ends[0], pinned(shift), pinned(weight), cut),
+                44,
+                name="interior",
+            )
         operands = (
             rot_offset,
             b_ends,
@@ -837,40 +807,52 @@
             left,
             right,
         )
-        operands += (beyond,) if known else (inner_cut, *early)
-        outs = result
+        last = (2, 2, SWEEPS, radial_cells, lanes)
+        work = [
+            scratch(2, 2, 2, rows, lanes),
+            scratch(2, 2, 2, rows, lanes),
+            scratch(3 * cells, lanes),
+            scratch(cells + 2 * (SWEEPS - 1), TILE, lanes),
+        ]
+        levels = scratch(SWEEPS, 2, 2, SWEEPS, rows, lanes)
         if not known:
-            outs = (
+            operands += (inner_cut,)
+            cut, edge, ends_now, fixed_tiles, beyond = call(
+                functools.partial(finish, step),
+                (
+                    array(1, 2, cells, SWEEPS, lanes),
+                    array(cells, lanes),
+                    array(*last),
+                    tiles,
+                    array(2, 2, 2, span, lanes),
+                ),
+                [smem] + [vmem] * (len(operands) - 1),
+                [vmem] * 5,
+                [levels, *work],
+                operands,
+                26,
+                name="finish",
+            )
+            ends = (ends_now, b_ends, w_ends)
+        else:
+            operands += (beyond,)
+            pressure = call(
+                functools.partial(finish, step),
                 result,
-                array(1, 2, cells, SWEEPS, lanes),
-                array(cells, lanes),
-                array(2, 2, SWEEPS, radial_cells, lanes),
-                array(2, 2, 2, span, lanes),
+                [smem] + [vmem] * (len(operands) - 1) + [hbm],
+                hbm,
+                [
+                    levels,
+                    scratch(*last),
+                    scratch(*tiles.shape),
+                    *work,
+                    pltpu.SemaphoreType.DMA((5,)),
+                ],
+                (*operands, done),
+                26,
+                input_output_aliases={len(operands): 0},
+                name="finish",
             )
-        pressure = call(
-            functools.partial(finish, step),
-            outs,
-            [smem] + [vmem] * (len(operands) - 1) + [hbm],
-            hbm if known else [hbm] + [vmem] * 4,
-            [
-                scratch(SWEEPS, 2, 2, SWEEPS, rows, lanes),
-                scratch(2, 2, SWEEPS, radial_cells, lanes),
-                scratch(*tiles.shape),
-                scratch(2, 2, 2, rows, lanes),
-                scratch(2, 2, 2, rows, lanes),
-                scratch(3 * cells, lanes),
-                scratch(cells + 2 * (SWEEPS - 1), TILE, lanes),
-                pltpu.SemaphoreType.DMA((5,)),
-            ],
-            (*operands, inner),
-            26,
-            input_output_aliases={len(operands): 0},
-            name="finish",
-        )
-        if not known:
-            pressure, cut, edge, ends_now, beyond = pressure
-            fields = tuple(pinned(x) for x in (pressure, shift, weight))
-            ends = (ends_now, b_ends, w_ends)
     return pressure
 
 

time: 55.1 us -> 53.4 us (0.969)
  the two profiles are of different devices: /device:TPU:4 before, /device:TPU:1 now
where the time goes in v5:
time: 53.4 us; the launch traced here: 53.7 us
  Pallas kernels  23.4 us (44%)
  waiting for transfers between devices  18.2 us (34%)
  starting transfers between devices  10.3 us (19%)
  between operations  0.95 us (2%)
  local copies, waits for them, and re-layouts  0.75 us (1%)
    pallas_call x7, Pallas kernels, call(): pl.pallas_call(kernel, out_shape=out_shape, in_specs=in_specs, out_specs=...  23.4 us
    ppermute x2, waiting for transfers between devices, per_device(): left = lax.ppermute(last, 'az', ring(size, 1))  8.01 us
    ppermute x2, waiting for transfers between devices, branch(): return lambda e: lax.ppermute(e, ('az', 'rad'), facing_pairs(size, t))  5.1 us
    ppermute x2, waiting for transfers between devices, per_device(): right = lax.ppermute(first, 'az', ring(size, -1))  4.81 us
    ppermute x2, starting transfers between devices, per_device(): left = lax.ppermute(last, 'az', ring(size, 1))  4 us
    ppermute x2, starting transfers between devices, branch(): return lambda e: lax.ppermute(e, ('az', 'rad'), facing_pairs(size, t))  3.56 us
    ppermute x2, starting transfers between devices, per_device(): cut = lax.ppermute(cut, 'rad', [(0, 1), (1, 0)])  2.28 us
  transfers between devices with their start and end apart: 8, of which 7 were waited for; matrix products, arithmetic and copies ran while one was open for 0% of the time, Pallas kernels for 26%

profile of v5, /device:TPU:1, one launch (start us, length us, event | category | flops | bytes accessed | tf_op | source)
XLA Modules:
  0.0 53.7 jit_solution(12379013864590354883)
XLA Ops:
  0.0 1.8 %pack.1 = (f32[3,2,16,4,128]{4,3,2,1,0:T(4,128)S(1)}, f32[16,128]{1,0:T(8,128)S(1)}, f32[2,2,4,96,128]{4,3,2,1,0:T(8,128)S(1)}, f32[2,2,3,96,128]{4,3,2,1,0:T(8,128)S(1)}, f32[2,2,3,96,128]{4,3,2,1,0:T(8,128)S(1)}) custom-call(f32[2,16,96,128]{3,2,1,0:T(8,128)} %p_ref.3, f32[2,16,96,128]{3,2,1,0:T(8,128)} %s_ref.3, f32[2,16,96,128]{3,2,1,0:T(8,128)} %d_ref.3), custom_call_target="tpu_custom_call" | custom-call | flops 319488 | bytes 212992 | tf_op jit(solution)/shard_map/pack/pallas_call | solution.py:713
  1.8 2.1 %collective-permute-start.32 = (f32[3,2,16,4,128]{4,3,2,1,0:T(4,128)S(1)}, f32[3,2,16,4,128]{4,3,2,1,0:T(4,128)S(1)}, u32[]{:S(2)}, u32[]{:S(2)}) collective-permute-start(f32[3,2,16,4,128]{4,3,2,1,0:T(4,128)S(1)} %get-tuple-element.98), channel_id=1, source_target_pairs={{0,1},{1,0},{2,3},{3,2},{4,5},{5,4},{6,7},{7,6},{8,9},{9,8},{10,11... | collective-permute-start | bytes 589832 | tf_op jit(solution)/shard_map/ppermute | solution.py:749
  4.7 3.7 %conditional.2 = (f32[16,128]{1,0:T(8,128)}) conditional(s32[]{:T(128)} %clamp.6, f32[16,128]{1,0:T(8,128)S(1)} %get-tuple-element.104, f32[16,128]{1,0:T(8,128)S(1)} %get-tuple-element.104, f32[16,128]{1,0:T(8,128)S(1)} %get-tuple-element.104, f32[16,128]{1,0:T(8,128)S(1)} %get-tuple-element.104, ...), branch_computations={%region_0.1_spmd, %region_1.2_spmd, %region_2.3_spmd, %region_3.4_... | conditional | bytes 32816 | solution.py:682
  4.7 1.2 %collective-permute-start.14 = (f32[16,128]{1,0:T(8,128)S(1)}, f32[16,128]{1,0:T(8,128)}, u32[]{:S(2)}, u32[]{:S(2)}) collective-permute-start(f32[16,128]{1,0:T(8,128)S(1)} %param.14), channel_id=1, source_target_pairs={{5,0},{28,1},{7,2},{30,3},{9,4},{0,5},{11,6},{2,7},{13,8},{4,9},{1... | collective-permute-start | bytes 24584 | tf_op jit(solution)/shard_map/cond/branch_14_fun/ppermute | solution.py:678
  5.9 2.5 %collective-permute-done.14 = f32[16,128]{1,0:T(8,128)} collective-permute-done((f32[16,128]{1,0:T(8,128)S(1)}, f32[16,128]{1,0:T(8,128)}, u32[]{:S(2)}, u32[]{:S(2)}) %collective-permute-start.14) | collective-permute-done | bytes 8224 | tf_op jit(solution)/shard_map/cond/branch_14_fun/ppermute | solution.py:678
  8.4 0.3 collective-permute-done.32.cut_ref
  8.7 1.3 %edges.2 = (f32[1184,128]{1,0:T(8,128)S(1)}, f32[1184,128]{1,0:T(8,128)S(1)}) custom-call(f32[2,2,4,96,128]{4,3,2,1,0:T(8,128)S(1)} %get-tuple-element.106.p_ends, f32[2,2,3,96,128]{4,3,2,1,0:T(8,128)S(1)} %get-tuple-element.107.s_ends, f32[2,2,3,96,128]{4,3,2,1,0:T(8,128)S(1)} %get-tuple-element.108.d_ends, ...), custom_call_target="tpu_custom_call" | custom-call | flops 3833856 | bytes 2555904 | tf_op jit(solution)/shard_map/edges/pallas_call | solution.py:713
  10.0 3.8 %collective-permute-start.33 = (f32[1184,128]{1,0:T(8,128)S(1)}, f32[1184,128]{1,0:T(8,128)S(1)}, u32[]{:S(2)}, u32[]{:S(2)}) collective-permute-start(f32[1184,128]{1,0:T(8,128)S(1)} %get-tuple-element.109), channel_id=1, source_target_pairs={{0,2},{2,4},{4,6},{6,8},{8,10},{10,12},{12,14},{14,16},{16,18},{18... | collective-permute-start | bytes 1818632 | tf_op jit(solution)/shard_map/ppermute | solution.py:764
  13.8 7.1 %interior.2 = (f32[2,8,96,128]{3,2,1,0:T(8,128)S(1)}, f32[2,4,2,2,128,128]{5,4,3,2,1,0:T(8,128)S(1)}, f32[8,8,128]{2,1,0:T(8,128)S(1)}, f32[16,8,128]{2,1,0:T(8,...) custom-call(f32[2,16,96,128]{3,2,1,0:T(8,128)} %p_ref.3, ...), custom_call_target="tpu_custom_call" | custom-call | flops 14057472 | bytes 9371648 | tf_op jit(solution)/shard_map/interior/pallas_call | solution.py:713
  20.9 6.4 %collective-permute-done.33.left_ref = f32[1184,128]{1,0:T(8,128)S(1)} collective-permute-done((f32[1184,128]{1,0:T(8,128)S(1)}, f32[1184,128]{1,0:T(8,128)S(1)}, u32[]{:S(2)}, u32[]{:S(2)}) %collective-permute-start.33) | collective-permute-done | bytes 606240 | tf_op jit(solution)/shard_map/ppermute | solution.py:764
  27.3 2.5 %collective-permute-done.34.right_ref = f32[1184,128]{1,0:T(8,128)S(1)} collective-permute-done((f32[1184,128]{1,0:T(8,128)S(1)}, f32[1184,128]{1,0:T(8,128)S(1)}, u32[]{:S(2)}, u32[]{:S(2)}) %collective-permute-start.34) | collective-permute-done | bytes 606240 | tf_op jit(solution)/shard_map/ppermute | solution.py:765
  29.7 2.1 %finish.2 = (f32[1,2,16,4,128]{4,3,2,1,0:T(4,128)S(1)}, f32[16,128]{1,0:T(8,128)S(1)}, f32[2,2,4,96,128]{4,3,2,1,0:T(8,128)S(1)}, f32[8,8,128]{2,1,0:T(8,128)S(1)}, f32[2,2,2,104,128]{4,3,2,1,0:T(8,128)S(1)}) custom-call(s32[1]{0:T(128)} %copy.39.turn_ref, f32[2,2,4,104,128]{4,3,2,1,0:T(8,128)S(1)} %get-tuple-element.99.b_ends, ...), custom_call_target="tpu_custom_call" | custom-call | flops 8306688 | bytes 5537792 | tf_op jit(solution)/shard_map/finish/pallas_call | solution.py:713
  31.9 0.7 %copy-done = f32[2,2,2,104,128]{4,3,2,1,0:T(8,128)} copy-done((f32[2,2,2,104,128]{4,3,2,1,0:T(8,128)}, f32[2,2,2,104,128]{4,3,2,1,0:T(8,128)S(1)}, u32[]{:S(2)}) %copy-start) | copy-done | bytes 426008
  32.6 0.1 collective-permute-start.35
  32.8 5.0 %conditional.3 = (f32[16,128]{1,0:T(8,128)}) conditional(s32[]{:T(128)} %clamp.7, f32[16,128]{1,0:T(8,128)S(1)} %get-tuple-element.119, f32[16,128]{1,0:T(8,128)S(1)} %get-tuple-element.119, f32[16,128]{1,0:T(8,128)S(1)} %get-tuple-element.119, f32[16,128]{1,0:T(8,128)S(1)} %get-tuple-element.119, ...), branch_computations={%region_16.17_spmd, %region_17.18_spmd, %region_18.19_spmd, %regio... | conditional | bytes 32816 | solution.py:682
  32.8 2.3 %collective-permute-start.27 = (f32[16,128]{1,0:T(8,128)S(1)}, f32[16,128]{1,0:T(8,128)}, u32[]{:S(2)}, u32[]{:S(2)}) collective-permute-start(f32[16,128]{1,0:T(8,128)S(1)} %param.27), channel_id=1, source_target_pairs={{11,0},{22,1},{13,2},{24,3},{15,4},{26,5},{17,6},{28,7},{19,8},{30... | collective-permute-start | bytes 24584 | tf_op jit(solution)/shard_map/cond/branch_11_fun/ppermute | solution.py:678
  35.1 2.6 %collective-permute-done.27 = f32[16,128]{1,0:T(8,128)} collective-permute-done((f32[16,128]{1,0:T(8,128)S(1)}, f32[16,128]{1,0:T(8,128)}, u32[]{:S(2)}, u32[]{:S(2)}) %collective-permute-start.27) | collective-permute-done | bytes 8224 | tf_op jit(solution)/shard_map/cond/branch_11_fun/ppermute | solution.py:678
  37.8 0.8 %edges.3 = (f32[792,128]{1,0:T(8,128)S(1)}, f32[792,128]{1,0:T(8,128)S(1)}) custom-call(f32[2,2,4,96,128]{4,3,2,1,0:T(8,128)S(1)} %get-tuple-element.113.p_ends, f32[2,2,4,104,128]{4,3,2,1,0:T(8,128)S(1)} %get-tuple-element.99.b_ends, f32[2,2,4,104,128]{4,3,2,1,0:T(8,128)S(1)} %get-tuple-element.100.w_ends, ...), custom_call_target="tpu_custom_call" | custom-call | flops 3833856 | bytes 2555904 | tf_op jit(solution)/shard_map/edges/pallas_call | solution.py:713
  38.6 0.2 collective-permute-start.36
  38.8 0.5 collective-permute-start.37
  39.3 7.1 %interior.3 = (f32[2,16,96,128]{3,2,1,0:T(8,128)}, f32[2,4,2,2,128,128]{5,4,3,2,1,0:T(8,128)S(1)}, f32[8,8,128]{2,1,0:T(8,128)S(1)}, f32[16,8,128]{2,1,0:T(8,128)S(1)}) custom-call(f32[2,8,96,128]{3,2,1,0:T(8,128)S(1)} %get-tuple-element.101.inner_ref, f32[8,8,128]{2,1,0:T(8,128)S(1)} %get-tuple-element.112.tile_ref, ...), custom_call_target="tpu_custom_call" | custom-call | flops 14057472 | bytes 9371648 | tf_op jit(solution)/shard_map/interior/pallas_call | solution.py:713
  46.4 1.6 %collective-permute-done.36.left_ref = f32[792,128]{1,0:T(8,128)S(1)} collective-permute-done((f32[792,128]{1,0:T(8,128)S(1)}, f32[792,128]{1,0:T(8,128)S(1)}, u32[]{:S(2)}, u32[]{:S(2)}) %collective-permute-start.36) | collective-permute-done | bytes 405536 | tf_op jit(solution)/shard_map/ppermute | solution.py:764
  48.0 2.3 %collective-permute-done.37.right_ref = f32[792,128]{1,0:T(8,128)S(1)} collective-permute-done((f32[792,128]{1,0:T(8,128)S(1)}, f32[792,128]{1,0:T(8,128)S(1)}, u32[]{:S(2)}, u32[]{:S(2)}) %collective-permute-start.37) | collective-permute-done | bytes 405536 | tf_op jit(solution)/shard_map/ppermute | solution.py:765
  50.4 3.1 %finish.3 = f32[2,16,96,128]{3,2,1,0:T(8,128)} custom-call(s32[1]{0:T(128)} %copy.39.turn_ref, f32[2,2,4,104,128]{4,3,2,1,0:T(8,128)S(1)} %get-tuple-element.99.b_ends, f32[2,2,4,104,128]{4,3,2,1,0:T(8,128)S(1)} %get-tuple-element.100.w_ends, f32[16,8,128]{2,1,0:T(8,128)S(1)} %get-tuple-element.117.w_tile, ...), custom_call_target="tpu_custom_call", output_to_operand_aliasing={{}: (10, {})} | custom-call | flops 8306688 | bytes 5537792 | tf_op jit(solution)/shard_map/finish/pallas_call | solution.py:713
  (5 shorter events, 0.0 us)
Async XLA Ops:
  1.8 6.8 %collective-permute-start.32 = (f32[3,2,16,4,128]{4,3,2,1,0:T(4,128)S(1)}, f32[3,2,16,4,128]{4,3,2,1,0:T(4,128)S(1)}, u32[]{:S(2)}, u32[]{:S(2)}) collective-permute-start(f32[3,2,16,4,128]{4,3,2,1,0:T(4,128)S(1)} %get-tuple-element.98), channel_id=1, source_target_pairs={{0,1},{1,0},{2,3},{3,2},{4,5},{5,4},{6,7},{7,6},{8,9},{9,8},{10,11... | collective-permute-start | bytes 589832 | tf_op jit(solution)/shard_map/ppermute | solution.py:749
  4.7 3.7 %collective-permute-start.14 = (f32[16,128]{1,0:T(8,128)S(1)}, f32[16,128]{1,0:T(8,128)}, u32[]{:S(2)}, u32[]{:S(2)}) collective-permute-start(f32[16,128]{1,0:T(8,128)S(1)} %param.14), channel_id=1, source_target_pairs={{5,0},{28,1},{7,2},{30,3},{9,4},{0,5},{11,6},{2,7},{13,8},{4,9},{1... | collective-permute-start | bytes 24584 | tf_op jit(solution)/shard_map/cond/branch_14_fun/ppermute | solution.py:678
  10.0 17.3 %collective-permute-start.33 = (f32[1184,128]{1,0:T(8,128)S(1)}, f32[1184,128]{1,0:T(8,128)S(1)}, u32[]{:S(2)}, u32[]{:S(2)}) collective-permute-start(f32[1184,128]{1,0:T(8,128)S(1)} %get-tuple-element.109), channel_id=1, source_target_pairs={{0,2},{2,4},{4,6},{6,8},{8,10},{10,12},{12,14},{14,16},{16,18},{18... | collective-permute-start | bytes 1818632 | tf_op jit(solution)/shard_map/ppermute | solution.py:764
  13.8 16.0 %collective-permute-start.34 = (f32[1184,128]{1,0:T(8,128)S(1)}, f32[1184,128]{1,0:T(8,128)S(1)}, u32[]{:S(2)}, u32[]{:S(2)}) collective-permute-start(f32[1184,128]{1,0:T(8,128)S(1)} %get-tuple-element.110), channel_id=1, source_target_pairs={{0,30},{2,0},{4,2},{6,4},{8,6},{10,8},{12,10},{14,12},{16,14},{18,... | collective-permute-start | bytes 1818632 | tf_op jit(solution)/shard_map/ppermute | solution.py:765
  31.9 0.8 %copy-start = (f32[2,2,2,104,128]{4,3,2,1,0:T(8,128)}, f32[2,2,2,104,128]{4,3,2,1,0:T(8,128)S(1)}, u32[]{:S(2)}) copy-start(f32[2,2,2,104,128]{4,3,2,1,0:T(8,128)S(1)} %get-tuple-element.123.rest_0_) | copy-start | bytes 1277956
  32.6 5.1 %collective-permute-start.35 = (f32[1,2,16,4,128]{4,3,2,1,0:T(4,128)S(1)}, f32[1,2,16,4,128]{4,3,2,1,0:T(4,128)S(1)}, u32[]{:S(2)}, u32[]{:S(2)}) collective-permute-start(f32[1,2,16,4,128]{4,3,2,1,0:T(4,128)S(1)} %get-tuple-element.116), channel_id=1, source_target_pairs={{0,1},{1,0},{2,3},{3,2},{4,5},{5,4},{6,7},{7,6},{8,9},{9,8},{10,11... | collective-permute-start | bytes 196616 | tf_op jit(solution)/shard_map/ppermute | solution.py:749
  32.8 5.0 %collective-permute-start.27 = (f32[16,128]{1,0:T(8,128)S(1)}, f32[16,128]{1,0:T(8,128)}, u32[]{:S(2)}, u32[]{:S(2)}) collective-permute-start(f32[16,128]{1,0:T(8,128)S(1)} %param.27), channel_id=1, source_target_pairs={{11,0},{22,1},{13,2},{24,3},{15,4},{26,5},{17,6},{28,7},{19,8},{30... | collective-permute-start | bytes 24584 | tf_op jit(solution)/shard_map/cond/branch_11_fun/ppermute | solution.py:678
  38.6 9.4 %collective-permute-start.36 = (f32[792,128]{1,0:T(8,128)S(1)}, f32[792,128]{1,0:T(8,128)S(1)}, u32[]{:S(2)}, u32[]{:S(2)}) collective-permute-start(f32[792,128]{1,0:T(8,128)S(1)} %get-tuple-element.121), channel_id=1, source_target_pairs={{0,2},{2,4},{4,6},{6,8},{8,10},{10,12},{12,14},{14,16},{16,18},{18... | collective-permute-start | bytes 1216520 | tf_op jit(solution)/shard_map/ppermute | solution.py:764
  38.8 11.5 %collective-permute-start.37 = (f32[792,128]{1,0:T(8,128)S(1)}, f32[792,128]{1,0:T(8,128)S(1)}, u32[]{:S(2)}, u32[]{:S(2)}) collective-permute-start(f32[792,128]{1,0:T(8,128)S(1)} %get-tuple-element.122), channel_id=1, source_target_pairs={{0,30},{2,0},{4,2},{6,4},{8,6},{10,8},{12,10},{14,12},{16,14},{18,... | collective-permute-start | bytes 1216520 | tf_op jit(solution)/shard_map/ppermute | solution.py:765
  39.3 11.0 %copy-start.1 = (f32[2,2,2,104,128]{4,3,2,1,0:T(8,128)S(1)}, f32[2,2,2,104,128]{4,3,2,1,0:T(8,128)}, u32[]{:S(2)}) copy-start(f32[2,2,2,104,128]{4,3,2,1,0:T(8,128)} %copy-done) | copy-start | bytes 1277956
